TPU v7x, 256 devices: a whole 4x4x8 slice. The times are simulated.
256 devices in a mesh: batch: 4 (over y_lo, core), cand: 64 (over y_hi, x, z).
Axes of the slice: x: 4, y: 4 (y_hi: 2, y_lo: 2; y = y_hi * 2 + y_lo), z: 8, core: 2. Of those that a mesh axis runs over, the one named last changes fastest.
Arguments:
- queries: bfloat16 [16384, 128], P(('batch', 'cand')), may hold values from -8 to 8
- candidates: bfloat16 [131072, 128], P(('batch', 'cand')), may hold values from -2 to 2
- positive: int32 [16384], P(('batch', 'cand')), may hold values from 0 to 131071
- bucket: int32 [131072], P(('batch', 'cand')), may hold values from 0 to 1023
- query_weight: bfloat16 [16384], P(('batch', 'cand')), may hold values from 0.5 to 2
- log_freq: float32 [1024], replicated, may hold values from -1 to 0
Outputs:
- query_grad: float32 [16384, 128], P(('batch', 'cand'))
- cand_grad: float32 [131072, 128], P(('batch', 'cand'))
All inputs are finite; a program needn't handle non-finite values.
Results may differ from a plain program's by a relative error of at most 0.0019.
Values may be sent and summed in bfloat16 or wider, within the bound.
No kernel may reach another device: no remote copies, remote signals or barrier semaphores. Data moves between devices by JAX's collectives and lax.ppermute only.
A program may use at most 192 MiB of HBM per device.

v0:
```python
import jax
import jax.numpy as jnp
from jax import lax
from jax.sharding import PartitionSpec as P


def per_device(queries, candidates, positive, bucket, query_weight, log_freq):
    n_batch = lax.axis_size("batch")
    n_cand = lax.axis_size("cand")
    cand_index = lax.axis_index("cand")
    cand_local = candidates.shape[0]
    feature_dim = candidates.shape[1]
    rows, row_ids, row_weight = (
        lax.all_gather(queries, "cand", axis=0, tiled=True),
        lax.all_gather(positive, "cand", axis=0, tiled=True),
        lax.all_gather(query_weight, "cand", axis=0, tiled=True),
    )
    columns, column_bucket = (
        lax.all_gather(candidates, "batch", axis=0, tiled=True),
        lax.all_gather(bucket, "batch", axis=0, tiled=True),
    )
    owners = jnp.arange(n_batch, dtype=jnp.int32) * n_cand + cand_index
    global_column = (
        owners[:, None] * cand_local + jnp.arange(cand_local, dtype=jnp.int32)[None, :]
    ).reshape(-1)
    shift = log_freq[column_bucket]
    total_rows = rows.shape[0]
    block_size = min(512, total_rows)
    block_count = total_rows // block_size
    row_blocks = rows.reshape(block_count, block_size, feature_dim)
    id_blocks = row_ids.reshape(block_count, block_size)
    weight_blocks = row_weight.reshape(block_count, block_size)

    def block_logits(query_block):
        product = lax.dot_general(
            query_block, columns, (((1,), (1,)), ((), ())), preferred_element_type=jnp.float32
        )
        return product - shift[None, :]

    def local_max(query_block):
        return jnp.max(block_logits(query_block), axis=1)

    def local_total(pieces):
        query_block, max_block = pieces
        return jnp.sum(jnp.exp(block_logits(query_block) - max_block[:, None]), axis=1)

    own_max = lax.map(local_max, row_blocks).reshape(-1)
    row_max = lax.pmax(own_max, "cand")
    own_total = lax.map(
        local_total, (row_blocks, row_max.reshape(block_count, block_size))
    ).reshape(-1)
    row_total = lax.psum(own_total, "cand")

    def backward_block(carry_grad, pieces):
        query_block, index_block, weight_block, max_block, total_block = pieces
        expo = jnp.exp(block_logits(query_block) - max_block[:, None])
        matched = (global_column[None, :] == index_block[:, None]).astype(jnp.float32)
        grad = (
            weight_block.astype(jnp.float32)[:, None] * (expo / total_block[:, None] - matched)
        ).astype(jnp.bfloat16)
        query_part = jnp.dot(grad, columns, preferred_element_type=jnp.float32)
        carry_grad = carry_grad + lax.dot_general(
            grad, query_block, (((0,), (0,)), ((), ())), preferred_element_type=jnp.float32
        )
        return (carry_grad, query_part)

    start_grad = jnp.zeros((columns.shape[0], feature_dim), jnp.float32)
    cand_terms, query_terms = lax.scan(
        backward_block,
        start_grad,
        (
            row_blocks,
            id_blocks,
            weight_blocks,
            row_max.reshape(block_count, block_size),
            row_total.reshape(block_count, block_size),
        ),
    )
    query_terms = query_terms.reshape(-1, feature_dim)
    query_grad = lax.psum_scatter(query_terms, "cand", scatter_dimension=0, tiled=True)
    cand_grad = lax.psum_scatter(cand_terms, "batch", scatter_dimension=0, tiled=True)
    return (query_grad, cand_grad)


def solution(mesh):
    in_specs = (
        P(("batch", "cand"), None),
        P(("batch", "cand"), None),
        P(("batch", "cand")),
        P(("batch", "cand")),
        P(("batch", "cand")),
        P(),
    )
    out_specs = (P(("batch", "cand"), None), P(("batch", "cand"), None))
    return jax.shard_map(
        per_device, mesh=mesh, in_specs=in_specs, out_specs=out_specs, check_vma=False
    )
```

profile of v0, /device:TPU:16, one launch (start us, length us, event | category | flops | bytes accessed | tf_op | source)
XLA Modules:
  0.0 1758.1 jit_solution(247980317081902198)
XLA Ops:
  10.8 358.7 %all-reduce.1 = s32[4096]{0:T(1024)S(1)} all-reduce(s32[4096]{0:T(1024)S(1)} %dynamic-update-slice.1), channel_id=1, replica_groups=mesh['batch'=4,'cand'=64] {'cand'}, use_global_device_ids=true, to_apply=%add.1 | all-reduce | flops 4096 | bytes 32768
  370.4 178.6 %all-reduce = bf16[4096]{0:T(1024)(128)(2,1)S(1)} all-reduce(bf16[4096]{0:T(1024)(128)(2,1)S(1)} %dynamic-update-slice), channel_id=1, replica_groups=mesh['batch'=4,'cand'=64] {'cand'}, use_global_device_ids=true, to_apply=%add | all-reduce | flops 4096 | bytes 16384
  549.0 5.6 all-gather
  554.6 8.6 gather_fusion
  563.2 8.1 all_gather.17
  571.3 15.9 while.33
  587.3 352.9 %pmax.7 = f32[8,512]{1,0:T(8,128)S(1)} all-reduce(f32[8,512]{1,0:T(8,128)S(1)} %get-tuple-element.119), channel_id=1, replica_groups=mesh['batch'=4,'cand'=64] {'cand'}, use_global_device_ids=true, to_apply=%region_3.4 | all-reduce | flops 4096 | bytes 32768 | tf_op jit(solution)/shard_map/pmax | solution.py:48
  940.2 17.2 while.34
  940.2 2.1 exponential_reduce_fusion.2
  946.6 2.1 exponential_reduce_fusion.2
  948.8 2.1 exponential_reduce_fusion.2
  951.0 2.1 exponential_reduce_fusion.2
  957.4 351.0 %psum.7 = f32[8,512]{1,0:T(8,128)S(1)} all-reduce(f32[8,512]{1,0:T(8,128)S(1)} %get-tuple-element.120), channel_id=1, replica_groups=mesh['batch'=4,'cand'=64] {'cand'}, use_global_device_ids=true, to_apply=%region_7.8 | all-reduce | flops 4096 | bytes 32768 | tf_op jit(solution)/shard_map/psum | solution.py:52
  1308.4 57.8 %while.35 = (s32[]{:T(128)}, f32[2048,128]{1,0:T(8,128)S(1)}, f32[8,512,128]{2,1,0:T(8,128)}, bf16[8,512]{1,0:T(8,128)(2,1)S(1)}, bf16[8,512,128]{2,1,0:T(8,128)...) while((s32[]{:T(128)}, f32[2048,128]{1,0:T(8,128)S(1)}, ...), condition=%wide.region_9.10_spmd.clone, body=%wide.region_8.9_spmd.clone.sunk | while | flops 814221824 | bytes 10027683 | solution.py:68
  1308.5 2.6 multiply_convert_fusion.2
  1311.2 2.5 fusion.43
  1315.7 2.6 multiply_convert_fusion.2
  1318.4 2.5 fusion.43
  1322.9 2.6 multiply_convert_fusion.2
  1325.6 2.5 fusion.43
  1330.2 2.6 multiply_convert_fusion.2
  1332.8 2.5 fusion.43
  1337.4 2.6 multiply_convert_fusion.2
  1340.0 2.5 fusion.43
  1344.6 2.6 multiply_convert_fusion.2
  1347.3 2.5 fusion.43
  1351.9 2.6 multiply_convert_fusion.2
  1354.5 2.5 fusion.43
  1359.1 2.6 multiply_convert_fusion.2
  1361.7 2.5 fusion.43
  1367.9 15.9 reduce-scatter.5.cloned.1.call-done
  1383.9 367.7 %reduce-scatter.3.cloned.1.call-done = f32[64,128]{1,0:T(8,128)} async-done(((f32[4096,128]{1,0:T(8,128)}), f32[64,128]{1,0:T(8,128)}) %reduce-scatter.3.cloned.1.call-update) | async-done | bytes 32784 | tf_op jit(solution)/shard_map/reduce_scatter | solution.py:80
  (110 shorter events, 46.5 us)
Async XLA Ops:
  7.2 547.4 %copy-start = (f32[1024]{0:T(1024)S(1)}, f32[1024]{0:T(1024)}, u32[]{:S(2)}) copy-start(f32[1024]{0:T(1024)} %param.17) | copy-start | bytes 12292
  7.2 564.2 %all-gather.3.cloned.1.call-start = ((), (), s32[]{:S(2)}) async-start(), calls=%async_computation.2 | async-start | bytes 1064960 | tf_op jit(solution)/shard_map/all_gather | solution.py:14
  7.9 1375.9 %reduce-scatter.5.cloned.1.call-start = ((), (), s32[]{:S(2)}) async-start(), calls=%async_computation.4 | async-start | bytes 1310720 | tf_op jit(solution)/shard_map/reduce_scatter | solution.py:81
  554.6 8.6 copy-start.2
  1366.2 1.0 copy-start.1
  1367.2 384.4 %reduce-scatter.3.cloned.1.call-start = ((), (), s32[]{:S(2)}) async-start(), calls=%async_computation.3 | async-start | bytes 2129920 | tf_op jit(solution)/shard_map/reduce_scatter | solution.py:80
Sparse Core Ops, SparseCore 0:
  11.5 115.2 all-gather.2
  1367.3 16.5 reduce-scatter.4
  1387.1 364.4 reduce-scatter.2
where the time goes:
time: 1760 us
  blocking collectives  1250 us (71%)
  waiting for transfers between devices  385 us (22%)
  matrix products  88.2 us (5%)
    unnamed x2, blocking collectives  537 us
    reduce_scatter x1, waiting for transfers between devices, per_device(): lax.psum_scatter(query_terms, 'cand', scatter_dimension=0, tiled=True)  368 us
    pmax x1, blocking collectives, per_device(): row_max = lax.pmax(own_max, 'cand')  353 us
    psum x1, blocking collectives, per_device(): row_total = lax.psum(own_total, 'cand')  351 us
    dot_general x24, matrix products, block_logits(): lax.dot_general(query_block, columns, (((1,), (1,)), ((), ())), preferred...  52.9 us
  transfers between devices with their start and end apart: 3, of which 2 were waited for; matrix products, arithmetic and copies ran while one was open for 1% of the time, Pallas kernels for 0%

commit v1 on v0

v1 whole, which is shorter than its diff:
```python
import functools

import jax
import jax.numpy as jnp
from jax import lax
from jax.experimental import pallas as pl
from jax.experimental.pallas import tpu as pltpu
from jax.sharding import Mesh, PartitionSpec as P

bf16 = jnp.bfloat16
f32 = jnp.float32
i32 = jnp.int32
NT = (((1,), (1,)), ((), ()))
NN = (((1,), (0,)), ((), ()))
TN = (((0,), (0,)), ((), ()))
AXES = ("yl", "c", "yh", "x", "z")
GROUP = ("x", "z")
RING = ("yl", "yh")
NY, NCORE, NGROUP = 4, 2, 32
VMEM = pl.BlockSpec(memory_space=pltpu.VMEM)
SMEM = pl.BlockSpec(memory_space=pltpu.SMEM)
E = 128
QB = 64
CB = 512
QPAD = 16
CPAD = 16
SIDE = 32
NQ = NGROUP * QB
HALF = NY * CB
NC = NCORE * HALF


def stats_kernel(here, table, q_in, own, other, c_ext, q_ext, aux, lse_out, meta):
    lane = lax.broadcasted_iota(i32, (SIDE, E), 1)
    row = lax.broadcasted_iota(i32, (SIDE, E), 0)
    freq = table[...]
    high = freq.astype(bf16).astype(f32)
    rest = freq - high
    middle = rest.astype(bf16).astype(f32)
    low = rest - middle
    parts = jnp.where(
        lane < SIDE, high, jnp.where(lane < 2 * SIDE, middle, jnp.where(lane < 3 * SIDE, low, 0.0))
    ).astype(bf16)
    pick = ((lane & (SIDE - 1)) == row).astype(f32).astype(bf16)

    for core, block_ref in enumerate((own, other)):
        for s in range(NY):
            first = core * HALF + s * CB
            c_ext[first : first + CB, :E] = block_ref[s, :CB, :]
            codes = block_ref[s, CB : CB + CPAD, :].astype(f32)
            for r in range(CB // E):
                major = codes[r : r + 1, :].astype(i32)
                minor = codes[4 + r : 5 + r, :].astype(i32)
                hot_major = (row == major).astype(f32).astype(bf16)
                hot_minor = (row == minor).astype(f32).astype(bf16)
                values = lax.dot_general(hot_major, parts, TN, preferred_element_type=f32)
                mask = lax.dot_general(hot_minor, pick, TN, preferred_element_type=f32)
                c_ext[first + r * E : first + (r + 1) * E, E:] = (-(values * mask)).astype(bf16)

    wide = lax.broadcasted_iota(i32, (8, E), 1)
    for k in range(NGROUP):
        q_ext[k * QB : (k + 1) * QB, :E] = q_in[k, :QB, :]
    q_ext[:, E:] = jnp.ones((NQ, E), bf16)
    for t in range(NGROUP // 2):
        even = q_in[2 * t, QB : QB + QPAD, :].astype(f32)[:8]
        odd = q_in[2 * t + 1, QB : QB + QPAD, :].astype(f32)[:8]
        meta[:, t * E : (t + 1) * E] = jnp.where(wide < QB, even, odd)
    weight = meta[0:1, :]
    position = (meta[1:2, :] * 4096.0 + meta[2:3, :] * 64.0 + meta[3:4, :]).astype(i32)
    block = position >> 9
    y_there = ((block >> 5) & 1) * 2 + ((block >> 7) & 1)
    c_there = (block >> 6) & 1
    slot = (c_there ^ here[1]) * NY + ((here[0] - y_there) & 3)
    local = jnp.where((block & 31) == here[2], slot * CB + (position & (CB - 1)), -1)
    aux[2:3, :] = weight
    aux[3:4, :] = local.astype(f32)

    rows = 256
    queries = q_ext[...]

    def chunk(k, carry):
        top, total = carry
        start = pl.multiple_of(k * rows, rows)
        logits = lax.dot_general(c_ext[pl.ds(start, rows), :], queries, NT, preferred_element_type=f32)
        tall = logits.reshape(rows // 8, 8, NQ)
        new = jnp.maximum(top, jnp.max(tall, axis=0))
        total = total * jnp.exp(top - new) + jnp.sum(jnp.exp(tall - new[None]), axis=0)
        return new, total

    top, total = lax.fori_loop(
        0,
        NC // rows,
        chunk,
        (jnp.full((8, NQ), -jnp.inf, f32), jnp.zeros((8, NQ), f32)),
        unroll=4,
    )
    best = jnp.max(top, axis=0, keepdims=True)
    total = jnp.sum(total * jnp.exp(top - best), axis=0, keepdims=True)
    aux[0:1, :] = best
    aux[1:2, :] = total
    aux[4:8, :] = jnp.zeros((4, NQ), f32)
    lse = best + jnp.log(total)
    tile = jnp.concatenate([lse[:, t * E : (t + 1) * E] for t in range(NQ // E)], axis=0)
    for k in range(NGROUP):
        lse_out[k] = tile


def grad_kernel(base, last, here, c_ext, q_ext, aux, lse_all, *refs):
    if last:
        before, u_out, g_out, acc = refs
    else:
        u_out, g_out, acc = refs
    best = aux[0:1, :]
    weight = aux[2:3, :]
    local = aux[3:4, :].astype(i32)
    theirs = lse_all[...]
    mine = jnp.concatenate([best[:, t * E : (t + 1) * E] for t in range(NQ // E)], axis=0)
    member = lax.broadcasted_iota(i32, (NGROUP, NQ // E, E), 0)
    others = jnp.sum(jnp.where(member == here[2], 0.0, jnp.exp(theirs - mine[None])), axis=0)
    others = jnp.concatenate([others[t : t + 1, :] for t in range(NQ // E)], axis=1)
    scale = weight / (aux[1:2, :] + others)
    rows = 512
    queries = q_ext[...]
    narrow = q_ext[:, :E]
    if last:
        acc[...] = before[...]
    else:
        acc[...] = jnp.zeros_like(acc)

    def chunk(k, carry):
        start = pl.multiple_of(k * rows, rows)
        block = c_ext[pl.ds(base + start, rows), :]
        logits = lax.dot_general(block, queries, NT, preferred_element_type=f32)
        expo = jnp.exp(logits - best) * scale
        matched = lax.broadcasted_iota(i32, (rows, NQ), 0) == (local - (base + start))
        grad = (expo - jnp.where(matched, weight, 0.0)).astype(bf16)
        g_out[k] = lax.dot_general(grad, narrow, NN, preferred_element_type=f32)
        acc[...] += lax.dot_general(block[:, :E].T, grad, NN, preferred_element_type=f32)
        return carry

    lax.fori_loop(0, HALF // rows, chunk, 0)
    if last:
        u_out[...] = acc[...].T
    else:
        u_out[...] = acc[...]


def ring(step):
    place = [(y & 1) * 2 + (y >> 1) for y in range(NY)]
    return [(place[y], place[(y + step) % NY]) for y in range(NY)]


def shaped(shape, dtype):
    return jax.ShapeDtypeStruct(shape, dtype)


PARAMS = pltpu.CompilerParams(vmem_limit_bytes=48 * 2**20)


def per_device(queries, candidates, positive, bucket, query_weight, log_freq):
    y = lax.axis_index("yh") * 2 + lax.axis_index("yl")
    here = jnp.stack([y, lax.axis_index("c"), lax.axis_index(GROUP)]).astype(i32)

    codes = jnp.concatenate([bucket >> 5, bucket & 31]).astype(bf16).reshape(8, E)
    c_block = jnp.concatenate([candidates, codes, jnp.zeros((CPAD - 8, E), bf16)])
    spread = [c_block]
    for s in range(1, NY):
        spread.append(lax.ppermute(c_block, RING, ring(s)))
    own = jnp.stack(spread)
    swap = [(0, 1), (1, 0)]
    other = lax.ppermute(own, "c", swap)

    notes = jnp.stack(
        [
            query_weight,
            (positive >> 12).astype(bf16),
            ((positive >> 6) & 63).astype(bf16),
            (positive & 63).astype(bf16),
        ]
    )
    notes = jnp.concatenate([notes, notes], axis=1)
    q_block = jnp.concatenate([queries, notes, jnp.zeros((QPAD - 4, E), bf16)])
    q_in = lax.all_to_all(
        jnp.broadcast_to(q_block[None], (NGROUP, QB + QPAD, E)), GROUP, 0, 0, tiled=True
    )
    table = jnp.tile(log_freq.reshape(SIDE, SIDE), (1, 4))

    c_ext, q_ext, aux, lse = pl.pallas_call(
        stats_kernel,
        out_shape=[
            shaped((NC, 2 * E), bf16),
            shaped((NQ, 2 * E), bf16),
            shaped((8, NQ), f32),
            shaped((NGROUP, NQ // E, E), f32),
        ],
        in_specs=[SMEM] + [VMEM] * 4,
        out_specs=[VMEM] * 4,
        scratch_shapes=[pltpu.VMEM((8, NQ), f32)],
        compiler_params=PARAMS,
        name="stats",
    )(here, table, q_in, own, other)
    lse_all = lax.all_to_all(lse, GROUP, 0, 0, tiled=True)

    u_part, g_other = pl.pallas_call(
        functools.partial(grad_kernel, HALF, False),
        out_shape=[shaped((E, NQ), f32), shaped((NY, CB, E), f32)],
        in_specs=[SMEM] + [VMEM] * 4,
        out_specs=[VMEM] * 2,
        scratch_shapes=[pltpu.VMEM((E, NQ), f32)],
        compiler_params=PARAMS,
        name="grad_other",
    )(here, c_ext, q_ext, aux, lse_all)
    g_came = lax.ppermute(g_other, "c", swap)
    u_all, g_own = pl.pallas_call(
        functools.partial(grad_kernel, 0, True),
        out_shape=[shaped((NQ, E), f32), shaped((NY, CB, E), f32)],
        in_specs=[SMEM] + [VMEM] * 5,
        out_specs=[VMEM] * 2,
        scratch_shapes=[pltpu.VMEM((E, NQ), f32)],
        compiler_params=PARAMS,
        name="grad_own",
    )(here, c_ext, q_ext, aux, lse_all, u_part)

    g_sum = g_own + g_came
    pieces = [g_sum[0]]
    for s in range(1, NY):
        pieces.append(lax.ppermute(g_sum[s], RING, ring(-s)))
    u_in = lax.all_to_all(u_all.reshape(NGROUP, QB, E), GROUP, 0, 0, tiled=True)
    query_grad = jnp.sum(u_in, axis=0)
    cand_grad = (pieces[0] + pieces[1]) + (pieces[2] + pieces[3])
    return query_grad, cand_grad


def solution(mesh):
    fine = Mesh(mesh.devices.reshape(2, 2, 2, 4, 8), AXES)
    split = P(AXES)
    in_specs = (P(AXES, None), P(AXES, None), split, split, split, P())
    out_specs = (P(AXES, None), P(AXES, None))
    return jax.shard_map(
        per_device, mesh=fine, in_specs=in_specs, out_specs=out_specs, check_vma=False
    )
```

time: 1760 us -> 115 us (0.07)
  blocking collectives: 1250 us -> 16.6 us
  waiting for transfers between devices: 385 us -> 39.5 us
  matrix products: 88.2 us -> 0 us
  Pallas kernels: 0 us -> 28.7 us
  starting transfers between devices: 0.12 us -> 22.3 us
    unnamed x2 -> x0, blocking collectives: 537 us -> none
    reduce_scatter x2 -> x0, waiting for transfers between devices: 384 us -> none  [the longest x1 368 us: per_device(): lax.psum_scatter(query_terms, 'cand', scatter_dimension=0, tiled=True)]
    pmax x1 -> x0, blocking collectives: 353 us -> none  [per_device(): row_max = lax.pmax(own_max, 'cand')]
    psum x1 -> x0, blocking collectives: 351 us -> none  [per_device(): row_total = lax.psum(own_total, 'cand')]
    dot_general x40 -> x0, matrix products: 88.2 us -> none  [the longest x24 52.9 us: block_logits(): lax.dot_general(query_block, columns, (((1,), (1,)), ((), ())), preferred...]
    pallas_call x0 -> x3, Pallas kernels: none -> 28.7 us  [the longest x1 10.6 us: per_device(): pl.pallas_call(stats_kernel, out_shape=[shaped((NC, 2 * E), bf16), shaped...]
    ppermute x0 -> x8, waiting for transfers between devices: none -> 22.8 us  [the longest x3 12.8 us: per_device(): pieces.append(lax.ppermute(g_sum[s], RING, ring(-s)))]
  transfers between devices with their start and end apart: 3 -> 10, of which waited for: 2 -> 8; matrix products, arithmetic and copies ran while one was open for 1% -> 2% of each run, Pallas kernels for 0% -> 0%
where the time goes in v1:
time: 115 us
  waiting for transfers between devices  39.5 us (34%)
  Pallas kernels  28.7 us (25%)
  starting transfers between devices  22.3 us (19%)
  blocking collectives  16.6 us (14%)
  other arithmetic  5.41 us (5%)
  local copies, waits for them, and re-layouts  1.33 us (1%)
    all_to_all x1, blocking collectives, per_device(): lse_all = lax.all_to_all(lse, GROUP, 0, 0, tiled=True)  16.6 us
    ppermute x3, waiting for transfers between devices, per_device(): pieces.append(lax.ppermute(g_sum[s], RING, ring(-s)))  12.8 us
    all_to_all x1, starting transfers between devices, per_device(): lax.all_to_all(jnp.broadcast_to(q_block[None], (NGROUP, QB + QPAD, E)), G...  11.3 us
    pallas_call x1, Pallas kernels, per_device(): pl.pallas_call(stats_kernel, out_shape=[shaped((NC, 2 * E), bf16), shaped...  10.6 us
    pallas_call x1, Pallas kernels, per_device(): pl.pallas_call(functools.partial(grad_kernel, 0, True), out_shape=[shaped...  10.2 us
    all_to_all x1, waiting for transfers between devices, per_device(): lax.all_to_all(jnp.broadcast_to(q_block[None], (NGROUP, QB + QPAD, E)), G...  8.68 us
    all_to_all x1, waiting for transfers between devices, per_device(): u_in = lax.all_to_all(u_all.reshape(NGROUP, QB, E), GROUP, 0, 0, tiled=True)  7.98 us
    pallas_call x1, Pallas kernels, per_device(): pl.pallas_call(functools.partial(grad_kernel, HALF, False), out_shape=[sh...  7.95 us
  transfers between devices with their start and end apart: 10, of which 8 were waited for; matrix products, arithmetic and copies ran while one was open for 2% of the time, Pallas kernels for 0%

profile of v1, /device:TPU:16, one launch (start us, length us, event | category | flops | bytes accessed | tf_op | source)
XLA Modules:
  0.0 114.6 jit_solution(14729206346488073428)
XLA Ops:
  0.7 0.7 convert_bitcast_fusion.2
  1.4 0.8 maximum_maximum_fusion.1
  2.3 0.9 broadcast_in_dim.13
  3.2 11.3 %all-to-all-start = ((bf16[32,80,128]{2,1,0:T(8,128)(2,1)}), bf16[32,80,128]{2,1,0:T(8,128)(2,1)S(1)}, u32[]{:S(2)}, u32[]{:S(2)}) async-start(bf16[32,80,128]{2,1,0:T(8,128)(2,1)} %broadcast_in_dim.13), calls=%async_computation | async-start | bytes 1310720 | tf_op jit(solution)/shard_map/all_to_all | solution.py:183
  14.6 0.7 fusion.2
  15.3 0.1 maximum_maximum_fusion
  15.4 0.4 collective-permute-start.1
  15.8 2.2 %collective-permute-start = (bf16[528,128]{1,0:T(8,128)(2,1)S(1)}, bf16[528,128]{1,0:T(8,128)(2,1)S(1)}, u32[]{:S(2)}, u32[]{:S(2)}) collective-permute-start(bf16[528,128]{1,0:T(8,128)(2,1)S(1)} %maximum_maximum_fusion), channel_id=1, source_target_pairs={{0,128},{128,32},{32,160},{160,0},{1,129},{129,33},{33,161},{161,1... | collective-permute-start | bytes 405512 | tf_op jit(solution)/shard_map/ppermute | solution.py:168
  18.0 0.2 collective-permute-start.2
  18.3 0.1 fusion.4
  18.4 5.1 %collective-permute-done.1 = bf16[528,128]{1,0:T(8,128)(2,1)S(1)} collective-permute-done((bf16[528,128]{1,0:T(8,128)(2,1)S(1)}, bf16[528,128]{1,0:T(8,128)(2,1)S(1)}, u32[]{:S(2)}, u32[]{:S(2)}) %collective-permute-start.1) | collective-permute-done | bytes 135200 | tf_op jit(solution)/shard_map/ppermute | solution.py:168
  23.5 0.6 collective-permute-done
  24.3 0.1 collective-permute-start.3
  24.5 0.1 tile.12.table
  24.7 1.6 %collective-permute-done.3.other = bf16[4,528,128]{2,1,0:T(8,128)(2,1)S(1)} collective-permute-done((bf16[4,528,128]{2,1,0:T(8,128)(2,1)S(1)}, bf16[4,528,128]{2,1,0:T(8,128)(2,1)S(1)}, u32[]{:S(2)}, u32[]{:S(2)}) %collective-permute-start.3) | collective-permute-done | bytes 540704 | tf_op jit(solution)/shard_map/ppermute | solution.py:171
  26.3 8.7 %all-to-all-done.q_in = bf16[32,80,128]{2,1,0:T(8,128)(2,1)S(1)} async-done(((bf16[32,80,128]{2,1,0:T(8,128)(2,1)}), bf16[32,80,128]{2,1,0:T(8,128)(2,1)S(1)}, u32[]{:S(2)}, u32[]{:S(2)}) %all-to-all-start) | async-done | bytes 655392 | tf_op jit(solution)/shard_map/all_to_all | solution.py:183
  35.0 10.6 %stats.1 = (bf16[4096,256]{1,0:T(8,128)(2,1)S(1)}, bf16[2048,256]{1,0:T(8,128)(2,1)S(1)}, f32[8,2048]{1,0:T(8,128)S(1)}, f32[32,16,128]{2,1,0:T(8,128)S(1)}) custom-call(s32[3]{0:T(128)S(1)} %pad_add_fusion.here, f32[32,128]{1,0:T(8,128)S(1)} %tile.12.table, bf16[32,80,128]{2,1,0:T(8,128)(2,1)S(1)} %all-to-all-done.q_in, ...), custom_call_target="tpu_custom_call" | custom-call | tf_op jit(solution)/shard_map/stats/pallas_call | solution.py:188
  45.5 16.6 %all_to_all.15.lse_all = f32[32,16,128]{2,1,0:T(8,128)S(1)} all-to-all(f32[32,16,128]{2,1,0:T(8,128)S(1)} %get-tuple-element.13), channel_id=1, replica_groups=mesh['yl'=2,'c'=2,'yh'=2,'x'=4,'z'=8] {'x','z'}, dimensions={0} | all-to-all | bytes 524288 | tf_op jit(solution)/shard_map/all_to_all | solution.py:202
  62.1 8.0 %grad_other.1 = (f32[128,2048]{1,0:T(8,128)S(1)}, f32[4,512,128]{2,1,0:T(8,128)S(1)}) custom-call(s32[3]{0:T(128)S(1)} %pad_add_fusion.here, bf16[4096,256]{1,0:T(8,128)(2,1)S(1)} %get-tuple-element.10.c_ext, bf16[2048,256]{1,0:T(8,128)(2,1)S(1)} %get-tuple-element.11.q_ext, f32[8,2048]{1,0:T(8,128)S(1)} %get-tuple-element.12.aux, ...), custom_call_target="tpu_custom_call" | custom-call | tf_op jit(solution)/shard_map/grad_other/pallas_call | solution.py:204
  70.1 10.2 %grad_own.1 = (f32[2048,128]{1,0:T(8,128)}, f32[4,512,128]{2,1,0:T(8,128)S(1)}) custom-call(s32[3]{0:T(128)S(1)} %pad_add_fusion.here, bf16[4096,256]{1,0:T(8,128)(2,1)} %copy-done, bf16[2048,256]{1,0:T(8,128)(2,1)S(1)} %get-tuple-element.11.q_ext, f32[8,2048]{1,0:T(8,128)S(1)} %get-tuple-element.12.aux, f32[32,16,128]{2,1,0:T(8,128)S(1)} %all_to_all.15.lse_all, ...), custom_call_target="tpu_custom_call" | custom-call | tf_op jit(solution)/shard_map/grad_own/pallas_call | solution.py:214
  80.3 4.7 %all-to-all-start.2 = ((f32[32,64,128]{2,1,0:T(8,128)}), f32[32,64,128]{2,1,0:T(8,128)}, u32[]{:S(2)}, u32[]{:S(2)}) async-start(f32[32,64,128]{2,1,0:T(8,128)} %bitcast.13), calls=%async_computation.2 | async-start | bytes 2097152 | tf_op jit(solution)/shard_map/all_to_all | solution.py:228
  85.0 0.3 collective-permute-start.4
  85.2 2.6 %collective-permute-done.4 = f32[4,512,128]{2,1,0:T(8,128)S(1)} collective-permute-done((f32[4,512,128]{2,1,0:T(8,128)S(1)}, f32[4,512,128]{2,1,0:T(8,128)S(1)}, u32[]{:S(2)}, u32[]{:S(2)}) %collective-permute-start.4) | collective-permute-done | bytes 1048608 | tf_op jit(solution)/shard_map/ppermute | solution.py:213
  87.9 0.1 add.20
  88.1 1.4 %collective-permute-start.7 = (f32[512,128]{1,0:T(8,128)S(1)}, f32[512,128]{1,0:T(8,128)S(1)}, u32[]{:S(2)}, u32[]{:S(2)}) collective-permute-start(f32[512,128]{1,0:T(8,128)S(1)} %get-tuple-element.18), channel_id=1, source_target_pairs={{0,128},{128,32},{32,160},{160,0},{1,129},{129,33},{33,161},{161,1... | collective-permute-start | bytes 786440 | tf_op jit(solution)/shard_map/ppermute | solution.py:227
  89.4 0.6 collective-permute-start.6
  90.0 1.2 %collective-permute-start.5 = (f32[512,128]{1,0:T(8,128)S(1)}, f32[512,128]{1,0:T(8,128)S(1)}, u32[]{:S(2)}, u32[]{:S(2)}) collective-permute-start(f32[512,128]{1,0:T(8,128)S(1)} %get-tuple-element.20), channel_id=1, source_target_pairs={{0,160},{128,0},{32,128},{160,32},{1,161},{129,1},{33,129},{161,33... | collective-permute-start | bytes 786440 | tf_op jit(solution)/shard_map/ppermute | solution.py:227
  91.2 10.9 %collective-permute-done.7 = f32[512,128]{1,0:T(8,128)S(1)} collective-permute-done((f32[512,128]{1,0:T(8,128)S(1)}, f32[512,128]{1,0:T(8,128)S(1)}, u32[]{:S(2)}, u32[]{:S(2)}) %collective-permute-start.7) | collective-permute-done | bytes 262176 | tf_op jit(solution)/shard_map/ppermute | solution.py:227
  102.1 1.8 %collective-permute-done.5 = f32[512,128]{1,0:T(8,128)S(1)} collective-permute-done((f32[512,128]{1,0:T(8,128)S(1)}, f32[512,128]{1,0:T(8,128)S(1)}, u32[]{:S(2)}, u32[]{:S(2)}) %collective-permute-start.5) | collective-permute-done | bytes 262176 | tf_op jit(solution)/shard_map/ppermute | solution.py:227
  103.9 0.8 fusion.1
  104.7 8.0 %all-to-all-done.2 = f32[32,64,128]{2,1,0:T(8,128)} async-done(((f32[32,64,128]{2,1,0:T(8,128)}), f32[32,64,128]{2,1,0:T(8,128)}, u32[]{:S(2)}, u32[]{:S(2)}) %all-to-all-start.2) | async-done | bytes 1048608 | tf_op jit(solution)/shard_map/all_to_all | solution.py:228
  112.7 1.9 %reduce_sum.9 = f32[64,128]{1,0:T(8,128)} reduce(f32[32,64,128]{2,1,0:T(8,128)} %all-to-all-done.2, f32[]{:T(128)} %constant.39.clone.1), dimensions={0}, to_apply=%region_0.0 | reduce | flops 253952 | bytes 1081348 | tf_op jit(solution)/shard_map/reduce_sum | solution.py:229
  (17 shorter events, 0.5 us)
Async XLA Ops:
  0.6 14.7 %copy-start.1 = (bf16[512,128]{1,0:T(8,128)(2,1)S(1)}, bf16[512,128]{1,0:T(8,128)(2,1)}, u32[]{:S(2)}) copy-start(bf16[512,128]{1,0:T(8,128)(2,1)} %param.7) | copy-start | bytes 393220
  0.6 23.7 %copy-start.2 = (f32[1024]{0:T(1024)S(1)}, f32[1024]{0:T(1024)}, u32[]{:S(2)}) copy-start(f32[1024]{0:T(1024)} %param.11) | copy-start | bytes 12292
  3.2 31.8 %all-to-all-start = ((bf16[32,80,128]{2,1,0:T(8,128)(2,1)}), bf16[32,80,128]{2,1,0:T(8,128)(2,1)S(1)}, u32[]{:S(2)}, u32[]{:S(2)}) async-start(bf16[32,80,128]{2,1,0:T(8,128)(2,1)} %broadcast_in_dim.13), calls=%async_computation | async-start | bytes 1310720 | tf_op jit(solution)/shard_map/all_to_all | solution.py:183
  15.4 8.1 %collective-permute-start.1 = (bf16[528,128]{1,0:T(8,128)(2,1)S(1)}, bf16[528,128]{1,0:T(8,128)(2,1)S(1)}, u32[]{:S(2)}, u32[]{:S(2)}) collective-permute-start(bf16[528,128]{1,0:T(8,128)(2,1)S(1)} %maximum_maximum_fusion), channel_id=1, source_target_pairs={{0,32},{128,160},{32,0},{160,128},{1,33},{129,161},{33,1},{161,129... | collective-permute-start | bytes 405512 | tf_op jit(solution)/shard_map/ppermute | solution.py:168
  15.8 8.3 %collective-permute-start = (bf16[528,128]{1,0:T(8,128)(2,1)S(1)}, bf16[528,128]{1,0:T(8,128)(2,1)S(1)}, u32[]{:S(2)}, u32[]{:S(2)}) collective-permute-start(bf16[528,128]{1,0:T(8,128)(2,1)S(1)} %maximum_maximum_fusion), channel_id=1, source_target_pairs={{0,128},{128,32},{32,160},{160,0},{1,129},{129,33},{33,161},{161,1... | collective-permute-start | bytes 405512 | tf_op jit(solution)/shard_map/ppermute | solution.py:168
  18.0 6.1 %collective-permute-start.2 = (bf16[528,128]{1,0:T(8,128)(2,1)S(1)}, bf16[528,128]{1,0:T(8,128)(2,1)S(1)}, u32[]{:S(2)}, u32[]{:S(2)}) collective-permute-start(bf16[528,128]{1,0:T(8,128)(2,1)S(1)} %maximum_maximum_fusion), channel_id=1, source_target_pairs={{0,160},{128,0},{32,128},{160,32},{1,161},{129,1},{33,129},{161,33... | collective-permute-start | bytes 405512 | tf_op jit(solution)/shard_map/ppermute | solution.py:168
  24.3 2.0 %collective-permute-start.3 = (bf16[4,528,128]{2,1,0:T(8,128)(2,1)S(1)}, bf16[4,528,128]{2,1,0:T(8,128)(2,1)S(1)}, u32[]{:S(2)}, u32[]{:S(2)}) collective-permute-start(bf16[4,528,128]{2,1,0:T(8,128)(2,1)S(1)} %pad_maximum_fusion.own), channel_id=1, source_target_pairs={{0,64},{64,0},{1,65},{65,1},{2,66},{66,2},{3,67},{67,3},{4,68},{68... | collective-permute-start | bytes 1622024 | tf_op jit(solution)/shard_map/ppermute | solution.py:171
  45.5 24.6 %copy-start = (bf16[4096,256]{1,0:T(8,128)(2,1)}, bf16[4096,256]{1,0:T(8,128)(2,1)S(1)}, u32[]{:S(2)}) copy-start(bf16[4096,256]{1,0:T(8,128)(2,1)S(1)} %get-tuple-element.10.c_ext) | copy-start | bytes 6291460
  80.3 32.4 %all-to-all-start.2 = ((f32[32,64,128]{2,1,0:T(8,128)}), f32[32,64,128]{2,1,0:T(8,128)}, u32[]{:S(2)}, u32[]{:S(2)}) async-start(f32[32,64,128]{2,1,0:T(8,128)} %bitcast.13), calls=%async_computation.2 | async-start | bytes 2097152 | tf_op jit(solution)/shard_map/all_to_all | solution.py:228
  85.0 2.9 %collective-permute-start.4 = (f32[4,512,128]{2,1,0:T(8,128)S(1)}, f32[4,512,128]{2,1,0:T(8,128)S(1)}, u32[]{:S(2)}, u32[]{:S(2)}) collective-permute-start(f32[4,512,128]{2,1,0:T(8,128)S(1)} %get-tuple-element.17), channel_id=1, source_target_pairs={{0,64},{64,0},{1,65},{65,1},{2,66},{66,2},{3,67},{67,3},{4,68},{68... | collective-permute-start | bytes 3145736 | tf_op jit(solution)/shard_map/ppermute | solution.py:213
  88.1 14.0 %collective-permute-start.7 = (f32[512,128]{1,0:T(8,128)S(1)}, f32[512,128]{1,0:T(8,128)S(1)}, u32[]{:S(2)}, u32[]{:S(2)}) collective-permute-start(f32[512,128]{1,0:T(8,128)S(1)} %get-tuple-element.18), channel_id=1, source_target_pairs={{0,128},{128,32},{32,160},{160,0},{1,129},{129,33},{33,161},{161,1... | collective-permute-start | bytes 786440 | tf_op jit(solution)/shard_map/ppermute | solution.py:227
  89.4 12.7 %collective-permute-start.6 = (f32[512,128]{1,0:T(8,128)S(1)}, f32[512,128]{1,0:T(8,128)S(1)}, u32[]{:S(2)}, u32[]{:S(2)}) collective-permute-start(f32[512,128]{1,0:T(8,128)S(1)} %get-tuple-element.19), channel_id=1, source_target_pairs={{0,32},{128,160},{32,0},{160,128},{1,33},{129,161},{33,1},{161,129... | collective-permute-start | bytes 786440 | tf_op jit(solution)/shard_map/ppermute | solution.py:227
  90.0 13.9 %collective-permute-start.5 = (f32[512,128]{1,0:T(8,128)S(1)}, f32[512,128]{1,0:T(8,128)S(1)}, u32[]{:S(2)}, u32[]{:S(2)}) collective-permute-start(f32[512,128]{1,0:T(8,128)S(1)} %get-tuple-element.20), channel_id=1, source_target_pairs={{0,160},{128,0},{32,128},{160,32},{1,161},{129,1},{33,129},{161,33... | collective-permute-start | bytes 786440 | tf_op jit(solution)/shard_map/ppermute | solution.py:227

commit v2 on v1

--- a/solution.py
+++ b/solution.py
@@ -16,7 +16,8 @@
 AXES = ("yl", "c", "yh", "x", "z")
 GROUP = ("x", "z")
 RING = ("yl", "yh")
-NY, NCORE, NGROUP = 4, 2, 32
+NY, NX, NZ, NCORE = 4, 4, 8, 2
+NGROUP = NX * NZ
 VMEM = pl.BlockSpec(memory_space=pltpu.VMEM)
 SMEM = pl.BlockSpec(memory_space=pltpu.SMEM)
 E = 128
@@ -27,10 +28,11 @@
 SIDE = 32
 NQ = NGROUP * QB
 HALF = NY * CB
+QUART = NZ * QB
 NC = NCORE * HALF
 
 
-def stats_kernel(here, table, q_in, own, other, c_ext, q_ext, aux, lse_out, meta):
+def stats_kernel(here, table, q0, q1, q2, q3, own, other, c_ext, q_ext, aux, lse_out, meta):
     lane = lax.broadcasted_iota(i32, (SIDE, E), 1)
     row = lax.broadcasted_iota(i32, (SIDE, E), 0)
     freq = table[...]
@@ -58,13 +60,15 @@
                 c_ext[first + r * E : first + (r + 1) * E, E:] = (-(values * mask)).astype(bf16)
 
     wide = lax.broadcasted_iota(i32, (8, E), 1)
-    for k in range(NGROUP):
-        q_ext[k * QB : (k + 1) * QB, :E] = q_in[k, :QB, :]
     q_ext[:, E:] = jnp.ones((NQ, E), bf16)
-    for t in range(NGROUP // 2):
-        even = q_in[2 * t, QB : QB + QPAD, :].astype(f32)[:8]
-        odd = q_in[2 * t + 1, QB : QB + QPAD, :].astype(f32)[:8]
-        meta[:, t * E : (t + 1) * E] = jnp.where(wide < QB, even, odd)
+    for s, q_in in enumerate((q0, q1, q2, q3)):
+        first = pl.multiple_of(((here[2] >> 3) - s & 3) * QUART, QUART)
+        for k in range(NZ):
+            q_ext[pl.ds(first + k * QB, QB), :E] = q_in[k, :QB, :]
+        for t in range(NZ // 2):
+            even = q_in[2 * t, QB : QB + QPAD, :].astype(f32)[:8]
+            odd = q_in[2 * t + 1, QB : QB + QPAD, :].astype(f32)[:8]
+            meta[:, pl.ds(first + t * E, E)] = jnp.where(wide < QB, even, odd)
     weight = meta[0:1, :]
     position = (meta[1:2, :] * 4096.0 + meta[2:3, :] * 64.0 + meta[3:4, :]).astype(i32)
     block = position >> 9
@@ -105,44 +109,67 @@
         lse_out[k] = tile
 
 
-def grad_kernel(base, last, here, c_ext, q_ext, aux, lse_all, *refs):
-    if last:
-        before, u_out, g_out, acc = refs
+def row_scale(here, aux, lse_all, first, count):
+    best = aux[0:1, pl.ds(first, count)]
+    tiles = count // E
+    if count == NQ:
+        theirs = lse_all[...]
     else:
-        u_out, g_out, acc = refs
-    best = aux[0:1, :]
-    weight = aux[2:3, :]
-    local = aux[3:4, :].astype(i32)
-    theirs = lse_all[...]
-    mine = jnp.concatenate([best[:, t * E : (t + 1) * E] for t in range(NQ // E)], axis=0)
-    member = lax.broadcasted_iota(i32, (NGROUP, NQ // E, E), 0)
+        theirs = jnp.concatenate(
+            [lse_all[k, pl.ds(first // E, tiles), :][None] for k in range(NGROUP)], axis=0
+        )
+    mine = jnp.concatenate([best[:, t * E : (t + 1) * E] for t in range(tiles)], axis=0)
+    member = lax.broadcasted_iota(i32, (NGROUP, tiles, E), 0)
     others = jnp.sum(jnp.where(member == here[2], 0.0, jnp.exp(theirs - mine[None])), axis=0)
-    others = jnp.concatenate([others[t : t + 1, :] for t in range(NQ // E)], axis=1)
-    scale = weight / (aux[1:2, :] + others)
-    rows = 512
+    others = jnp.concatenate([others[t : t + 1, :] for t in range(tiles)], axis=1)
+    weight = aux[2:3, pl.ds(first, count)]
+    return weight / (aux[1:2, pl.ds(first, count)] + others)
+
+
+def grad_chunk(c_ext, row, rows, queries, narrow, best, scale, weight, local):
+    block = c_ext[row : row + rows, :]
+    logits = lax.dot_general(block, queries, NT, preferred_element_type=f32)
+    expo = jnp.exp(logits - best) * scale
+    matched = lax.broadcasted_iota(i32, logits.shape, 0) == (local - row)
+    grad = (expo - jnp.where(matched, weight, 0.0)).astype(bf16)
+    g_part = lax.dot_general(grad, narrow, NN, preferred_element_type=f32)
+    u_part = lax.dot_general(block[:, :E].T, grad, NN, preferred_element_type=f32)
+    return g_part, u_part
+
+
+def other_kernel(here, c_ext, q_ext, aux, lse_all, u_out, g_out, aux_out):
+    scale = row_scale(here, aux, lse_all, 0, NQ)
+    aux_out[0:1, :] = aux[0:1, :]
+    aux_out[1:2, :] = scale
+    aux_out[2:8, :] = aux[2:8, :]
     queries = q_ext[...]
-    narrow = q_ext[:, :E]
-    if last:
-        acc[...] = before[...]
-    else:
-        acc[...] = jnp.zeros_like(acc)
-
-    def chunk(k, carry):
-        start = pl.multiple_of(k * rows, rows)
-        block = c_ext[pl.ds(base + start, rows), :]
-        logits = lax.dot_general(block, queries, NT, preferred_element_type=f32)
-        expo = jnp.exp(logits - best) * scale
-        matched = lax.broadcasted_iota(i32, (rows, NQ), 0) == (local - (base + start))
-        grad = (expo - jnp.where(matched, weight, 0.0)).astype(bf16)
-        g_out[k] = lax.dot_general(grad, narrow, NN, preferred_element_type=f32)
-        acc[...] += lax.dot_general(block[:, :E].T, grad, NN, preferred_element_type=f32)
-        return carry
-
-    lax.fori_loop(0, HALF // rows, chunk, 0)
-    if last:
-        u_out[...] = acc[...].T
-    else:
-        u_out[...] = acc[...]
+    total = None
+    for k in range(HALF // CB):
+        g_part, u_part = grad_chunk(
+            c_ext, HALF + k * CB, CB, queries, queries[:, :E], aux[0:1, :], scale, aux[2:3, :],
+            aux[3:4, :].astype(i32),
+        )
+        g_out[k] = g_part
+        total = u_part if total is None else total + u_part
+        u_out[...] = total
+
+
+def own_kernel(shift, here, c_ext, q_ext, aux, before, *refs):
+    g_in = refs[0] if len(refs) == 3 else None
+    u_out, g_out = refs[-2:]
+    first = pl.multiple_of(((here[2] >> 3) - shift & 3) * QUART, QUART)
+    span = pl.ds(first, QUART)
+    queries = q_ext[span, :]
+    total = before[:, span]
+    best, scale, weight = aux[0:1, span], aux[1:2, span], aux[2:3, span]
+    local = aux[3:4, span].astype(i32)
+    for k in range(HALF // CB):
+        g_part, u_part = grad_chunk(
+            c_ext, k * CB, CB, queries, queries[:, :E], best, scale, weight, local
+        )
+        g_out[k] = g_part if g_in is None else g_in[k] + g_part
+        total = total + u_part
+    u_out[...] = total.T
 
 
 def ring(step):
@@ -152,6 +179,12 @@
 
 def shaped(shape, dtype):
     return jax.ShapeDtypeStruct(shape, dtype)
+
+
+def cost(pairs, products):
+    return pl.CostEstimate(
+        flops=2 * pairs * E * products * 2, bytes_accessed=8 * pairs, transcendentals=pairs
+    )
 
 
 PARAMS = pltpu.CompilerParams(vmem_limit_bytes=48 * 2**20)
@@ -180,9 +213,12 @@
     )
     notes = jnp.concatenate([notes, notes], axis=1)
     q_block = jnp.concatenate([queries, notes, jnp.zeros((QPAD - 4, E), bf16)])
-    q_in = lax.all_to_all(
-        jnp.broadcast_to(q_block[None], (NGROUP, QB + QPAD, E)), GROUP, 0, 0, tiled=True
-    )
+    q_line = lax.all_to_all(
+        jnp.broadcast_to(q_block[None], (NZ, QB + QPAD, E)), "z", 0, 0, tiled=True
+    )
+    q_in = [q_line]
+    for s in range(1, NX):
+        q_in.append(lax.ppermute(q_line, "x", [(i, (i + s) % NX) for i in range(NX)]))
     table = jnp.tile(log_freq.reshape(SIDE, SIDE), (1, 4))
 
     c_ext, q_ext, aux, lse = pl.pallas_call(
@@ -193,39 +229,49 @@
             shaped((8, NQ), f32),
             shaped((NGROUP, NQ // E, E), f32),
         ],
-        in_specs=[SMEM] + [VMEM] * 4,
+        in_specs=[SMEM] + [VMEM] * 7,
         out_specs=[VMEM] * 4,
         scratch_shapes=[pltpu.VMEM((8, NQ), f32)],
         compiler_params=PARAMS,
+        cost_estimate=cost(NQ * NC, 1),
         name="stats",
-    )(here, table, q_in, own, other)
+    )(here, table, *q_in, own, other)
     lse_all = lax.all_to_all(lse, GROUP, 0, 0, tiled=True)
 
-    u_part, g_other = pl.pallas_call(
-        functools.partial(grad_kernel, HALF, False),
-        out_shape=[shaped((E, NQ), f32), shaped((NY, CB, E), f32)],
+    u_part, g_other, aux = pl.pallas_call(
+        other_kernel,
+        out_shape=[shaped((E, NQ), f32), shaped((NY, CB, E), f32), shaped((8, NQ), f32)],
         in_specs=[SMEM] + [VMEM] * 4,
-        out_specs=[VMEM] * 2,
-        scratch_shapes=[pltpu.VMEM((E, NQ), f32)],
+        out_specs=[VMEM] * 3,
         compiler_params=PARAMS,
+        cost_estimate=cost(NQ * HALF, 3),
         name="grad_other",
     )(here, c_ext, q_ext, aux, lse_all)
     g_came = lax.ppermute(g_other, "c", swap)
-    u_all, g_own = pl.pallas_call(
-        functools.partial(grad_kernel, 0, True),
-        out_shape=[shaped((NQ, E), f32), shaped((NY, CB, E), f32)],
-        in_specs=[SMEM] + [VMEM] * 5,
-        out_specs=[VMEM] * 2,
-        scratch_shapes=[pltpu.VMEM((E, NQ), f32)],
-        compiler_params=PARAMS,
-        name="grad_own",
-    )(here, c_ext, q_ext, aux, lse_all, u_part)
-
-    g_sum = g_own + g_came
+    g_own = []
+    u_sum = []
+    for shift in (2, 1, 3, 0):
+        u_piece, g_next = pl.pallas_call(
+            functools.partial(own_kernel, shift),
+            out_shape=[shaped((QUART, E), f32), shaped((NY, CB, E), f32)],
+            in_specs=[SMEM] + [VMEM] * (4 + len(g_own)),
+            out_specs=[VMEM] * 2,
+            input_output_aliases={5: 1} if g_own else {},
+            compiler_params=PARAMS,
+            cost_estimate=cost(QUART * HALF, 3),
+            name="grad_own",
+        )(here, c_ext, q_ext, aux, u_part, *g_own)
+        g_own = [g_next]
+        if shift:
+            u_piece = lax.ppermute(u_piece, "x", [(i, (i - shift) % NX) for i in range(NX)])
+        u_sum.append(u_piece)
+
+    g_sum = g_own[0] + g_came
     pieces = [g_sum[0]]
     for s in range(1, NY):
         pieces.append(lax.ppermute(g_sum[s], RING, ring(-s)))
-    u_in = lax.all_to_all(u_all.reshape(NGROUP, QB, E), GROUP, 0, 0, tiled=True)
+    u_line = (u_sum[0] + u_sum[1]) + (u_sum[2] + u_sum[3])
+    u_in = lax.all_to_all(u_line.reshape(NZ, QB, E), "z", 0, 0, tiled=True)
     query_grad = jnp.sum(u_in, axis=0)
     cand_grad = (pieces[0] + pieces[1]) + (pieces[2] + pieces[3])
     return query_grad, cand_grad

time: 115 us -> 121 us (1.052); the launches traced: 115 us -> 119 us
  blocking collectives: 16.6 us -> 33.7 us
  waiting for transfers between devices: 39.5 us -> 26.9 us
  starting transfers between devices: 22.3 us -> 20.4 us
  other arithmetic: 5.41 us -> 6.67 us
    all_to_all x0 -> x1, blocking collectives: none -> 18.7 us  [per_device(): lax.all_to_all(jnp.broadcast_to(q_block[None], (NZ, QB + QPAD, E)), 'z',...]
    ppermute x0 -> x6, waiting for transfers between devices: none -> 13.9 us  [the longest x3 7.87 us: per_device(): lax.ppermute(q_line, 'x', [(i, (i + s) % NX) for i in range(NX)])]
    all_to_all x2 -> x1, starting transfers between devices: 16 us -> 3.41 us  [per_device(): u_in = lax.all_to_all(u_line.reshape(NZ, QB, E), 'z', 0, 0, tiled=True)]
    all_to_all x2 -> x1, waiting for transfers between devices: 16.7 us -> 6.91 us  [per_device(): u_in = lax.all_to_all(u_line.reshape(NZ, QB, E), 'z', 0, 0, tiled=True)]
    ppermute x3, waiting for transfers between devices: 12.8 us -> 3.06 us  [per_device(): pieces.append(lax.ppermute(g_sum[s], RING, ring(-s)))]
    ppermute x0 -> x6, starting transfers between devices: none -> 8.44 us  [the longest x3 4.44 us: per_device(): lax.ppermute(q_line, 'x', [(i, (i + s) % NX) for i in range(NX)])]
    ppermute x3, waiting for transfers between devices: 5.78 us -> 3.06 us  [per_device(): spread.append(lax.ppermute(c_block, RING, ring(s)))]
    ppermute x1, waiting for transfers between devices: 2.65 us -> 0.01 us  [per_device(): g_came = lax.ppermute(g_other, 'c', swap)]
  transfers between devices with their start and end apart: 10 -> 15, of which waited for: 8 -> 10; matrix products, arithmetic and copies ran while one was open for 2% -> 4% of each run, Pallas kernels for 0% -> 10%
where the time goes in v2:
time: 121 us; the launch traced here: 119 us
  blocking collectives  33.7 us (28%)
  Pallas kernels  29.5 us (24%)
  waiting for transfers between devices  26.9 us (22%)
  starting transfers between devices  20.4 us (17%)
  other arithmetic  6.67 us (6%)
    all_to_all x1, blocking collectives, per_device(): lax.all_to_all(jnp.broadcast_to(q_block[None], (NZ, QB + QPAD, E)), 'z',...  18.7 us
    all_to_all x1, blocking collectives, per_device(): lse_all = lax.all_to_all(lse, GROUP, 0, 0, tiled=True)  15 us
    pallas_call x4, Pallas kernels, per_device(): pl.pallas_call(functools.partial(own_kernel, shift), out_shape=[shaped((Q...  11.9 us
    pallas_call x1, Pallas kernels, per_device(): pl.pallas_call(stats_kernel, out_shape=[shaped((NC, 2 * E), bf16), shaped...  10.6 us
    ppermute x3, waiting for transfers between devices, per_device(): lax.ppermute(q_line, 'x', [(i, (i + s) % NX) for i in range(NX)])  7.87 us
    pallas_call x1, Pallas kernels, per_device(): pl.pallas_call(other_kernel, out_shape=[shaped((E, NQ), f32), shaped((NY,...  7.02 us
    all_to_all x1, waiting for transfers between devices, per_device(): u_in = lax.all_to_all(u_line.reshape(NZ, QB, E), 'z', 0, 0, tiled=True)  6.91 us
    ppermute x3, waiting for transfers between devices, per_device(): lax.ppermute(u_piece, 'x', [(i, (i - shift) % NX) for i in range(NX)])  6.04 us
  transfers between devices with their start and end apart: 15, of which 10 were waited for; matrix products, arithmetic and copies ran while one was open for 4% of the time, Pallas kernels for 10%

profile of v2, /device:TPU:16, one launch (start us, length us, event | category | flops | bytes accessed | tf_op | source)
XLA Modules:
  0.0 118.5 jit_solution(8745058321745770001)
XLA Ops:
  1.4 1.0 maximum_maximum_fusion
  2.5 2.2 %collective-permute-start.4 = (bf16[528,128]{1,0:T(8,128)(2,1)S(1)}, bf16[528,128]{1,0:T(8,128)(2,1)S(1)}, u32[]{:S(2)}, u32[]{:S(2)}) collective-permute-start(bf16[528,128]{1,0:T(8,128)(2,1)S(1)} %maximum_maximum_fusion), channel_id=1, source_target_pairs={{0,32},{128,160},{32,0},{160,128},{1,33},{129,161},{33,1},{161,129... | collective-permute-start | bytes 405512 | tf_op jit(solution)/shard_map/ppermute | solution.py:201
  5.1 1.6 %collective-permute-start.5 = (bf16[528,128]{1,0:T(8,128)(2,1)S(1)}, bf16[528,128]{1,0:T(8,128)(2,1)S(1)}, u32[]{:S(2)}, u32[]{:S(2)}) collective-permute-start(bf16[528,128]{1,0:T(8,128)(2,1)S(1)} %maximum_maximum_fusion), channel_id=1, source_target_pairs={{0,160},{128,0},{32,128},{160,32},{1,161},{129,1},{33,129},{161,33... | collective-permute-start | bytes 405512 | tf_op jit(solution)/shard_map/ppermute | solution.py:201
  6.6 1.0 fusion.4
  8.4 2.1 %collective-permute-done.4 = bf16[528,128]{1,0:T(8,128)(2,1)S(1)} collective-permute-done((bf16[528,128]{1,0:T(8,128)(2,1)S(1)}, bf16[528,128]{1,0:T(8,128)(2,1)S(1)}, u32[]{:S(2)}, u32[]{:S(2)}) %collective-permute-start.4) | collective-permute-done | bytes 135200 | tf_op jit(solution)/shard_map/ppermute | solution.py:201
  10.5 1.0 collective-permute-done.3
  11.7 0.8 maximum_maximum_fusion.1
  12.5 18.7 %all_to_all.15.q0 = bf16[8,80,128]{2,1,0:T(8,128)(2,1)S(1)} all-to-all(bf16[8,80,128]{2,1,0:T(8,128)(2,1)S(1)} %broadcast_in_dim.13), channel_id=1, replica_groups=mesh['yl'=2,'c'=2,'yh'=2,'x'=4,'z'=8] {'z'}, dimensions={0} | all-to-all | bytes 327680 | tf_op jit(solution)/shard_map/all_to_all | solution.py:216
  31.2 2.8 %collective-permute-start.2 = (bf16[8,80,128]{2,1,0:T(8,128)(2,1)S(1)}, bf16[8,80,128]{2,1,0:T(8,128)(2,1)S(1)}, u32[]{:S(2)}, u32[]{:S(2)}) collective-permute-start(bf16[8,80,128]{2,1,0:T(8,128)(2,1)S(1)} %all_to_all.15.q0), channel_id=1, source_target_pairs={{0,24},{8,0},{16,8},{24,16},{1,25},{9,1},{17,9},{25,17},{2,26},{10... | collective-permute-start | bytes 491528 | tf_op jit(solution)/shard_map/ppermute | solution.py:221
  34.0 0.8 collective-permute-start.1
  34.8 0.9 collective-permute-start
  36.0 4.2 %collective-permute-done.2.q3 = bf16[8,80,128]{2,1,0:T(8,128)(2,1)S(1)} collective-permute-done((bf16[8,80,128]{2,1,0:T(8,128)(2,1)S(1)}, bf16[8,80,128]{2,1,0:T(8,128)(2,1)S(1)}, u32[]{:S(2)}, u32[]{:S(2)}) %collective-permute-start.2) | collective-permute-done | bytes 163872 | tf_op jit(solution)/shard_map/ppermute | solution.py:221
  40.2 2.0 %collective-permute-done.1.q2 = bf16[8,80,128]{2,1,0:T(8,128)(2,1)S(1)} collective-permute-done((bf16[8,80,128]{2,1,0:T(8,128)(2,1)S(1)}, bf16[8,80,128]{2,1,0:T(8,128)(2,1)S(1)}, u32[]{:S(2)}, u32[]{:S(2)}) %collective-permute-start.1) | collective-permute-done | bytes 163872 | tf_op jit(solution)/shard_map/ppermute | solution.py:221
  42.1 1.7 %collective-permute-done.q1 = bf16[8,80,128]{2,1,0:T(8,128)(2,1)S(1)} collective-permute-done((bf16[8,80,128]{2,1,0:T(8,128)(2,1)S(1)}, bf16[8,80,128]{2,1,0:T(8,128)(2,1)S(1)}, u32[]{:S(2)}, u32[]{:S(2)}) %collective-permute-start) | collective-permute-done | bytes 163872 | tf_op jit(solution)/shard_map/ppermute | solution.py:221
  43.8 10.6 %stats.1 = (bf16[4096,256]{1,0:T(8,128)(2,1)S(1)}, bf16[2048,256]{1,0:T(8,128)(2,1)S(1)}, f32[8,2048]{1,0:T(8,128)S(1)}, f32[32,16,128]{2,1,0:T(8,128)S(1)}) custom-call(s32[3]{0:T(128)S(1)} %pad_add_fusion.here, f32[32,128]{1,0:T(8,128)S(1)} %tile.12.table, bf16[8,80,128]{2,1,0:T(8,128)(2,1)S(1)} %all_to_all.15.q0, ...), custom_call_target="tpu_custom_call" | custom-call | flops 4294967296 | bytes 67108864 | tf_op jit(solution)/shard_map/stats/pallas_call | solution.py:224
  54.4 15.0 %all_to_all.16.lse_all = f32[32,16,128]{2,1,0:T(8,128)S(1)} all-to-all(f32[32,16,128]{2,1,0:T(8,128)S(1)} %get-tuple-element.20), channel_id=1, replica_groups=mesh['yl'=2,'c'=2,'yh'=2,'x'=4,'z'=8] {'x','z'}, dimensions={0} | all-to-all | bytes 524288 | tf_op jit(solution)/shard_map/all_to_all | solution.py:239
  69.5 7.0 %grad_other.1 = (f32[128,2048]{1,0:T(8,128)S(1)}, f32[4,512,128]{2,1,0:T(8,128)S(1)}, f32[8,2048]{1,0:T(8,128)S(1)}) custom-call(s32[3]{0:T(128)S(1)} %pad_add_fusion.here, bf16[4096,256]{1,0:T(8,128)(2,1)S(1)} %get-tuple-element.17.c_ext, bf16[2048,256]{1,0:T(8,128)(2,1)S(1)} %get-tuple-element.18.q_ext, f32[8,2048]{1,0:T(8,128)S(1)} %get-tuple-element.19.aux, ...), custom_call_target="tpu_custom_call" | custom-call | flops 6442450944 | bytes 33554432 | tf_op jit(solution)/shard_map/grad_other/pallas_call | solution.py:241
  76.6 2.8 %grad_own.4 = (f32[512,128]{1,0:T(8,128)S(1)}, f32[4,512,128]{2,1,0:T(8,128)S(1)}) custom-call(s32[3]{0:T(128)S(1)} %pad_add_fusion.here, bf16[4096,256]{1,0:T(8,128)(2,1)S(1)} %get-tuple-element.17.c_ext, bf16[2048,256]{1,0:T(8,128)(2,1)S(1)} %get-tuple-element.18.q_ext, f32[8,2048]{1,0:T(8,128)S(1)} %get-tuple-element.21.aux, ...), custom_call_target="tpu_custom_call" | custom-call | flops 1610612736 | bytes 8388608 | tf_op jit(solution)/shard_map/grad_own/pallas_call | solution.py:254
  79.4 1.6 %collective-permute-start.7 = (f32[512,128]{1,0:T(8,128)S(1)}, f32[512,128]{1,0:T(8,128)S(1)}, u32[]{:S(2)}, u32[]{:S(2)}) collective-permute-start(f32[512,128]{1,0:T(8,128)S(1)} %get-tuple-element.23), channel_id=1, source_target_pairs={{0,16},{8,24},{16,0},{24,8},{1,17},{9,25},{17,1},{25,9},{2,18},{10... | collective-permute-start | bytes 786440 | tf_op jit(solution)/shard_map/ppermute | solution.py:266
  81.0 3.0 %grad_own.5 = (f32[512,128]{1,0:T(8,128)S(1)}, f32[4,512,128]{2,1,0:T(8,128)S(1)}) custom-call(s32[3]{0:T(128)S(1)} %pad_add_fusion.here, bf16[4096,256]{1,0:T(8,128)(2,1)S(1)} %get-tuple-element.17.c_ext, bf16[2048,256]{1,0:T(8,128)(2,1)S(1)} %get-tuple-element.18.q_ext, f32[8,2048]{1,0:T(8,128)S(1)} %get-tuple-element.21.aux, ...), custom_call_target="tpu_custom_call", output_to_operand_aliasing={{1}: (5, {})} | custom-call | flops 1610612736 | bytes 8388608 | tf_op jit(solution)/shard_map/grad_own/pallas_call | solution.py:254
  84.0 2.1 %collective-permute-start.8 = (f32[512,128]{1,0:T(8,128)S(1)}, f32[512,128]{1,0:T(8,128)S(1)}, u32[]{:S(2)}, u32[]{:S(2)}) collective-permute-start(f32[512,128]{1,0:T(8,128)S(1)} %get-tuple-element.25), channel_id=1, source_target_pairs={{0,24},{8,0},{16,8},{24,16},{1,25},{9,1},{17,9},{25,17},{2,26},{10... | collective-permute-start | bytes 786440 | tf_op jit(solution)/shard_map/ppermute | solution.py:266
  86.1 3.1 %grad_own.6 = (f32[512,128]{1,0:T(8,128)S(1)}, f32[4,512,128]{2,1,0:T(8,128)S(1)}) custom-call(s32[3]{0:T(128)S(1)} %pad_add_fusion.here, bf16[4096,256]{1,0:T(8,128)(2,1)S(1)} %get-tuple-element.17.c_ext, bf16[2048,256]{1,0:T(8,128)(2,1)S(1)} %get-tuple-element.18.q_ext, f32[8,2048]{1,0:T(8,128)S(1)} %get-tuple-element.21.aux, ...), custom_call_target="tpu_custom_call", output_to_operand_aliasing={{1}: (5, {})} | custom-call | flops 1610612736 | bytes 8388608 | tf_op jit(solution)/shard_map/grad_own/pallas_call | solution.py:254
  89.5 3.1 %grad_own.7 = (f32[512,128]{1,0:T(8,128)S(1)}, f32[4,512,128]{2,1,0:T(8,128)S(1)}) custom-call(s32[3]{0:T(128)S(1)} %pad_add_fusion.here, bf16[4096,256]{1,0:T(8,128)(2,1)S(1)} %get-tuple-element.17.c_ext, bf16[2048,256]{1,0:T(8,128)(2,1)S(1)} %get-tuple-element.18.q_ext, f32[8,2048]{1,0:T(8,128)S(1)} %get-tuple-element.21.aux, ...), custom_call_target="tpu_custom_call", output_to_operand_aliasing={{1}: (5, {})} | custom-call | flops 1610612736 | bytes 8388608 | tf_op jit(solution)/shard_map/grad_own/pallas_call | solution.py:254
  92.6 1.3 %collective-permute-done.8 = f32[512,128]{1,0:T(8,128)S(1)} collective-permute-done((f32[512,128]{1,0:T(8,128)S(1)}, f32[512,128]{1,0:T(8,128)S(1)}, u32[]{:S(2)}, u32[]{:S(2)}) %collective-permute-start.8) | collective-permute-done | bytes 262176 | tf_op jit(solution)/shard_map/ppermute | solution.py:266
  93.8 4.8 %collective-permute-done.9 = f32[512,128]{1,0:T(8,128)S(1)} collective-permute-done((f32[512,128]{1,0:T(8,128)S(1)}, f32[512,128]{1,0:T(8,128)S(1)}, u32[]{:S(2)}, u32[]{:S(2)}) %collective-permute-start.9) | collective-permute-done | bytes 262176 | tf_op jit(solution)/shard_map/ppermute | solution.py:266
  98.6 0.8 add_add_fusion
  99.4 3.4 %all-to-all-start.2 = ((f32[8,64,128]{2,1,0:T(8,128)}), f32[8,64,128]{2,1,0:T(8,128)S(1)}, u32[]{:S(2)}, u32[]{:S(2)}) async-start(f32[8,64,128]{2,1,0:T(8,128)} %bitcast.13), calls=%async_computation.2 | async-start | bytes 524288 | tf_op jit(solution)/shard_map/all_to_all | solution.py:274
  103.0 2.6 %collective-permute-start.13 = (f32[512,128]{1,0:T(8,128)S(1)}, f32[512,128]{1,0:T(8,128)S(1)}, u32[]{:S(2)}, u32[]{:S(2)}) collective-permute-start(f32[512,128]{1,0:T(8,128)S(1)} %get-tuple-element.32), channel_id=1, source_target_pairs={{0,128},{128,32},{32,160},{160,0},{1,129},{129,33},{33,161},{161,1... | collective-permute-start | bytes 786440 | tf_op jit(solution)/shard_map/ppermute | solution.py:272
  105.9 1.3 %collective-permute-start.11 = (f32[512,128]{1,0:T(8,128)S(1)}, f32[512,128]{1,0:T(8,128)S(1)}, u32[]{:S(2)}, u32[]{:S(2)}) collective-permute-start(f32[512,128]{1,0:T(8,128)S(1)} %get-tuple-element.34), channel_id=1, source_target_pairs={{0,160},{128,0},{32,128},{160,32},{1,161},{129,1},{33,129},{161,33... | collective-permute-start | bytes 786440 | tf_op jit(solution)/shard_map/ppermute | solution.py:272
  107.2 6.9 %all-to-all-done.2 = f32[8,64,128]{2,1,0:T(8,128)S(1)} async-done(((f32[8,64,128]{2,1,0:T(8,128)}), f32[8,64,128]{2,1,0:T(8,128)S(1)}, u32[]{:S(2)}, u32[]{:S(2)}) %all-to-all-start.2) | async-done | bytes 262176 | tf_op jit(solution)/shard_map/all_to_all | solution.py:274
  114.7 2.1 %collective-permute-done.12 = f32[512,128]{1,0:T(8,128)S(1)} collective-permute-done((f32[512,128]{1,0:T(8,128)S(1)}, f32[512,128]{1,0:T(8,128)S(1)}, u32[]{:S(2)}, u32[]{:S(2)}) %collective-permute-start.12) | collective-permute-done | bytes 262176 | tf_op jit(solution)/shard_map/ppermute | solution.py:272
  116.8 1.0 collective-permute-done.11
  (28 shorter events, 4.8 us)
Async XLA Ops:
  0.6 35.0 %copy-start = (f32[1024]{0:T(1024)S(1)}, f32[1024]{0:T(1024)}, u32[]{:S(2)}) copy-start(f32[1024]{0:T(1024)} %param.11) | copy-start | bytes 12292
  2.5 8.1 %collective-permute-start.4 = (bf16[528,128]{1,0:T(8,128)(2,1)S(1)}, bf16[528,128]{1,0:T(8,128)(2,1)S(1)}, u32[]{:S(2)}, u32[]{:S(2)}) collective-permute-start(bf16[528,128]{1,0:T(8,128)(2,1)S(1)} %maximum_maximum_fusion), channel_id=1, source_target_pairs={{0,32},{128,160},{32,0},{160,128},{1,33},{129,161},{33,1},{161,129... | collective-permute-start | bytes 405512 | tf_op jit(solution)/shard_map/ppermute | solution.py:201
  4.6 6.9 %collective-permute-start.3 = (bf16[528,128]{1,0:T(8,128)(2,1)S(1)}, bf16[528,128]{1,0:T(8,128)(2,1)S(1)}, u32[]{:S(2)}, u32[]{:S(2)}) collective-permute-start(bf16[528,128]{1,0:T(8,128)(2,1)S(1)} %maximum_maximum_fusion), channel_id=1, source_target_pairs={{0,128},{128,32},{32,160},{160,0},{1,129},{129,33},{33,161},{161,1... | collective-permute-start | bytes 405512 | tf_op jit(solution)/shard_map/ppermute | solution.py:201
  5.1 6.4 %collective-permute-start.5 = (bf16[528,128]{1,0:T(8,128)(2,1)S(1)}, bf16[528,128]{1,0:T(8,128)(2,1)S(1)}, u32[]{:S(2)}, u32[]{:S(2)}) collective-permute-start(bf16[528,128]{1,0:T(8,128)(2,1)S(1)} %maximum_maximum_fusion), channel_id=1, source_target_pairs={{0,160},{128,0},{32,128},{160,32},{1,161},{129,1},{33,129},{161,33... | collective-permute-start | bytes 405512 | tf_op jit(solution)/shard_map/ppermute | solution.py:201
  11.6 32.3 %collective-permute-start.6 = (bf16[4,528,128]{2,1,0:T(8,128)(2,1)S(1)}, bf16[4,528,128]{2,1,0:T(8,128)(2,1)S(1)}, u32[]{:S(2)}, u32[]{:S(2)}) collective-permute-start(bf16[4,528,128]{2,1,0:T(8,128)(2,1)S(1)} %pad_maximum_fusion.own), channel_id=1, source_target_pairs={{0,64},{64,0},{1,65},{65,1},{2,66},{66,2},{3,67},{67,3},{4,68},{68... | collective-permute-start | bytes 1622024 | tf_op jit(solution)/shard_map/ppermute | solution.py:204
  31.2 8.9 %collective-permute-start.2 = (bf16[8,80,128]{2,1,0:T(8,128)(2,1)S(1)}, bf16[8,80,128]{2,1,0:T(8,128)(2,1)S(1)}, u32[]{:S(2)}, u32[]{:S(2)}) collective-permute-start(bf16[8,80,128]{2,1,0:T(8,128)(2,1)S(1)} %all_to_all.15.q0), channel_id=1, source_target_pairs={{0,24},{8,0},{16,8},{24,16},{1,25},{9,1},{17,9},{25,17},{2,26},{10... | collective-permute-start | bytes 491528 | tf_op jit(solution)/shard_map/ppermute | solution.py:221
  34.0 8.1 %collective-permute-start.1 = (bf16[8,80,128]{2,1,0:T(8,128)(2,1)S(1)}, bf16[8,80,128]{2,1,0:T(8,128)(2,1)S(1)}, u32[]{:S(2)}, u32[]{:S(2)}) collective-permute-start(bf16[8,80,128]{2,1,0:T(8,128)(2,1)S(1)} %all_to_all.15.q0), channel_id=1, source_target_pairs={{0,16},{8,24},{16,0},{24,8},{1,17},{9,25},{17,1},{25,9},{2,18},{10... | collective-permute-start | bytes 491528 | tf_op jit(solution)/shard_map/ppermute | solution.py:221
  34.8 9.0 %collective-permute-start = (bf16[8,80,128]{2,1,0:T(8,128)(2,1)S(1)}, bf16[8,80,128]{2,1,0:T(8,128)(2,1)S(1)}, u32[]{:S(2)}, u32[]{:S(2)}) collective-permute-start(bf16[8,80,128]{2,1,0:T(8,128)(2,1)S(1)} %all_to_all.15.q0), channel_id=1, source_target_pairs={{0,8},{8,16},{16,24},{24,0},{1,9},{9,17},{17,25},{25,1},{2,10},{10... | collective-permute-start | bytes 491528 | tf_op jit(solution)/shard_map/ppermute | solution.py:221
  76.5 26.3 %collective-permute-start.10 = (f32[4,512,128]{2,1,0:T(8,128)S(1)}, f32[4,512,128]{2,1,0:T(8,128)S(1)}, u32[]{:S(2)}, u32[]{:S(2)}) collective-permute-start(f32[4,512,128]{2,1,0:T(8,128)S(1)} %get-tuple-element.31), channel_id=1, source_target_pairs={{0,64},{64,0},{1,65},{65,1},{2,66},{66,2},{3,67},{67,3},{4,68},{68... | collective-permute-start | bytes 3145736 | tf_op jit(solution)/shard_map/ppermute | solution.py:250
  79.4 13.2 %collective-permute-start.7 = (f32[512,128]{1,0:T(8,128)S(1)}, f32[512,128]{1,0:T(8,128)S(1)}, u32[]{:S(2)}, u32[]{:S(2)}) collective-permute-start(f32[512,128]{1,0:T(8,128)S(1)} %get-tuple-element.23), channel_id=1, source_target_pairs={{0,16},{8,24},{16,0},{24,8},{1,17},{9,25},{17,1},{25,9},{2,18},{10... | collective-permute-start | bytes 786440 | tf_op jit(solution)/shard_map/ppermute | solution.py:266
  84.0 9.8 %collective-permute-start.8 = (f32[512,128]{1,0:T(8,128)S(1)}, f32[512,128]{1,0:T(8,128)S(1)}, u32[]{:S(2)}, u32[]{:S(2)}) collective-permute-start(f32[512,128]{1,0:T(8,128)S(1)} %get-tuple-element.25), channel_id=1, source_target_pairs={{0,24},{8,0},{16,8},{24,16},{1,25},{9,1},{17,9},{25,17},{2,26},{10... | collective-permute-start | bytes 786440 | tf_op jit(solution)/shard_map/ppermute | solution.py:266
  89.2 9.4 %collective-permute-start.9 = (f32[512,128]{1,0:T(8,128)S(1)}, f32[512,128]{1,0:T(8,128)S(1)}, u32[]{:S(2)}, u32[]{:S(2)}) collective-permute-start(f32[512,128]{1,0:T(8,128)S(1)} %get-tuple-element.27), channel_id=1, source_target_pairs={{0,8},{8,16},{16,24},{24,0},{1,9},{9,17},{17,25},{25,1},{2,10},{10... | collective-permute-start | bytes 786440 | tf_op jit(solution)/shard_map/ppermute | solution.py:266
  99.4 14.7 %all-to-all-start.2 = ((f32[8,64,128]{2,1,0:T(8,128)}), f32[8,64,128]{2,1,0:T(8,128)S(1)}, u32[]{:S(2)}, u32[]{:S(2)}) async-start(f32[8,64,128]{2,1,0:T(8,128)} %bitcast.13), calls=%async_computation.2 | async-start | bytes 524288 | tf_op jit(solution)/shard_map/all_to_all | solution.py:274
  103.0 11.8 %collective-permute-start.13 = (f32[512,128]{1,0:T(8,128)S(1)}, f32[512,128]{1,0:T(8,128)S(1)}, u32[]{:S(2)}, u32[]{:S(2)}) collective-permute-start(f32[512,128]{1,0:T(8,128)S(1)} %get-tuple-element.32), channel_id=1, source_target_pairs={{0,128},{128,32},{32,160},{160,0},{1,129},{129,33},{33,161},{161,1... | collective-permute-start | bytes 786440 | tf_op jit(solution)/shard_map/ppermute | solution.py:272
  105.5 11.3 %collective-permute-start.12 = (f32[512,128]{1,0:T(8,128)S(1)}, f32[512,128]{1,0:T(8,128)S(1)}, u32[]{:S(2)}, u32[]{:S(2)}) collective-permute-start(f32[512,128]{1,0:T(8,128)S(1)} %get-tuple-element.33), channel_id=1, source_target_pairs={{0,32},{128,160},{32,0},{160,128},{1,33},{129,161},{33,1},{161,129... | collective-permute-start | bytes 786440 | tf_op jit(solution)/shard_map/ppermute | solution.py:272
  105.9 11.9 %collective-permute-start.11 = (f32[512,128]{1,0:T(8,128)S(1)}, f32[512,128]{1,0:T(8,128)S(1)}, u32[]{:S(2)}, u32[]{:S(2)}) collective-permute-start(f32[512,128]{1,0:T(8,128)S(1)} %get-tuple-element.34), channel_id=1, source_target_pairs={{0,160},{128,0},{32,128},{160,32},{1,161},{129,1},{33,129},{161,33... | collective-permute-start | bytes 786440 | tf_op jit(solution)/shard_map/ppermute | solution.py:272

commit v3 on v1

v3 whole, which is shorter than its diff:
```python
import functools

import jax
import jax.numpy as jnp
from jax import lax
from jax.experimental import pallas as pl
from jax.experimental.pallas import tpu as pltpu
from jax.sharding import Mesh, PartitionSpec as P

bf16 = jnp.bfloat16
f32 = jnp.float32
i32 = jnp.int32
NT = (((1,), (1,)), ((), ()))
NN = (((1,), (0,)), ((), ()))
TN = (((0,), (0,)), ((), ()))
AXES = ("yl", "c", "yh", "x", "z")
GROUP = ("x", "z")
RING = ("yl", "yh")
NY, NX, NZ, NCORE = 4, 4, 8, 2
NGROUP = NX * NZ
VMEM = pl.BlockSpec(memory_space=pltpu.VMEM)
SMEM = pl.BlockSpec(memory_space=pltpu.SMEM)
E = 128
QB = 64
CB = 512
QPAD = 8
CPAD = 16
SIDE = 32
NQ = NGROUP * QB
HALF = NY * CB
QUART = NZ * QB
NC = NCORE * HALF


def pack_kernel(queries, positive, weight, candidates, bucket, q_out, c_out):
    place = positive[...]
    rows = [
        weight[...].astype(f32),
        (place >> 12).astype(f32),
        ((place >> 6) & 63).astype(f32),
        (place & 63).astype(f32),
        jnp.zeros((QPAD - 4, QB), f32),
    ]
    notes = jnp.concatenate(rows, axis=0)
    notes = jnp.concatenate([notes, notes], axis=1).astype(bf16)
    block = queries[...]
    for k in range(NGROUP):
        q_out[k, :QB, :] = block
        q_out[k, QB:, :] = notes
    codes = bucket[...]
    c_out[:CB, :] = candidates[...]
    c_out[CB:, :] = jnp.concatenate(
        [(codes >> 5).astype(f32), (codes & 31).astype(f32), jnp.zeros((CPAD - 8, E), f32)], axis=0
    ).astype(bf16)


def stats_kernel(here, table, q_in, own, other, c_ext, q_ext, aux, lse_out, meta, ref_max, sums):
    lane = lax.broadcasted_iota(i32, (SIDE, E), 1)
    row = lax.broadcasted_iota(i32, (SIDE, E), 0)
    freq = table[...]
    high = freq.astype(bf16).astype(f32)
    rest = freq - high
    middle = rest.astype(bf16).astype(f32)
    low = rest - middle
    parts = jnp.where(
        lane < SIDE, high, jnp.where(lane < 2 * SIDE, middle, jnp.where(lane < 3 * SIDE, low, 0.0))
    ).astype(bf16)
    pick = ((lane & (SIDE - 1)) == row).astype(f32).astype(bf16)

    for core, block_ref in enumerate((own, other)):
        for s in range(NY):
            first = core * HALF + s * CB
            c_ext[first : first + CB, :E] = block_ref[s, :CB, :]
            codes = block_ref[s, CB : CB + CPAD, :].astype(f32)
            for r in range(CB // E):
                major = codes[r : r + 1, :].astype(i32)
                minor = codes[4 + r : 5 + r, :].astype(i32)
                hot_major = (row == major).astype(f32).astype(bf16)
                hot_minor = (row == minor).astype(f32).astype(bf16)
                values = lax.dot_general(hot_major, parts, TN, preferred_element_type=f32)
                mask = lax.dot_general(hot_minor, pick, TN, preferred_element_type=f32)
                c_ext[first + r * E : first + (r + 1) * E, E:] = (-(values * mask)).astype(bf16)

    wide = lax.broadcasted_iota(i32, (8, E), 1)
    q_ext[:, E:] = jnp.ones((NQ, E), bf16)
    for k in range(NGROUP):
        q_ext[k * QB : (k + 1) * QB, :E] = q_in[k, :QB, :]
    for t in range(NGROUP // 2):
        even = q_in[2 * t, QB : QB + QPAD, :].astype(f32)
        odd = q_in[2 * t + 1, QB : QB + QPAD, :].astype(f32)
        meta[:, t * E : (t + 1) * E] = jnp.where(wide < QB, even, odd)
    weight = meta[0:1, :]
    position = (meta[1:2, :] * 4096.0 + meta[2:3, :] * 64.0 + meta[3:4, :]).astype(i32)
    block = position >> 9
    y_there = ((block >> 5) & 1) * 2 + ((block >> 7) & 1)
    c_there = (block >> 6) & 1
    slot = (c_there ^ here[1]) * NY + ((here[0] - y_there) & 3)
    local = jnp.where((block & 31) == here[2], slot * CB + (position & (CB - 1)), -1)
    aux[2:3, :] = weight
    aux[3:4, :] = local.astype(f32)

    rows = 512
    queries = q_ext[...]

    def tall(k):
        start = k * rows if isinstance(k, int) else pl.multiple_of(k * rows, rows)
        logits = lax.dot_general(c_ext[pl.ds(start, rows), :], queries, NT, preferred_element_type=f32)
        return logits.reshape(rows // 8, 8, NQ)

    def summed(logits, shift):
        return jnp.sum(jnp.exp(logits - shift[None]), axis=0)

    block = tall(0)
    first = jnp.max(block, axis=0)
    top, total = first, summed(block, first)
    ref_max[...] = first
    for k in range(1, NC // rows):
        block = tall(k)
        top = jnp.maximum(top, jnp.max(block, axis=0))
        total = total + summed(block, ref_max[...])
    sums[...] = total
    best = jnp.max(top, axis=0, keepdims=True)

    @pl.when(jnp.max(top - ref_max[...]) > 40.0)
    def _():
        peak = jnp.broadcast_to(best, (8, NQ))
        ref_max[...] = peak
        sums[...] = lax.fori_loop(
            0, NC // rows, lambda k, acc: acc + summed(tall(k), peak), jnp.zeros((8, NQ), f32)
        )

    total = jnp.sum(sums[...] * jnp.exp(ref_max[...] - best), axis=0, keepdims=True)
    aux[0:1, :] = best
    aux[1:2, :] = total
    aux[4:8, :] = jnp.zeros((4, NQ), f32)
    lse = best + jnp.log(total)
    tile = jnp.concatenate([lse[:, t * E : (t + 1) * E] for t in range(NQ // E)], axis=0)
    for k in range(NGROUP):
        lse_out[k] = tile


def row_scale(here, aux, lse_all, first, count):
    best = aux[0:1, pl.ds(first, count)]
    tiles = count // E
    if count == NQ:
        theirs = lse_all[...]
    else:
        theirs = jnp.concatenate(
            [lse_all[k, pl.ds(first // E, tiles), :][None] for k in range(NGROUP)], axis=0
        )
    mine = jnp.concatenate([best[:, t * E : (t + 1) * E] for t in range(tiles)], axis=0)
    member = lax.broadcasted_iota(i32, (NGROUP, tiles, E), 0)
    others = jnp.sum(jnp.where(member == here[2], 0.0, jnp.exp(theirs - mine[None])), axis=0)
    others = jnp.concatenate([others[t : t + 1, :] for t in range(tiles)], axis=1)
    weight = aux[2:3, pl.ds(first, count)]
    return weight / (aux[1:2, pl.ds(first, count)] + others)


def grad_kernel(shift, halves, here, c_ext, q_ext, aux, lse_all, *refs):
    n = len(halves)
    before = refs[: len(refs) - 1 - n]
    u_out, g_outs = refs[-1 - n], refs[-n:]
    u_in = before[0] if len(before) in (1, n + 1) and shift == 0 and halves == (0,) else None
    g_ins = before[-n:] if len(before) >= n and shift != 2 else [None] * n
    first = pl.multiple_of(((here[2] >> 3) - shift & 3) * QUART, QUART)
    span = pl.ds(first, QUART)
    scale = row_scale(here, aux, lse_all, first, QUART)
    queries = q_ext[span, :]
    narrow = queries[:, :E]
    best, weight = aux[0:1, span], aux[2:3, span]
    local = aux[3:4, span].astype(i32)
    total = jnp.zeros((QUART, E), f32) if u_in is None else u_in[...]
    for half, g_in, g_out in zip(halves, g_ins, g_outs):
        for k in range(NY):
            row = half * HALF + k * CB
            block = c_ext[row : row + CB, :]
            logits = lax.dot_general(block, queries, NT, preferred_element_type=f32)
            expo = jnp.exp(logits - best) * scale
            matched = lax.broadcasted_iota(i32, logits.shape, 0) == (local - row)
            grad = (expo - jnp.where(matched, weight, 0.0)).astype(bf16)
            g_part = lax.dot_general(grad, narrow, NN, preferred_element_type=f32)
            g_out[k] = g_part if g_in is None else g_in[k] + g_part
            total = total + lax.dot_general(grad, block[:, :E], TN, preferred_element_type=f32)
    u_out[...] = total


def merge_kernel(own, came, *outs):
    for s, out in enumerate(outs):
        out[...] = own[s] + came[s]


def ring(step):
    place = [(y & 1) * 2 + (y >> 1) for y in range(NY)]
    return [(place[y], place[(y + step) % NY]) for y in range(NY)]


def shaped(shape, dtype):
    return jax.ShapeDtypeStruct(shape, dtype)


def cost(pairs, products):
    return pl.CostEstimate(
        flops=pairs * E * products // 2, bytes_accessed=pairs, transcendentals=pairs // 8
    )


PARAMS = pltpu.CompilerParams(vmem_limit_bytes=48 * 2**20)


def per_device(queries, candidates, positive, bucket, query_weight, log_freq):
    y = lax.axis_index("yh") * 2 + lax.axis_index("yl")
    here = jnp.stack([y, lax.axis_index("c"), lax.axis_index(GROUP)]).astype(i32)

    q_block, c_block = pl.pallas_call(
        pack_kernel,
        out_shape=[shaped((NGROUP, QB + QPAD, E), bf16), shaped((CB + CPAD, E), bf16)],
        in_specs=[VMEM] * 5,
        out_specs=[VMEM] * 2,
        compiler_params=pltpu.CompilerParams(vmem_limit_bytes=60 * 2**20),
        name="pack",
    )(
        queries,
        positive.reshape(1, QB),
        query_weight.reshape(1, QB),
        candidates,
        bucket.reshape(4, E),
    )
    q_in = lax.all_to_all(q_block, GROUP, 0, 0, tiled=True)
    spread = [c_block]
    for s in range(1, NY):
        spread.append(lax.ppermute(c_block, RING, ring(s)))
    own = jnp.stack(spread)
    swap = [(0, 1), (1, 0)]
    other = lax.ppermute(own, "c", swap)

    table = jnp.tile(log_freq.reshape(SIDE, SIDE), (1, 4))

    c_ext, q_ext, aux, lse = pl.pallas_call(
        stats_kernel,
        out_shape=[
            shaped((NC, 2 * E), bf16),
            shaped((NQ, 2 * E), bf16),
            shaped((8, NQ), f32),
            shaped((NGROUP, NQ // E, E), f32),
        ],
        in_specs=[SMEM] + [VMEM] * 4,
        out_specs=[VMEM] * 4,
        scratch_shapes=[pltpu.VMEM((8, NQ), f32)] * 3,
        compiler_params=PARAMS,
        cost_estimate=cost(NQ * NC, 1),
        name="stats",
    )(here, table, q_in, own, other)
    lse_all = lax.all_to_all(lse, GROUP, 0, 0, tiled=True)

    def grads(shift, halves, *extra, aliases):
        n = len(halves)
        return pl.pallas_call(
            functools.partial(grad_kernel, shift, halves),
            out_shape=[shaped((QUART, E), f32)] + [shaped((NY, CB, E), f32)] * n,
            in_specs=[SMEM] + [VMEM] * (4 + len(extra)),
            out_specs=[VMEM] * (1 + n),
            input_output_aliases=aliases,
            compiler_params=PARAMS,
            cost_estimate=cost(QUART * HALF * n, 3),
            name="grad",
        )(here, c_ext, q_ext, aux, lse_all, *extra)

    def along_x(piece, shift):
        return lax.ppermute(piece, "x", [(i, (i - shift) % NX) for i in range(NX)])

    piece, g_a, g_b = grads(2, (0, 1), aliases={})
    u_two = along_x(piece, 2)
    piece, g_a, g_b = grads(1, (0, 1), g_a, g_b, aliases={5: 1, 6: 2})
    u_one = along_x(piece, 1)
    piece, g_a, g_b = grads(3, (0, 1), g_a, g_b, aliases={5: 1, 6: 2})
    u_three = along_x(piece, 3)
    u_two, g_b = lax.optimization_barrier((u_two, g_b))
    u_own, g_other = grads(0, (1,), g_b, aliases={5: 1})
    u_one, g_other = lax.optimization_barrier((u_one, g_other))
    g_came = lax.ppermute(g_other, "c", swap)
    u_own, g_own = grads(0, (0,), u_own, g_a, aliases={5: 0, 6: 1})

    pieces = pl.pallas_call(
        merge_kernel,
        out_shape=[shaped((CB, E), f32)] * NY,
        in_specs=[VMEM] * 2,
        out_specs=[VMEM] * NY,
        compiler_params=PARAMS,
        name="merge",
    )(g_own, g_came)
    u_sum = [u_two, u_one, u_three, u_own]
    u_sum[3], *pieces = lax.optimization_barrier((u_sum[3], *pieces))
    for s in range(1, NY):
        pieces[s] = lax.ppermute(pieces[s], RING, ring(-s))
    u_line = (u_sum[0] + u_sum[1]) + (u_sum[2] + u_sum[3])
    u_in = lax.all_to_all(u_line.reshape(NZ, QB, E), "z", 0, 0, tiled=True)
    query_grad = jnp.sum(u_in, axis=0)
    cand_grad = (pieces[0] + pieces[1]) + (pieces[2] + pieces[3])
    return query_grad, cand_grad


def solution(mesh):
    fine = Mesh(mesh.devices.reshape(2, 2, 2, 4, 8), AXES)
    split = P(AXES)
    in_specs = (P(AXES, None), P(AXES, None), split, split, split, P())
    out_specs = (P(AXES, None), P(AXES, None))
    return jax.shard_map(
        per_device, mesh=fine, in_specs=in_specs, out_specs=out_specs, check_vma=False
    )
```

time: 115 us -> 112 us (0.974); the launches traced: 115 us -> 110 us
  waiting for transfers between devices: 39.5 us -> 26.4 us
  Pallas kernels: 28.7 us -> 34.8 us
  starting transfers between devices: 22.3 us -> 27.5 us
  other arithmetic: 5.41 us -> 3.19 us
  local copies, waits for them, and re-layouts: 1.33 us -> 0.18 us
    ppermute x3 -> x6, waiting for transfers between devices: 12.8 us -> 6.36 us  [the longest x3 4.75 us: per_device(): pieces[s] = lax.ppermute(pieces[s], RING, ring(-s))]
    ppermute x3 -> x6, starting transfers between devices: 3.09 us -> 9.21 us  [the longest x3 5.21 us: per_device(): pieces[s] = lax.ppermute(pieces[s], RING, ring(-s))]
    all_to_all x2, waiting for transfers between devices: 16.7 us -> 11.9 us  [the longest x1 6.36 us: per_device(): u_in = lax.all_to_all(u_line.reshape(NZ, QB, E), 'z', 0, 0, tiled=True)]
    pallas_call x1, Pallas kernels: 10.6 us -> 13.9 us  [per_device(): pl.pallas_call(stats_kernel, out_shape=[shaped((NC, 2 * E), bf16), shaped...]
    pallas_call x2 -> x7, Pallas kernels: 18.1 us -> 20.9 us  [the longest x5 18.9 us: grads(): pl.pallas_call(functools.partial(grad_kernel, shift, halves), out_shape=[...]
    ppermute x1, waiting for transfers between devices: 2.65 us -> 0.01 us  [per_device(): g_came = lax.ppermute(g_other, 'c', swap)]
    concatenate x3 -> x0, other arithmetic: 1.66 us -> none  [the longest x1 0.83 us: per_device(): q_block = jnp.concatenate([queries, notes, jnp.zeros((QPAD - 4, E), bf16)])]
    reduce_sum x1, other arithmetic: 1.91 us -> 0.63 us  [per_device(): query_grad = jnp.sum(u_in, axis=0)]
  transfers between devices with their start and end apart: 10 -> 13, of which waited for: 8 -> 9; matrix products, arithmetic and copies ran while one was open for 2% -> 2% of each run, Pallas kernels for 0% -> 13%
where the time goes in v3:
time: 112 us; the launch traced here: 110 us
  Pallas kernels  34.8 us (31%)
  starting transfers between devices  27.5 us (25%)
  waiting for transfers between devices  26.4 us (24%)
  blocking collectives  16.9 us (15%)
  other arithmetic  3.19 us (3%)
    pallas_call x5, Pallas kernels, grads(): pl.pallas_call(functools.partial(grad_kernel, shift, halves), out_shape=[...  18.9 us
    all_to_all x1, blocking collectives, per_device(): lse_all = lax.all_to_all(lse, GROUP, 0, 0, tiled=True)  16.9 us
    pallas_call x1, Pallas kernels, per_device(): pl.pallas_call(stats_kernel, out_shape=[shaped((NC, 2 * E), bf16), shaped...  13.9 us
    all_to_all x1, starting transfers between devices, per_device(): q_in = lax.all_to_all(q_block, GROUP, 0, 0, tiled=True)  11.3 us
    ppermute x3, waiting for transfers between devices, per_device(): spread.append(lax.ppermute(c_block, RING, ring(s)))  6.47 us
    all_to_all x1, waiting for transfers between devices, per_device(): u_in = lax.all_to_all(u_line.reshape(NZ, QB, E), 'z', 0, 0, tiled=True)  6.36 us
    all_to_all x1, waiting for transfers between devices, per_device(): q_in = lax.all_to_all(q_block, GROUP, 0, 0, tiled=True)  5.56 us
    ppermute x3, starting transfers between devices, per_device(): pieces[s] = lax.ppermute(pieces[s], RING, ring(-s))  5.21 us
  transfers between devices with their start and end apart: 13, of which 9 were waited for; matrix products, arithmetic and copies ran while one was open for 2% of the time, Pallas kernels for 13%

profile of v3, /device:TPU:16, one launch (start us, length us, event | category | flops | bytes accessed | tf_op | source)
XLA Modules:
  0.0 109.8 jit_solution(6969459060011966604)
XLA Ops:
  0.6 1.9 %pack.1 = (bf16[32,72,128]{2,1,0:T(8,128)(2,1)}, bf16[528,128]{1,0:T(8,128)(2,1)}) custom-call(bf16[64,128]{1,0:T(8,128)(2,1)} %queries.1, s32[1,64]{1,0:T(1,128)} %bitcast.16, bf16[1,64]{1,0:T(2,128)(2,1)} %bitcast.17, bf16[512,128]{1,0:T(8,128)(2,1)} %candidates.1, s32[4,128]{1,0:T(4,128)} %bitcast.15), custom_call_target="tpu_custom_call" | custom-call | tf_op jit(solution)/shard_map/pack/pallas_call | solution.py:214
  2.5 11.3 %all-to-all-start = ((bf16[32,72,128]{2,1,0:T(8,128)(2,1)}), bf16[32,72,128]{2,1,0:T(8,128)(2,1)S(1)}, u32[]{:S(2)}, u32[]{:S(2)}) async-start(bf16[32,72,128]{2,1,0:T(8,128)(2,1)} %get-tuple-element.34), calls=%async_computation | async-start | bytes 1179648 | tf_op jit(solution)/shard_map/all_to_all | solution.py:228
  13.8 0.5 collective-permute-start.2
  14.4 2.9 %collective-permute-start.1 = (bf16[528,128]{1,0:T(8,128)(2,1)}, bf16[528,128]{1,0:T(8,128)(2,1)S(1)}, u32[]{:S(2)}, u32[]{:S(2)}) collective-permute-start(bf16[528,128]{1,0:T(8,128)(2,1)} %get-tuple-element.35), channel_id=1, source_target_pairs={{0,32},{128,160},{32,0},{160,128},{1,33},{129,161},{33,1},{161,129... | collective-permute-start | bytes 405512 | tf_op jit(solution)/shard_map/ppermute | solution.py:231
  17.3 3.3 %collective-permute-done.2 = bf16[528,128]{1,0:T(8,128)(2,1)S(1)} collective-permute-done((bf16[528,128]{1,0:T(8,128)(2,1)}, bf16[528,128]{1,0:T(8,128)(2,1)S(1)}, u32[]{:S(2)}, u32[]{:S(2)}) %collective-permute-start.2) | collective-permute-done | bytes 135200 | tf_op jit(solution)/shard_map/ppermute | solution.py:231
  20.6 1.7 %collective-permute-done.1 = bf16[528,128]{1,0:T(8,128)(2,1)S(1)} collective-permute-done((bf16[528,128]{1,0:T(8,128)(2,1)}, bf16[528,128]{1,0:T(8,128)(2,1)S(1)}, u32[]{:S(2)}, u32[]{:S(2)}) %collective-permute-start.1) | collective-permute-done | bytes 135200 | tf_op jit(solution)/shard_map/ppermute | solution.py:231
  22.3 1.4 %collective-permute-done = bf16[528,128]{1,0:T(8,128)(2,1)S(1)} collective-permute-done((bf16[528,128]{1,0:T(8,128)(2,1)}, bf16[528,128]{1,0:T(8,128)(2,1)S(1)}, u32[]{:S(2)}, u32[]{:S(2)}) %collective-permute-start) | collective-permute-done | bytes 135200 | tf_op jit(solution)/shard_map/ppermute | solution.py:231
  23.7 1.0 pad_maximum_fusion.own
  25.1 1.6 %collective-permute-done.3.other = bf16[4,528,128]{2,1,0:T(8,128)(2,1)S(1)} collective-permute-done((bf16[4,528,128]{2,1,0:T(8,128)(2,1)S(1)}, bf16[4,528,128]{2,1,0:T(8,128)(2,1)S(1)}, u32[]{:S(2)}, u32[]{:S(2)}) %collective-permute-start.3) | collective-permute-done | bytes 540704 | tf_op jit(solution)/shard_map/ppermute | solution.py:234
  26.7 5.6 %all-to-all-done.q_in = bf16[32,72,128]{2,1,0:T(8,128)(2,1)S(1)} async-done(((bf16[32,72,128]{2,1,0:T(8,128)(2,1)}), bf16[32,72,128]{2,1,0:T(8,128)(2,1)S(1)}, u32[]{:S(2)}, u32[]{:S(2)}) %all-to-all-start) | async-done | bytes 589856 | tf_op jit(solution)/shard_map/all_to_all | solution.py:228
  32.3 13.9 %stats.1 = (bf16[4096,256]{1,0:T(8,128)(2,1)S(1)}, bf16[2048,256]{1,0:T(8,128)(2,1)S(1)}, f32[8,2048]{1,0:T(8,128)S(1)}, f32[32,16,128]{2,1,0:T(8,128)S(1)}) custom-call(s32[3]{0:T(128)S(1)} %pad_add_fusion.here, f32[32,128]{1,0:T(8,128)S(1)} %tile.12.table, bf16[32,72,128]{2,1,0:T(8,128)(2,1)S(1)} %all-to-all-done.q_in, ...), custom_call_target="tpu_custom_call" | custom-call | flops 536870912 | bytes 8388608 | tf_op jit(solution)/shard_map/stats/pallas_call | solution.py:238
  46.3 16.9 %all_to_all.15.lse_all = f32[32,16,128]{2,1,0:T(8,128)S(1)} all-to-all(f32[32,16,128]{2,1,0:T(8,128)S(1)} %get-tuple-element.39), channel_id=1, replica_groups=mesh['yl'=2,'c'=2,'yh'=2,'x'=4,'z'=8] {'x','z'}, dimensions={0} | all-to-all | bytes 524288 | tf_op jit(solution)/shard_map/all_to_all | solution.py:253
  63.1 4.6 %grad.5 = (f32[512,128]{1,0:T(8,128)S(1)}, f32[4,512,128]{2,1,0:T(8,128)S(1)}, f32[4,512,128]{2,1,0:T(8,128)S(1)}) custom-call(s32[3]{0:T(128)S(1)} %pad_add_fusion.here, bf16[4096,256]{1,0:T(8,128)(2,1)S(1)} %get-tuple-element.36.c_ext, bf16[2048,256]{1,0:T(8,128)(2,1)S(1)} %get-tuple-element.37.q_ext, f32[8,2048]{1,0:T(8,128)S(1)} %get-tuple-element.38.aux, ...), custom_call_target="tpu_custom_call" | custom-call | flops 402653184 | bytes 2097152 | tf_op jit(solution)/shard_map/grad/pallas_call | solution.py:257
  67.7 1.6 %collective-permute-start.4 = (f32[512,128]{1,0:T(8,128)S(1)}, f32[512,128]{1,0:T(8,128)S(1)}, u32[]{:S(2)}, u32[]{:S(2)}) collective-permute-start(f32[512,128]{1,0:T(8,128)S(1)} %get-tuple-element.40), channel_id=1, source_target_pairs={{0,16},{8,24},{16,0},{24,8},{1,17},{9,25},{17,1},{25,9},{2,18},{10... | collective-permute-start | bytes 786440 | tf_op jit(solution)/shard_map/ppermute | solution.py:269
  69.3 4.5 %grad.6 = (f32[512,128]{1,0:T(8,128)S(1)}, f32[4,512,128]{2,1,0:T(8,128)S(1)}, f32[4,512,128]{2,1,0:T(8,128)S(1)}) custom-call(s32[3]{0:T(128)S(1)} %pad_add_fusion.here, bf16[4096,256]{1,0:T(8,128)(2,1)S(1)} %get-tuple-element.36.c_ext, bf16[2048,256]{1,0:T(8,128)(2,1)S(1)} %get-tuple-element.37.q_ext, ...), custom_call_target="tpu_custom_call", output_to_operand_aliasing={{1}: (5, {}), {2}: (6, {})} | custom-call | flops 402653184 | bytes 2097152 | tf_op jit(solution)/shard_map/grad/pallas_call | solution.py:257
  73.8 2.1 %collective-permute-start.5 = (f32[512,128]{1,0:T(8,128)S(1)}, f32[512,128]{1,0:T(8,128)S(1)}, u32[]{:S(2)}, u32[]{:S(2)}) collective-permute-start(f32[512,128]{1,0:T(8,128)S(1)} %get-tuple-element.47), channel_id=1, source_target_pairs={{0,24},{8,0},{16,8},{24,16},{1,25},{9,1},{17,9},{25,17},{2,26},{10... | collective-permute-start | bytes 786440 | tf_op jit(solution)/shard_map/ppermute | solution.py:269
  75.9 4.5 %grad.7 = (f32[512,128]{1,0:T(8,128)S(1)}, f32[4,512,128]{2,1,0:T(8,128)S(1)}, f32[4,512,128]{2,1,0:T(8,128)S(1)}) custom-call(s32[3]{0:T(128)S(1)} %pad_add_fusion.here, bf16[4096,256]{1,0:T(8,128)(2,1)S(1)} %get-tuple-element.36.c_ext, bf16[2048,256]{1,0:T(8,128)(2,1)S(1)} %get-tuple-element.37.q_ext, ...), custom_call_target="tpu_custom_call", output_to_operand_aliasing={{1}: (5, {}), {2}: (6, {})} | custom-call | flops 402653184 | bytes 2097152 | tf_op jit(solution)/shard_map/grad/pallas_call | solution.py:257
  80.3 2.7 %grad.8 = (f32[512,128]{1,0:T(8,128)S(1)}, f32[4,512,128]{2,1,0:T(8,128)S(1)}) custom-call(s32[3]{0:T(128)S(1)} %pad_add_fusion.here, bf16[4096,256]{1,0:T(8,128)(2,1)S(1)} %get-tuple-element.36.c_ext, bf16[2048,256]{1,0:T(8,128)(2,1)S(1)} %get-tuple-element.37.q_ext, f32[8,2048]{1,0:T(8,128)S(1)} %get-tuple-element.38.aux, ...), custom_call_target="tpu_custom_call", output_to_operand_aliasing={{1}: (5, {})} | custom-call | flops 201326592 | bytes 1048576 | tf_op jit(solution)/shard_map/grad/pallas_call | solution.py:257
  83.2 0.3 collective-permute-start.6
  83.5 2.6 %grad.9 = (f32[512,128]{1,0:T(8,128)S(1)}, f32[4,512,128]{2,1,0:T(8,128)S(1)}) custom-call(s32[3]{0:T(128)S(1)} %pad_add_fusion.here, bf16[4096,256]{1,0:T(8,128)(2,1)S(1)} %get-tuple-element.36.c_ext, bf16[2048,256]{1,0:T(8,128)(2,1)S(1)} %get-tuple-element.37.q_ext, ...), custom_call_target="tpu_custom_call", output_to_operand_aliasing={{0}: (5, {}), {1}: (6, {})} | custom-call | flops 201326592 | bytes 1048576 | tf_op jit(solution)/shard_map/grad/pallas_call | solution.py:257
  86.2 0.1 merge.1
  86.3 0.5 collective-permute-start.8
  86.8 2.9 %collective-permute-start.9 = (f32[512,128]{1,0:T(8,128)S(1)}, f32[512,128]{1,0:T(8,128)S(1)}, u32[]{:S(2)}, u32[]{:S(2)}) collective-permute-start(f32[512,128]{1,0:T(8,128)S(1)} %get-tuple-element.64), channel_id=1, source_target_pairs={{0,32},{128,160},{32,0},{160,128},{1,33},{129,161},{33,1},{161,129... | collective-permute-start | bytes 786440 | tf_op jit(solution)/shard_map/ppermute | solution.py:294
  89.7 1.8 %collective-permute-start.10 = (f32[512,128]{1,0:T(8,128)S(1)}, f32[512,128]{1,0:T(8,128)S(1)}, u32[]{:S(2)}, u32[]{:S(2)}) collective-permute-start(f32[512,128]{1,0:T(8,128)S(1)} %get-tuple-element.65), channel_id=1, source_target_pairs={{0,128},{128,32},{32,160},{160,0},{1,129},{129,33},{33,161},{161,1... | collective-permute-start | bytes 786440 | tf_op jit(solution)/shard_map/ppermute | solution.py:294
  91.5 1.6 %collective-permute-done.6 = f32[512,128]{1,0:T(8,128)S(1)} collective-permute-done((f32[512,128]{1,0:T(8,128)S(1)}, f32[512,128]{1,0:T(8,128)S(1)}, u32[]{:S(2)}, u32[]{:S(2)}) %collective-permute-start.6) | collective-permute-done | bytes 262176 | tf_op jit(solution)/shard_map/ppermute | solution.py:269
  93.1 0.7 add_add_fusion.1
  93.8 3.4 %all-to-all-start.2 = ((f32[8,64,128]{2,1,0:T(8,128)}), f32[8,64,128]{2,1,0:T(8,128)S(1)}, u32[]{:S(2)}, u32[]{:S(2)}) async-start(f32[8,64,128]{2,1,0:T(8,128)} %bitcast.10), calls=%async_computation.2 | async-start | bytes 524288 | tf_op jit(solution)/shard_map/all_to_all | solution.py:296
  97.3 0.3 collective-permute-done.9
  97.5 4.5 %collective-permute-done.10 = f32[512,128]{1,0:T(8,128)S(1)} collective-permute-done((f32[512,128]{1,0:T(8,128)S(1)}, f32[512,128]{1,0:T(8,128)S(1)}, u32[]{:S(2)}, u32[]{:S(2)}) %collective-permute-start.10) | collective-permute-done | bytes 262176 | tf_op jit(solution)/shard_map/ppermute | solution.py:294
  102.0 0.8 add_add_fusion
  102.8 6.4 %all-to-all-done.2 = f32[8,64,128]{2,1,0:T(8,128)S(1)} async-done(((f32[8,64,128]{2,1,0:T(8,128)}), f32[8,64,128]{2,1,0:T(8,128)S(1)}, u32[]{:S(2)}, u32[]{:S(2)}) %all-to-all-start.2) | async-done | bytes 262176 | tf_op jit(solution)/shard_map/all_to_all | solution.py:296
  109.1 0.6 reduce_sum.9
  (13 shorter events, 0.5 us)
Async XLA Ops:
  0.6 24.2 %copy-start = (f32[1024]{0:T(1024)S(1)}, f32[1024]{0:T(1024)}, u32[]{:S(2)}) copy-start(f32[1024]{0:T(1024)} %param.11) | copy-start | bytes 12292
  2.5 29.8 %all-to-all-start = ((bf16[32,72,128]{2,1,0:T(8,128)(2,1)}), bf16[32,72,128]{2,1,0:T(8,128)(2,1)S(1)}, u32[]{:S(2)}, u32[]{:S(2)}) async-start(bf16[32,72,128]{2,1,0:T(8,128)(2,1)} %get-tuple-element.34), calls=%async_computation | async-start | bytes 1179648 | tf_op jit(solution)/shard_map/all_to_all | solution.py:228
  13.8 6.8 %collective-permute-start.2 = (bf16[528,128]{1,0:T(8,128)(2,1)}, bf16[528,128]{1,0:T(8,128)(2,1)S(1)}, u32[]{:S(2)}, u32[]{:S(2)}) collective-permute-start(bf16[528,128]{1,0:T(8,128)(2,1)} %get-tuple-element.35), channel_id=1, source_target_pairs={{0,160},{128,0},{32,128},{160,32},{1,161},{129,1},{33,129},{161,33... | collective-permute-start | bytes 405512 | tf_op jit(solution)/shard_map/ppermute | solution.py:231
  14.4 8.0 %collective-permute-start.1 = (bf16[528,128]{1,0:T(8,128)(2,1)}, bf16[528,128]{1,0:T(8,128)(2,1)S(1)}, u32[]{:S(2)}, u32[]{:S(2)}) collective-permute-start(bf16[528,128]{1,0:T(8,128)(2,1)} %get-tuple-element.35), channel_id=1, source_target_pairs={{0,32},{128,160},{32,0},{160,128},{1,33},{129,161},{33,1},{161,129... | collective-permute-start | bytes 405512 | tf_op jit(solution)/shard_map/ppermute | solution.py:231
  17.3 6.5 %collective-permute-start = (bf16[528,128]{1,0:T(8,128)(2,1)}, bf16[528,128]{1,0:T(8,128)(2,1)S(1)}, u32[]{:S(2)}, u32[]{:S(2)}) collective-permute-start(bf16[528,128]{1,0:T(8,128)(2,1)} %get-tuple-element.35), channel_id=1, source_target_pairs={{0,128},{128,32},{32,160},{160,0},{1,129},{129,33},{33,161},{161,1... | collective-permute-start | bytes 405512 | tf_op jit(solution)/shard_map/ppermute | solution.py:231
  24.7 2.0 %collective-permute-start.3 = (bf16[4,528,128]{2,1,0:T(8,128)(2,1)S(1)}, bf16[4,528,128]{2,1,0:T(8,128)(2,1)S(1)}, u32[]{:S(2)}, u32[]{:S(2)}) collective-permute-start(bf16[4,528,128]{2,1,0:T(8,128)(2,1)S(1)} %pad_maximum_fusion.own), channel_id=1, source_target_pairs={{0,64},{64,0},{1,65},{65,1},{2,66},{66,2},{3,67},{67,3},{4,68},{68... | collective-permute-start | bytes 1622024 | tf_op jit(solution)/shard_map/ppermute | solution.py:234
  67.7 12.6 %collective-permute-start.4 = (f32[512,128]{1,0:T(8,128)S(1)}, f32[512,128]{1,0:T(8,128)S(1)}, u32[]{:S(2)}, u32[]{:S(2)}) collective-permute-start(f32[512,128]{1,0:T(8,128)S(1)} %get-tuple-element.40), channel_id=1, source_target_pairs={{0,16},{8,24},{16,0},{24,8},{1,17},{9,25},{17,1},{25,9},{2,18},{10... | collective-permute-start | bytes 786440 | tf_op jit(solution)/shard_map/ppermute | solution.py:269
  73.8 9.2 %collective-permute-start.5 = (f32[512,128]{1,0:T(8,128)S(1)}, f32[512,128]{1,0:T(8,128)S(1)}, u32[]{:S(2)}, u32[]{:S(2)}) collective-permute-start(f32[512,128]{1,0:T(8,128)S(1)} %get-tuple-element.47), channel_id=1, source_target_pairs={{0,24},{8,0},{16,8},{24,16},{1,25},{9,1},{17,9},{25,17},{2,26},{10... | collective-permute-start | bytes 786440 | tf_op jit(solution)/shard_map/ppermute | solution.py:269
  83.1 3.1 %collective-permute-start.7 = (f32[4,512,128]{2,1,0:T(8,128)S(1)}, f32[4,512,128]{2,1,0:T(8,128)S(1)}, u32[]{:S(2)}, u32[]{:S(2)}) collective-permute-start(f32[4,512,128]{2,1,0:T(8,128)S(1)} %get-tuple-element.56), channel_id=1, source_target_pairs={{0,64},{64,0},{1,65},{65,1},{2,66},{66,2},{3,67},{67,3},{4,68},{68... | collective-permute-start | bytes 3145736 | tf_op jit(solution)/shard_map/ppermute | solution.py:280
  83.2 9.9 %collective-permute-start.6 = (f32[512,128]{1,0:T(8,128)S(1)}, f32[512,128]{1,0:T(8,128)S(1)}, u32[]{:S(2)}, u32[]{:S(2)}) collective-permute-start(f32[512,128]{1,0:T(8,128)S(1)} %get-tuple-element.51), channel_id=1, source_target_pairs={{0,8},{8,16},{16,24},{24,0},{1,9},{9,17},{17,25},{25,1},{2,10},{10... | collective-permute-start | bytes 786440 | tf_op jit(solution)/shard_map/ppermute | solution.py:269
  86.3 11.0 %collective-permute-start.8 = (f32[512,128]{1,0:T(8,128)S(1)}, f32[512,128]{1,0:T(8,128)S(1)}, u32[]{:S(2)}, u32[]{:S(2)}) collective-permute-start(f32[512,128]{1,0:T(8,128)S(1)} %get-tuple-element.63), channel_id=1, source_target_pairs={{0,160},{128,0},{32,128},{160,32},{1,161},{129,1},{33,129},{161,33... | collective-permute-start | bytes 786440 | tf_op jit(solution)/shard_map/ppermute | solution.py:294
  86.8 10.7 %collective-permute-start.9 = (f32[512,128]{1,0:T(8,128)S(1)}, f32[512,128]{1,0:T(8,128)S(1)}, u32[]{:S(2)}, u32[]{:S(2)}) collective-permute-start(f32[512,128]{1,0:T(8,128)S(1)} %get-tuple-element.64), channel_id=1, source_target_pairs={{0,32},{128,160},{32,0},{160,128},{1,33},{129,161},{33,1},{161,129... | collective-permute-start | bytes 786440 | tf_op jit(solution)/shard_map/ppermute | solution.py:294
  89.7 12.3 %collective-permute-start.10 = (f32[512,128]{1,0:T(8,128)S(1)}, f32[512,128]{1,0:T(8,128)S(1)}, u32[]{:S(2)}, u32[]{:S(2)}) collective-permute-start(f32[512,128]{1,0:T(8,128)S(1)} %get-tuple-element.65), channel_id=1, source_target_pairs={{0,128},{128,32},{32,160},{160,0},{1,129},{129,33},{33,161},{161,1... | collective-permute-start | bytes 786440 | tf_op jit(solution)/shard_map/ppermute | solution.py:294
  93.8 15.3 %all-to-all-start.2 = ((f32[8,64,128]{2,1,0:T(8,128)}), f32[8,64,128]{2,1,0:T(8,128)S(1)}, u32[]{:S(2)}, u32[]{:S(2)}) async-start(f32[8,64,128]{2,1,0:T(8,128)} %bitcast.10), calls=%async_computation.2 | async-start | bytes 524288 | tf_op jit(solution)/shard_map/all_to_all | solution.py:296

commit v4 on v3

--- a/solution.py
+++ b/solution.py
@@ -29,6 +29,7 @@
 NQ = NGROUP * QB
 HALF = NY * CB
 QUART = NZ * QB
+KEPT = 7
 NC = NCORE * HALF
 
 
@@ -54,7 +55,8 @@
     ).astype(bf16)
 
 
-def stats_kernel(here, table, q_in, own, other, c_ext, q_ext, aux, lse_out, meta, ref_max, sums):
+def stats_kernel(here, table, q_in, own, other, c_ext, q_ext, aux, lse_out, *refs):
+    kept, (meta, ref_max, sums) = refs[:KEPT], refs[KEPT:]
     lane = lax.broadcasted_iota(i32, (SIDE, E), 1)
     row = lax.broadcasted_iota(i32, (SIDE, E), 0)
     freq = table[...]
@@ -105,6 +107,8 @@
     def tall(k):
         start = k * rows if isinstance(k, int) else pl.multiple_of(k * rows, rows)
         logits = lax.dot_general(c_ext[pl.ds(start, rows), :], queries, NT, preferred_element_type=f32)
+        if isinstance(k, int) and k < KEPT:
+            kept[k][...] = logits
         return logits.reshape(rows // 8, 8, NQ)
 
     def summed(logits, shift):
@@ -158,6 +162,7 @@
 
 def grad_kernel(shift, halves, here, c_ext, q_ext, aux, lse_all, *refs):
     n = len(halves)
+    kept, refs = refs[: KEPT], refs[KEPT:]
     before = refs[: len(refs) - 1 - n]
     u_out, g_outs = refs[-1 - n], refs[-n:]
     u_in = before[0] if len(before) in (1, n + 1) and shift == 0 and halves == (0,) else None
@@ -174,7 +179,10 @@
         for k in range(NY):
             row = half * HALF + k * CB
             block = c_ext[row : row + CB, :]
-            logits = lax.dot_general(block, queries, NT, preferred_element_type=f32)
+            if half * NY + k < KEPT:
+                logits = kept[half * NY + k][:, span]
+            else:
+                logits = lax.dot_general(block, queries, NT, preferred_element_type=f32)
             expo = jnp.exp(logits - best) * scale
             matched = lax.broadcasted_iota(i32, logits.shape, 0) == (local - row)
             grad = (expo - jnp.where(matched, weight, 0.0)).astype(bf16)
@@ -204,7 +212,7 @@
     )
 
 
-PARAMS = pltpu.CompilerParams(vmem_limit_bytes=48 * 2**20)
+PARAMS = pltpu.CompilerParams(vmem_limit_bytes=18 * 2**20)
 
 
 def per_device(queries, candidates, positive, bucket, query_weight, log_freq):
@@ -235,16 +243,17 @@
 
     table = jnp.tile(log_freq.reshape(SIDE, SIDE), (1, 4))
 
-    c_ext, q_ext, aux, lse = pl.pallas_call(
+    c_ext, q_ext, aux, lse, *kept = pl.pallas_call(
         stats_kernel,
         out_shape=[
             shaped((NC, 2 * E), bf16),
             shaped((NQ, 2 * E), bf16),
             shaped((8, NQ), f32),
             shaped((NGROUP, NQ // E, E), f32),
-        ],
+        ]
+        + [shaped((CB, NQ), f32)] * KEPT,
         in_specs=[SMEM] + [VMEM] * 4,
-        out_specs=[VMEM] * 4,
+        out_specs=[VMEM] * (4 + KEPT),
         scratch_shapes=[pltpu.VMEM((8, NQ), f32)] * 3,
         compiler_params=PARAMS,
         cost_estimate=cost(NQ * NC, 1),
@@ -257,13 +266,13 @@
         return pl.pallas_call(
             functools.partial(grad_kernel, shift, halves),
             out_shape=[shaped((QUART, E), f32)] + [shaped((NY, CB, E), f32)] * n,
-            in_specs=[SMEM] + [VMEM] * (4 + len(extra)),
+            in_specs=[SMEM] + [VMEM] * (4 + KEPT + len(extra)),
             out_specs=[VMEM] * (1 + n),
-            input_output_aliases=aliases,
+            input_output_aliases={i + KEPT: o for i, o in aliases.items()},
             compiler_params=PARAMS,
             cost_estimate=cost(QUART * HALF * n, 3),
             name="grad",
-        )(here, c_ext, q_ext, aux, lse_all, *extra)
+        )(here, c_ext, q_ext, aux, lse_all, *kept, *extra)
 
     def along_x(piece, shift):
         return lax.ppermute(piece, "x", [(i, (i - shift) % NX) for i in range(NX)])

time: 112 us -> 108 us (0.964)
  Pallas kernels: 34.8 us -> 30.9 us
    pallas_call x5, Pallas kernels: 18.9 us -> 15 us  [grads(): pl.pallas_call(functools.partial(grad_kernel, shift, halves), out_shape=[...]
  transfers between devices with their start and end apart: 13 -> 13, of which waited for: 9 -> 9; matrix products, arithmetic and copies ran while one was open for 2% -> 3% of each run, Pallas kernels for 13% -> 11%
where the time goes in v4:
time: 108 us; the launch traced here: 106 us
  Pallas kernels  30.9 us (29%)
  starting transfers between devices  28.2 us (26%)
  waiting for transfers between devices  25.6 us (24%)
  blocking collectives  16.9 us (16%)
  other arithmetic  3.19 us (3%)
    all_to_all x1, blocking collectives, per_device(): lse_all = lax.all_to_all(lse, GROUP, 0, 0, tiled=True)  16.9 us
    pallas_call x5, Pallas kernels, grads(): pl.pallas_call(functools.partial(grad_kernel, shift, halves), out_shape=[...  15 us
    pallas_call x1, Pallas kernels, per_device(): pl.pallas_call(stats_kernel, out_shape=[shaped((NC, 2 * E), bf16), shaped...  14 us
    all_to_all x1, starting transfers between devices, per_device(): q_in = lax.all_to_all(q_block, GROUP, 0, 0, tiled=True)  11.3 us
    ppermute x3, waiting for transfers between devices, per_device(): spread.append(lax.ppermute(c_block, RING, ring(s)))  6.47 us
    all_to_all x1, waiting for transfers between devices, per_device(): u_in = lax.all_to_all(u_line.reshape(NZ, QB, E), 'z', 0, 0, tiled=True)  6.39 us
    all_to_all x1, waiting for transfers between devices, per_device(): q_in = lax.all_to_all(q_block, GROUP, 0, 0, tiled=True)  5.56 us
    ppermute x3, starting transfers between devices, per_device(): pieces[s] = lax.ppermute(pieces[s], RING, ring(-s))  5.36 us
  transfers between devices with their start and end apart: 13, of which 9 were waited for; matrix products, arithmetic and copies ran while one was open for 3% of the time, Pallas kernels for 11%

profile of v4, /device:TPU:16, one launch (start us, length us, event | category | flops | bytes accessed | tf_op | source)
XLA Modules:
  0.0 106.4 jit_solution(735381744893417011)
XLA Ops:
  0.6 1.9 %pack.1 = (bf16[32,72,128]{2,1,0:T(8,128)(2,1)}, bf16[528,128]{1,0:T(8,128)(2,1)}) custom-call(bf16[64,128]{1,0:T(8,128)(2,1)} %queries.1, s32[1,64]{1,0:T(1,128)} %bitcast.16, bf16[1,64]{1,0:T(2,128)(2,1)} %bitcast.17, bf16[512,128]{1,0:T(8,128)(2,1)} %candidates.1, s32[4,128]{1,0:T(4,128)} %bitcast.15), custom_call_target="tpu_custom_call" | custom-call | tf_op jit(solution)/shard_map/pack/pallas_call | solution.py:222
  2.5 11.3 %all-to-all-start = ((bf16[32,72,128]{2,1,0:T(8,128)(2,1)}), bf16[32,72,128]{2,1,0:T(8,128)(2,1)S(1)}, u32[]{:S(2)}, u32[]{:S(2)}) async-start(bf16[32,72,128]{2,1,0:T(8,128)(2,1)} %get-tuple-element.41), calls=%async_computation | async-start | bytes 1179648 | tf_op jit(solution)/shard_map/all_to_all | solution.py:236
  13.8 0.5 collective-permute-start.2
  14.4 2.9 %collective-permute-start.1 = (bf16[528,128]{1,0:T(8,128)(2,1)}, bf16[528,128]{1,0:T(8,128)(2,1)S(1)}, u32[]{:S(2)}, u32[]{:S(2)}) collective-permute-start(bf16[528,128]{1,0:T(8,128)(2,1)} %get-tuple-element.42), channel_id=1, source_target_pairs={{0,32},{128,160},{32,0},{160,128},{1,33},{129,161},{33,1},{161,129... | collective-permute-start | bytes 405512 | tf_op jit(solution)/shard_map/ppermute | solution.py:239
  17.3 3.3 %collective-permute-done.2 = bf16[528,128]{1,0:T(8,128)(2,1)S(1)} collective-permute-done((bf16[528,128]{1,0:T(8,128)(2,1)}, bf16[528,128]{1,0:T(8,128)(2,1)S(1)}, u32[]{:S(2)}, u32[]{:S(2)}) %collective-permute-start.2) | collective-permute-done | bytes 135200 | tf_op jit(solution)/shard_map/ppermute | solution.py:239
  20.6 1.7 %collective-permute-done.1 = bf16[528,128]{1,0:T(8,128)(2,1)S(1)} collective-permute-done((bf16[528,128]{1,0:T(8,128)(2,1)}, bf16[528,128]{1,0:T(8,128)(2,1)S(1)}, u32[]{:S(2)}, u32[]{:S(2)}) %collective-permute-start.1) | collective-permute-done | bytes 135200 | tf_op jit(solution)/shard_map/ppermute | solution.py:239
  22.3 1.4 %collective-permute-done = bf16[528,128]{1,0:T(8,128)(2,1)S(1)} collective-permute-done((bf16[528,128]{1,0:T(8,128)(2,1)}, bf16[528,128]{1,0:T(8,128)(2,1)S(1)}, u32[]{:S(2)}, u32[]{:S(2)}) %collective-permute-start) | collective-permute-done | bytes 135200 | tf_op jit(solution)/shard_map/ppermute | solution.py:239
  23.7 1.0 pad_maximum_fusion.own
  24.8 0.8 tile.10
  25.8 0.9 collective-permute-done.3.other
  26.7 5.6 %all-to-all-done.q_in = bf16[32,72,128]{2,1,0:T(8,128)(2,1)S(1)} async-done(((bf16[32,72,128]{2,1,0:T(8,128)(2,1)}), bf16[32,72,128]{2,1,0:T(8,128)(2,1)S(1)}, u32[]{:S(2)}, u32[]{:S(2)}) %all-to-all-start) | async-done | bytes 589856 | tf_op jit(solution)/shard_map/all_to_all | solution.py:236
  32.3 14.0 %stats.1 = (bf16[4096,256]{1,0:T(8,128)(2,1)S(1)}, bf16[2048,256]{1,0:T(8,128)(2,1)S(1)}, f32[8,2048]{1,0:T(8,128)S(1)}, f32[32,16,128]{2,1,0:T(8,128)S(1)}, f32...) custom-call(s32[3]{0:T(128)S(1)} %pad_add_fusion.here, ...), custom_call_target="tpu_custom_call" | custom-call | flops 536870912 | bytes 8388608 | tf_op jit(solution)/shard_map/stats/pallas_call | solution.py:246
  46.3 16.9 %all_to_all.15.lse_all = f32[32,16,128]{2,1,0:T(8,128)S(1)} all-to-all(f32[32,16,128]{2,1,0:T(8,128)S(1)} %get-tuple-element.46), channel_id=1, replica_groups=mesh['yl'=2,'c'=2,'yh'=2,'x'=4,'z'=8] {'x','z'}, dimensions={0} | all-to-all | bytes 524288 | tf_op jit(solution)/shard_map/all_to_all | solution.py:262
  63.1 3.4 %grad.5 = (f32[512,128]{1,0:T(8,128)S(1)}, f32[4,512,128]{2,1,0:T(8,128)S(1)}, f32[4,512,128]{2,1,0:T(8,128)S(1)}) custom-call(s32[3]{0:T(128)S(1)} %pad_add_fusion.here, bf16[4096,256]{1,0:T(8,128)(2,1)S(1)} %get-tuple-element.43.c_ext, bf16[2048,256]{1,0:T(8,128)(2,1)S(1)} %get-tuple-element.44.q_ext, f32[8,2048]{1,0:T(8,128)S(1)} %get-tuple-element.45.aux, ...), custom_call_target="tpu_custom_call" | custom-call | flops 402653184 | bytes 2097152 | tf_op jit(solution)/shard_map/grad/pallas_call | solution.py:266
  66.6 1.6 %collective-permute-start.4 = (f32[512,128]{1,0:T(8,128)S(1)}, f32[512,128]{1,0:T(8,128)S(1)}, u32[]{:S(2)}, u32[]{:S(2)}) collective-permute-start(f32[512,128]{1,0:T(8,128)S(1)} %get-tuple-element.54), channel_id=1, source_target_pairs={{0,16},{8,24},{16,0},{24,8},{1,17},{9,25},{17,1},{25,9},{2,18},{10... | collective-permute-start | bytes 786440 | tf_op jit(solution)/shard_map/ppermute | solution.py:278
  68.2 3.6 %grad.6 = (f32[512,128]{1,0:T(8,128)S(1)}, f32[4,512,128]{2,1,0:T(8,128)S(1)}, f32[4,512,128]{2,1,0:T(8,128)S(1)}) custom-call(s32[3]{0:T(128)S(1)} %pad_add_fusion.here, bf16[4096,256]{1,0:T(8,128)(2,1)S(1)} %get-tuple-element.43.c_ext, bf16[2048,256]{1,0:T(8,128)(2,1)S(1)} %get-tuple-element.44.q_ext, ...), custom_call_target="tpu_custom_call", output_to_operand_aliasing={{1}: (12, {}), {2}: (13, {})} | custom-call | flops 402653184 | bytes 2097152 | tf_op jit(solution)/shard_map/grad/pallas_call | solution.py:266
  71.7 2.1 %collective-permute-start.5 = (f32[512,128]{1,0:T(8,128)S(1)}, f32[512,128]{1,0:T(8,128)S(1)}, u32[]{:S(2)}, u32[]{:S(2)}) collective-permute-start(f32[512,128]{1,0:T(8,128)S(1)} %get-tuple-element.61), channel_id=1, source_target_pairs={{0,24},{8,0},{16,8},{24,16},{1,25},{9,1},{17,9},{25,17},{2,26},{10... | collective-permute-start | bytes 786440 | tf_op jit(solution)/shard_map/ppermute | solution.py:278
  73.8 3.6 %grad.7 = (f32[512,128]{1,0:T(8,128)S(1)}, f32[4,512,128]{2,1,0:T(8,128)S(1)}, f32[4,512,128]{2,1,0:T(8,128)S(1)}) custom-call(s32[3]{0:T(128)S(1)} %pad_add_fusion.here, bf16[4096,256]{1,0:T(8,128)(2,1)S(1)} %get-tuple-element.43.c_ext, bf16[2048,256]{1,0:T(8,128)(2,1)S(1)} %get-tuple-element.44.q_ext, ...), custom_call_target="tpu_custom_call", output_to_operand_aliasing={{1}: (12, {}), {2}: (13, {})} | custom-call | flops 402653184 | bytes 2097152 | tf_op jit(solution)/shard_map/grad/pallas_call | solution.py:266
  77.4 2.3 %grad.8 = (f32[512,128]{1,0:T(8,128)S(1)}, f32[4,512,128]{2,1,0:T(8,128)S(1)}) custom-call(s32[3]{0:T(128)S(1)} %pad_add_fusion.here, bf16[4096,256]{1,0:T(8,128)(2,1)S(1)} %get-tuple-element.43.c_ext, bf16[2048,256]{1,0:T(8,128)(2,1)S(1)} %get-tuple-element.44.q_ext, f32[8,2048]{1,0:T(8,128)S(1)} %get-tuple-element.45.aux, ...), custom_call_target="tpu_custom_call", output_to_operand_aliasing={{1}: (12, {})} | custom-call | flops 201326592 | bytes 1048576 | tf_op jit(solution)/shard_map/grad/pallas_call | solution.py:266
  79.8 0.8 collective-permute-start.6
  80.6 2.1 %grad.9 = (f32[512,128]{1,0:T(8,128)S(1)}, f32[4,512,128]{2,1,0:T(8,128)S(1)}) custom-call(s32[3]{0:T(128)S(1)} %pad_add_fusion.here, bf16[4096,256]{1,0:T(8,128)(2,1)S(1)} %get-tuple-element.43.c_ext, bf16[2048,256]{1,0:T(8,128)(2,1)S(1)} %get-tuple-element.44.q_ext, ...), custom_call_target="tpu_custom_call", output_to_operand_aliasing={{0}: (12, {}), {1}: (13, {})} | custom-call | flops 201326592 | bytes 1048576 | tf_op jit(solution)/shard_map/grad/pallas_call | solution.py:266
  82.9 0.5 collective-permute-start.8
  83.4 2.9 %collective-permute-start.9 = (f32[512,128]{1,0:T(8,128)S(1)}, f32[512,128]{1,0:T(8,128)S(1)}, u32[]{:S(2)}, u32[]{:S(2)}) collective-permute-start(f32[512,128]{1,0:T(8,128)S(1)} %get-tuple-element.78), channel_id=1, source_target_pairs={{0,32},{128,160},{32,0},{160,128},{1,33},{129,161},{33,1},{161,129... | collective-permute-start | bytes 786440 | tf_op jit(solution)/shard_map/ppermute | solution.py:303
  86.3 1.9 %collective-permute-start.10 = (f32[512,128]{1,0:T(8,128)S(1)}, f32[512,128]{1,0:T(8,128)S(1)}, u32[]{:S(2)}, u32[]{:S(2)}) collective-permute-start(f32[512,128]{1,0:T(8,128)S(1)} %get-tuple-element.79), channel_id=1, source_target_pairs={{0,128},{128,32},{32,160},{160,0},{1,129},{129,33},{33,161},{161,1... | collective-permute-start | bytes 786440 | tf_op jit(solution)/shard_map/ppermute | solution.py:303
  88.2 1.5 %collective-permute-done.6 = f32[512,128]{1,0:T(8,128)S(1)} collective-permute-done((f32[512,128]{1,0:T(8,128)S(1)}, f32[512,128]{1,0:T(8,128)S(1)}, u32[]{:S(2)}, u32[]{:S(2)}) %collective-permute-start.6) | collective-permute-done | bytes 262176 | tf_op jit(solution)/shard_map/ppermute | solution.py:278
  89.7 0.8 add_add_fusion.1
  90.5 3.4 %all-to-all-start.2 = ((f32[8,64,128]{2,1,0:T(8,128)}), f32[8,64,128]{2,1,0:T(8,128)S(1)}, u32[]{:S(2)}, u32[]{:S(2)}) async-start(f32[8,64,128]{2,1,0:T(8,128)} %bitcast.10), calls=%async_computation.2 | async-start | bytes 524288 | tf_op jit(solution)/shard_map/all_to_all | solution.py:305
  93.9 0.2 collective-permute-done.9
  94.1 4.6 %collective-permute-done.10 = f32[512,128]{1,0:T(8,128)S(1)} collective-permute-done((f32[512,128]{1,0:T(8,128)S(1)}, f32[512,128]{1,0:T(8,128)S(1)}, u32[]{:S(2)}, u32[]{:S(2)}) %collective-permute-start.10) | collective-permute-done | bytes 262176 | tf_op jit(solution)/shard_map/ppermute | solution.py:303
  98.7 0.8 add_add_fusion
  99.4 6.4 %all-to-all-done.2 = f32[8,64,128]{2,1,0:T(8,128)S(1)} async-done(((f32[8,64,128]{2,1,0:T(8,128)}), f32[8,64,128]{2,1,0:T(8,128)S(1)}, u32[]{:S(2)}, u32[]{:S(2)}) %all-to-all-start.2) | async-done | bytes 262176 | tf_op jit(solution)/shard_map/all_to_all | solution.py:305
  105.8 0.6 reduce_sum.9
  (11 shorter events, 0.5 us)
Async XLA Ops:
  2.5 29.8 %all-to-all-start = ((bf16[32,72,128]{2,1,0:T(8,128)(2,1)}), bf16[32,72,128]{2,1,0:T(8,128)(2,1)S(1)}, u32[]{:S(2)}, u32[]{:S(2)}) async-start(bf16[32,72,128]{2,1,0:T(8,128)(2,1)} %get-tuple-element.41), calls=%async_computation | async-start | bytes 1179648 | tf_op jit(solution)/shard_map/all_to_all | solution.py:236
  13.8 6.8 %collective-permute-start.2 = (bf16[528,128]{1,0:T(8,128)(2,1)}, bf16[528,128]{1,0:T(8,128)(2,1)S(1)}, u32[]{:S(2)}, u32[]{:S(2)}) collective-permute-start(bf16[528,128]{1,0:T(8,128)(2,1)} %get-tuple-element.42), channel_id=1, source_target_pairs={{0,160},{128,0},{32,128},{160,32},{1,161},{129,1},{33,129},{161,33... | collective-permute-start | bytes 405512 | tf_op jit(solution)/shard_map/ppermute | solution.py:239
  14.4 8.0 %collective-permute-start.1 = (bf16[528,128]{1,0:T(8,128)(2,1)}, bf16[528,128]{1,0:T(8,128)(2,1)S(1)}, u32[]{:S(2)}, u32[]{:S(2)}) collective-permute-start(bf16[528,128]{1,0:T(8,128)(2,1)} %get-tuple-element.42), channel_id=1, source_target_pairs={{0,32},{128,160},{32,0},{160,128},{1,33},{129,161},{33,1},{161,129... | collective-permute-start | bytes 405512 | tf_op jit(solution)/shard_map/ppermute | solution.py:239
  17.3 6.5 %collective-permute-start = (bf16[528,128]{1,0:T(8,128)(2,1)}, bf16[528,128]{1,0:T(8,128)(2,1)S(1)}, u32[]{:S(2)}, u32[]{:S(2)}) collective-permute-start(bf16[528,128]{1,0:T(8,128)(2,1)} %get-tuple-element.42), channel_id=1, source_target_pairs={{0,128},{128,32},{32,160},{160,0},{1,129},{129,33},{33,161},{161,1... | collective-permute-start | bytes 405512 | tf_op jit(solution)/shard_map/ppermute | solution.py:239
  24.7 2.0 %collective-permute-start.3 = (bf16[4,528,128]{2,1,0:T(8,128)(2,1)S(1)}, bf16[4,528,128]{2,1,0:T(8,128)(2,1)S(1)}, u32[]{:S(2)}, u32[]{:S(2)}) collective-permute-start(bf16[4,528,128]{2,1,0:T(8,128)(2,1)S(1)} %pad_maximum_fusion.own), channel_id=1, source_target_pairs={{0,64},{64,0},{1,65},{65,1},{2,66},{66,2},{3,67},{67,3},{4,68},{68... | collective-permute-start | bytes 1622024 | tf_op jit(solution)/shard_map/ppermute | solution.py:242
  66.6 10.8 %collective-permute-start.4 = (f32[512,128]{1,0:T(8,128)S(1)}, f32[512,128]{1,0:T(8,128)S(1)}, u32[]{:S(2)}, u32[]{:S(2)}) collective-permute-start(f32[512,128]{1,0:T(8,128)S(1)} %get-tuple-element.54), channel_id=1, source_target_pairs={{0,16},{8,24},{16,0},{24,8},{1,17},{9,25},{17,1},{25,9},{2,18},{10... | collective-permute-start | bytes 786440 | tf_op jit(solution)/shard_map/ppermute | solution.py:278
  71.7 8.0 %collective-permute-start.5 = (f32[512,128]{1,0:T(8,128)S(1)}, f32[512,128]{1,0:T(8,128)S(1)}, u32[]{:S(2)}, u32[]{:S(2)}) collective-permute-start(f32[512,128]{1,0:T(8,128)S(1)} %get-tuple-element.61), channel_id=1, source_target_pairs={{0,24},{8,0},{16,8},{24,16},{1,25},{9,1},{17,9},{25,17},{2,26},{10... | collective-permute-start | bytes 786440 | tf_op jit(solution)/shard_map/ppermute | solution.py:278
  79.7 3.0 %collective-permute-start.7 = (f32[4,512,128]{2,1,0:T(8,128)S(1)}, f32[4,512,128]{2,1,0:T(8,128)S(1)}, u32[]{:S(2)}, u32[]{:S(2)}) collective-permute-start(f32[4,512,128]{2,1,0:T(8,128)S(1)} %get-tuple-element.70), channel_id=1, source_target_pairs={{0,64},{64,0},{1,65},{65,1},{2,66},{66,2},{3,67},{67,3},{4,68},{68... | collective-permute-start | bytes 3145736 | tf_op jit(solution)/shard_map/ppermute | solution.py:289
  79.8 9.9 %collective-permute-start.6 = (f32[512,128]{1,0:T(8,128)S(1)}, f32[512,128]{1,0:T(8,128)S(1)}, u32[]{:S(2)}, u32[]{:S(2)}) collective-permute-start(f32[512,128]{1,0:T(8,128)S(1)} %get-tuple-element.65), channel_id=1, source_target_pairs={{0,8},{8,16},{16,24},{24,0},{1,9},{9,17},{17,25},{25,1},{2,10},{10... | collective-permute-start | bytes 786440 | tf_op jit(solution)/shard_map/ppermute | solution.py:278
  82.9 11.1 %collective-permute-start.8 = (f32[512,128]{1,0:T(8,128)S(1)}, f32[512,128]{1,0:T(8,128)S(1)}, u32[]{:S(2)}, u32[]{:S(2)}) collective-permute-start(f32[512,128]{1,0:T(8,128)S(1)} %get-tuple-element.77), channel_id=1, source_target_pairs={{0,160},{128,0},{32,128},{160,32},{1,161},{129,1},{33,129},{161,33... | collective-permute-start | bytes 786440 | tf_op jit(solution)/shard_map/ppermute | solution.py:303
  83.4 10.7 %collective-permute-start.9 = (f32[512,128]{1,0:T(8,128)S(1)}, f32[512,128]{1,0:T(8,128)S(1)}, u32[]{:S(2)}, u32[]{:S(2)}) collective-permute-start(f32[512,128]{1,0:T(8,128)S(1)} %get-tuple-element.78), channel_id=1, source_target_pairs={{0,32},{128,160},{32,0},{160,128},{1,33},{129,161},{33,1},{161,129... | collective-permute-start | bytes 786440 | tf_op jit(solution)/shard_map/ppermute | solution.py:303
  86.3 12.4 %collective-permute-start.10 = (f32[512,128]{1,0:T(8,128)S(1)}, f32[512,128]{1,0:T(8,128)S(1)}, u32[]{:S(2)}, u32[]{:S(2)}) collective-permute-start(f32[512,128]{1,0:T(8,128)S(1)} %get-tuple-element.79), channel_id=1, source_target_pairs={{0,128},{128,32},{32,160},{160,0},{1,129},{129,33},{33,161},{161,1... | collective-permute-start | bytes 786440 | tf_op jit(solution)/shard_map/ppermute | solution.py:303
  90.5 15.3 %all-to-all-start.2 = ((f32[8,64,128]{2,1,0:T(8,128)}), f32[8,64,128]{2,1,0:T(8,128)S(1)}, u32[]{:S(2)}, u32[]{:S(2)}) async-start(f32[8,64,128]{2,1,0:T(8,128)} %bitcast.10), calls=%async_computation.2 | async-start | bytes 524288 | tf_op jit(solution)/shard_map/all_to_all | solution.py:305

commit v5 on v4

--- a/solution.py
+++ b/solution.py
@@ -197,6 +197,10 @@
         out[...] = own[s] + came[s]
 
 
+def add_kernel(a, b, c, d, out):
+    out[...] = (a[...] + b[...]) + (c[...] + d[...])
+
+
 def ring(step):
     place = [(y & 1) * 2 + (y >> 1) for y in range(NY)]
     return [(place[y], place[(y + step) % NY]) for y in range(NY)]
@@ -289,6 +293,16 @@
     g_came = lax.ppermute(g_other, "c", swap)
     u_own, g_own = grads(0, (0,), u_own, g_a, aliases={5: 0, 6: 1})
 
+    u_line = pl.pallas_call(
+        add_kernel,
+        out_shape=shaped((QUART, E), f32),
+        in_specs=[VMEM] * 4,
+        out_specs=VMEM,
+        compiler_params=PARAMS,
+        cost_estimate=cost(NQ * NC, 150),
+        name="add",
+    )(u_two, u_one, u_three, u_own)
+    u_line, g_own = lax.optimization_barrier((u_line, g_own))
     pieces = pl.pallas_call(
         merge_kernel,
         out_shape=[shaped((CB, E), f32)] * NY,
@@ -297,11 +311,9 @@
         compiler_params=PARAMS,
         name="merge",
     )(g_own, g_came)
-    u_sum = [u_two, u_one, u_three, u_own]
-    u_sum[3], *pieces = lax.optimization_barrier((u_sum[3], *pieces))
+    u_line, *pieces = lax.optimization_barrier((u_line, *pieces))
     for s in range(1, NY):
         pieces[s] = lax.ppermute(pieces[s], RING, ring(-s))
-    u_line = (u_sum[0] + u_sum[1]) + (u_sum[2] + u_sum[3])
     u_in = lax.all_to_all(u_line.reshape(NZ, QB, E), "z", 0, 0, tiled=True)
     query_grad = jnp.sum(u_in, axis=0)
     cand_grad = (pieces[0] + pieces[1]) + (pieces[2] + pieces[3])

time: 108 us -> 106 us (0.981); the launches traced: 106 us -> 106 us
    all_to_all x1, waiting for transfers between devices: 6.39 us -> 5.04 us  [per_device(): u_in = lax.all_to_all(u_line.reshape(NZ, QB, E), 'z', 0, 0, tiled=True)]
    ppermute x3, waiting for transfers between devices: 1.54 us -> 2.79 us  [along_x(): return lax.ppermute(piece, 'x', [(i, (i - shift) % NX) for i in range(NX)])]
  transfers between devices with their start and end apart: 13 -> 13, of which waited for: 9 -> 10; matrix products, arithmetic and copies ran while one was open for 3% -> 3% of each run, Pallas kernels for 11% -> 12%
where the time goes in v5:
time: 106 us
  Pallas kernels  31.7 us (30%)
  starting transfers between devices  27.5 us (26%)
  waiting for transfers between devices  25.5 us (24%)
  blocking collectives  16.9 us (16%)
  other arithmetic  2.44 us (2%)
    all_to_all x1, blocking collectives, per_device(): lse_all = lax.all_to_all(lse, GROUP, 0, 0, tiled=True)  16.9 us
    pallas_call x5, Pallas kernels, grads(): pl.pallas_call(functools.partial(grad_kernel, shift, halves), out_shape=[...  15 us
    pallas_call x1, Pallas kernels, per_device(): pl.pallas_call(stats_kernel, out_shape=[shaped((NC, 2 * E), bf16), shaped...  14 us
    all_to_all x1, starting transfers between devices, per_device(): q_in = lax.all_to_all(q_block, GROUP, 0, 0, tiled=True)  11.3 us
    ppermute x3, waiting for transfers between devices, per_device(): spread.append(lax.ppermute(c_block, RING, ring(s)))  6.47 us
    all_to_all x1, waiting for transfers between devices, per_device(): q_in = lax.all_to_all(q_block, GROUP, 0, 0, tiled=True)  5.56 us
    ppermute x3, starting transfers between devices, per_device(): pieces[s] = lax.ppermute(pieces[s], RING, ring(-s))  5.21 us
    all_to_all x1, waiting for transfers between devices, per_device(): u_in = lax.all_to_all(u_line.reshape(NZ, QB, E), 'z', 0, 0, tiled=True)  5.04 us
  transfers between devices with their start and end apart: 13, of which 10 were waited for; matrix products, arithmetic and copies ran while one was open for 3% of the time, Pallas kernels for 12%

profile of v5, /device:TPU:16, one launch (start us, length us, event | category | flops | bytes accessed | tf_op | source)
XLA Modules:
  0.0 105.6 jit_solution(16362300118719421391)
XLA Ops:
  0.6 1.9 %pack.1 = (bf16[32,72,128]{2,1,0:T(8,128)(2,1)}, bf16[528,128]{1,0:T(8,128)(2,1)}) custom-call(bf16[64,128]{1,0:T(8,128)(2,1)} %queries.1, s32[1,64]{1,0:T(1,128)} %bitcast.16, bf16[1,64]{1,0:T(2,128)(2,1)} %bitcast.17, bf16[512,128]{1,0:T(8,128)(2,1)} %candidates.1, s32[4,128]{1,0:T(4,128)} %bitcast.15), custom_call_target="tpu_custom_call" | custom-call | tf_op jit(solution)/shard_map/pack/pallas_call | solution.py:226
  2.5 11.3 %all-to-all-start = ((bf16[32,72,128]{2,1,0:T(8,128)(2,1)}), bf16[32,72,128]{2,1,0:T(8,128)(2,1)S(1)}, u32[]{:S(2)}, u32[]{:S(2)}) async-start(bf16[32,72,128]{2,1,0:T(8,128)(2,1)} %get-tuple-element.43), calls=%async_computation | async-start | bytes 1179648 | tf_op jit(solution)/shard_map/all_to_all | solution.py:240
  13.8 0.5 collective-permute-start.2
  14.4 2.9 %collective-permute-start.1 = (bf16[528,128]{1,0:T(8,128)(2,1)}, bf16[528,128]{1,0:T(8,128)(2,1)S(1)}, u32[]{:S(2)}, u32[]{:S(2)}) collective-permute-start(bf16[528,128]{1,0:T(8,128)(2,1)} %get-tuple-element.44), channel_id=1, source_target_pairs={{0,32},{128,160},{32,0},{160,128},{1,33},{129,161},{33,1},{161,129... | collective-permute-start | bytes 405512 | tf_op jit(solution)/shard_map/ppermute | solution.py:243
  17.3 3.3 %collective-permute-done.2 = bf16[528,128]{1,0:T(8,128)(2,1)S(1)} collective-permute-done((bf16[528,128]{1,0:T(8,128)(2,1)}, bf16[528,128]{1,0:T(8,128)(2,1)S(1)}, u32[]{:S(2)}, u32[]{:S(2)}) %collective-permute-start.2) | collective-permute-done | bytes 135200 | tf_op jit(solution)/shard_map/ppermute | solution.py:243
  20.6 1.7 %collective-permute-done.1 = bf16[528,128]{1,0:T(8,128)(2,1)S(1)} collective-permute-done((bf16[528,128]{1,0:T(8,128)(2,1)}, bf16[528,128]{1,0:T(8,128)(2,1)S(1)}, u32[]{:S(2)}, u32[]{:S(2)}) %collective-permute-start.1) | collective-permute-done | bytes 135200 | tf_op jit(solution)/shard_map/ppermute | solution.py:243
  22.3 1.4 %collective-permute-done = bf16[528,128]{1,0:T(8,128)(2,1)S(1)} collective-permute-done((bf16[528,128]{1,0:T(8,128)(2,1)}, bf16[528,128]{1,0:T(8,128)(2,1)S(1)}, u32[]{:S(2)}, u32[]{:S(2)}) %collective-permute-start) | collective-permute-done | bytes 135200 | tf_op jit(solution)/shard_map/ppermute | solution.py:243
  23.7 1.0 pad_maximum_fusion.own
  24.8 0.8 tile.10
  25.8 0.9 collective-permute-done.3.other
  26.7 5.6 %all-to-all-done.q_in = bf16[32,72,128]{2,1,0:T(8,128)(2,1)S(1)} async-done(((bf16[32,72,128]{2,1,0:T(8,128)(2,1)}), bf16[32,72,128]{2,1,0:T(8,128)(2,1)S(1)}, u32[]{:S(2)}, u32[]{:S(2)}) %all-to-all-start) | async-done | bytes 589856 | tf_op jit(solution)/shard_map/all_to_all | solution.py:240
  32.3 14.0 %stats.1 = (bf16[4096,256]{1,0:T(8,128)(2,1)S(1)}, bf16[2048,256]{1,0:T(8,128)(2,1)S(1)}, f32[8,2048]{1,0:T(8,128)S(1)}, f32[32,16,128]{2,1,0:T(8,128)S(1)}, f32...) custom-call(s32[3]{0:T(128)S(1)} %pad_add_fusion.here, ...), custom_call_target="tpu_custom_call" | custom-call | flops 536870912 | bytes 8388608 | tf_op jit(solution)/shard_map/stats/pallas_call | solution.py:250
  46.3 16.9 %all_to_all.15.lse_all = f32[32,16,128]{2,1,0:T(8,128)S(1)} all-to-all(f32[32,16,128]{2,1,0:T(8,128)S(1)} %get-tuple-element.48), channel_id=1, replica_groups=mesh['yl'=2,'c'=2,'yh'=2,'x'=4,'z'=8] {'x','z'}, dimensions={0} | all-to-all | bytes 524288 | tf_op jit(solution)/shard_map/all_to_all | solution.py:266
  63.1 3.4 %grad.5 = (f32[512,128]{1,0:T(8,128)S(1)}, f32[4,512,128]{2,1,0:T(8,128)S(1)}, f32[4,512,128]{2,1,0:T(8,128)S(1)}) custom-call(s32[3]{0:T(128)S(1)} %pad_add_fusion.here, bf16[4096,256]{1,0:T(8,128)(2,1)S(1)} %get-tuple-element.45.c_ext, bf16[2048,256]{1,0:T(8,128)(2,1)S(1)} %get-tuple-element.46.q_ext, f32[8,2048]{1,0:T(8,128)S(1)} %get-tuple-element.47.aux, ...), custom_call_target="tpu_custom_call" | custom-call | flops 402653184 | bytes 2097152 | tf_op jit(solution)/shard_map/grad/pallas_call | solution.py:270
  66.6 1.6 %collective-permute-start.4 = (f32[512,128]{1,0:T(8,128)S(1)}, f32[512,128]{1,0:T(8,128)S(1)}, u32[]{:S(2)}, u32[]{:S(2)}) collective-permute-start(f32[512,128]{1,0:T(8,128)S(1)} %get-tuple-element.56), channel_id=1, source_target_pairs={{0,16},{8,24},{16,0},{24,8},{1,17},{9,25},{17,1},{25,9},{2,18},{10... | collective-permute-start | bytes 786440 | tf_op jit(solution)/shard_map/ppermute | solution.py:282
  68.2 3.6 %grad.6 = (f32[512,128]{1,0:T(8,128)S(1)}, f32[4,512,128]{2,1,0:T(8,128)S(1)}, f32[4,512,128]{2,1,0:T(8,128)S(1)}) custom-call(s32[3]{0:T(128)S(1)} %pad_add_fusion.here, bf16[4096,256]{1,0:T(8,128)(2,1)S(1)} %get-tuple-element.45.c_ext, bf16[2048,256]{1,0:T(8,128)(2,1)S(1)} %get-tuple-element.46.q_ext, ...), custom_call_target="tpu_custom_call", output_to_operand_aliasing={{1}: (12, {}), {2}: (13, {})} | custom-call | flops 402653184 | bytes 2097152 | tf_op jit(solution)/shard_map/grad/pallas_call | solution.py:270
  71.7 1.8 %collective-permute-start.5 = (f32[512,128]{1,0:T(8,128)S(1)}, f32[512,128]{1,0:T(8,128)S(1)}, u32[]{:S(2)}, u32[]{:S(2)}) collective-permute-start(f32[512,128]{1,0:T(8,128)S(1)} %get-tuple-element.63), channel_id=1, source_target_pairs={{0,24},{8,0},{16,8},{24,16},{1,25},{9,1},{17,9},{25,17},{2,26},{10... | collective-permute-start | bytes 786440 | tf_op jit(solution)/shard_map/ppermute | solution.py:282
  73.6 3.6 %grad.7 = (f32[512,128]{1,0:T(8,128)S(1)}, f32[4,512,128]{2,1,0:T(8,128)S(1)}, f32[4,512,128]{2,1,0:T(8,128)S(1)}) custom-call(s32[3]{0:T(128)S(1)} %pad_add_fusion.here, bf16[4096,256]{1,0:T(8,128)(2,1)S(1)} %get-tuple-element.45.c_ext, bf16[2048,256]{1,0:T(8,128)(2,1)S(1)} %get-tuple-element.46.q_ext, ...), custom_call_target="tpu_custom_call", output_to_operand_aliasing={{1}: (12, {}), {2}: (13, {})} | custom-call | flops 402653184 | bytes 2097152 | tf_op jit(solution)/shard_map/grad/pallas_call | solution.py:270
  77.2 0.6 collective-permute-start.6
  77.7 2.3 %grad.8 = (f32[512,128]{1,0:T(8,128)S(1)}, f32[4,512,128]{2,1,0:T(8,128)S(1)}) custom-call(s32[3]{0:T(128)S(1)} %pad_add_fusion.here, bf16[4096,256]{1,0:T(8,128)(2,1)S(1)} %get-tuple-element.45.c_ext, bf16[2048,256]{1,0:T(8,128)(2,1)S(1)} %get-tuple-element.46.q_ext, f32[8,2048]{1,0:T(8,128)S(1)} %get-tuple-element.47.aux, ...), custom_call_target="tpu_custom_call", output_to_operand_aliasing={{1}: (12, {})} | custom-call | flops 201326592 | bytes 1048576 | tf_op jit(solution)/shard_map/grad/pallas_call | solution.py:270
  80.1 2.1 %grad.9 = (f32[512,128]{1,0:T(8,128)S(1)}, f32[4,512,128]{2,1,0:T(8,128)S(1)}) custom-call(s32[3]{0:T(128)S(1)} %pad_add_fusion.here, bf16[4096,256]{1,0:T(8,128)(2,1)S(1)} %get-tuple-element.45.c_ext, bf16[2048,256]{1,0:T(8,128)(2,1)S(1)} %get-tuple-element.46.q_ext, ...), custom_call_target="tpu_custom_call", output_to_operand_aliasing={{0}: (12, {}), {1}: (13, {})} | custom-call | flops 201326592 | bytes 1048576 | tf_op jit(solution)/shard_map/grad/pallas_call | solution.py:270
  82.3 2.8 %collective-permute-done.6.c = f32[512,128]{1,0:T(8,128)S(1)} collective-permute-done((f32[512,128]{1,0:T(8,128)S(1)}, f32[512,128]{1,0:T(8,128)S(1)}, u32[]{:S(2)}, u32[]{:S(2)}) %collective-permute-start.6) | collective-permute-done | bytes 262176 | tf_op jit(solution)/shard_map/ppermute | solution.py:282
  85.0 0.8 add.28
  85.9 0.5 collective-permute-start.8
  86.4 2.9 %collective-permute-start.9 = (f32[512,128]{1,0:T(8,128)S(1)}, f32[512,128]{1,0:T(8,128)S(1)}, u32[]{:S(2)}, u32[]{:S(2)}) collective-permute-start(f32[512,128]{1,0:T(8,128)S(1)} %get-tuple-element.82), channel_id=1, source_target_pairs={{0,32},{128,160},{32,0},{160,128},{1,33},{129,161},{33,1},{161,129... | collective-permute-start | bytes 786440 | tf_op jit(solution)/shard_map/ppermute | solution.py:316
  89.3 1.8 %collective-permute-start.10 = (f32[512,128]{1,0:T(8,128)S(1)}, f32[512,128]{1,0:T(8,128)S(1)}, u32[]{:S(2)}, u32[]{:S(2)}) collective-permute-start(f32[512,128]{1,0:T(8,128)S(1)} %get-tuple-element.83), channel_id=1, source_target_pairs={{0,128},{128,32},{32,160},{160,0},{1,129},{129,33},{33,161},{161,1... | collective-permute-start | bytes 786440 | tf_op jit(solution)/shard_map/ppermute | solution.py:316
  91.1 3.4 %all-to-all-start.2 = ((f32[8,64,128]{2,1,0:T(8,128)}), f32[8,64,128]{2,1,0:T(8,128)S(1)}, u32[]{:S(2)}, u32[]{:S(2)}) async-start(f32[8,64,128]{2,1,0:T(8,128)} %bitcast.10), calls=%async_computation.2 | async-start | bytes 524288 | tf_op jit(solution)/shard_map/all_to_all | solution.py:317
  94.8 1.8 %collective-permute-done.9 = f32[512,128]{1,0:T(8,128)S(1)} collective-permute-done((f32[512,128]{1,0:T(8,128)S(1)}, f32[512,128]{1,0:T(8,128)S(1)}, u32[]{:S(2)}, u32[]{:S(2)}) %collective-permute-start.9) | collective-permute-done | bytes 262176 | tf_op jit(solution)/shard_map/ppermute | solution.py:316
  96.5 2.7 %collective-permute-done.10 = f32[512,128]{1,0:T(8,128)S(1)} collective-permute-done((f32[512,128]{1,0:T(8,128)S(1)}, f32[512,128]{1,0:T(8,128)S(1)}, u32[]{:S(2)}, u32[]{:S(2)}) %collective-permute-start.10) | collective-permute-done | bytes 262176 | tf_op jit(solution)/shard_map/ppermute | solution.py:316
  99.2 0.8 add_add_fusion
  100.0 5.0 %all-to-all-done.2 = f32[8,64,128]{2,1,0:T(8,128)S(1)} async-done(((f32[8,64,128]{2,1,0:T(8,128)}), f32[8,64,128]{2,1,0:T(8,128)S(1)}, u32[]{:S(2)}, u32[]{:S(2)}) %all-to-all-start.2) | async-done | bytes 262176 | tf_op jit(solution)/shard_map/all_to_all | solution.py:317
  105.0 0.6 reduce_sum.9
  (11 shorter events, 0.7 us)
Async XLA Ops:
  2.5 29.8 %all-to-all-start = ((bf16[32,72,128]{2,1,0:T(8,128)(2,1)}), bf16[32,72,128]{2,1,0:T(8,128)(2,1)S(1)}, u32[]{:S(2)}, u32[]{:S(2)}) async-start(bf16[32,72,128]{2,1,0:T(8,128)(2,1)} %get-tuple-element.43), calls=%async_computation | async-start | bytes 1179648 | tf_op jit(solution)/shard_map/all_to_all | solution.py:240
  13.8 6.8 %collective-permute-start.2 = (bf16[528,128]{1,0:T(8,128)(2,1)}, bf16[528,128]{1,0:T(8,128)(2,1)S(1)}, u32[]{:S(2)}, u32[]{:S(2)}) collective-permute-start(bf16[528,128]{1,0:T(8,128)(2,1)} %get-tuple-element.44), channel_id=1, source_target_pairs={{0,160},{128,0},{32,128},{160,32},{1,161},{129,1},{33,129},{161,33... | collective-permute-start | bytes 405512 | tf_op jit(solution)/shard_map/ppermute | solution.py:243
  14.4 8.0 %collective-permute-start.1 = (bf16[528,128]{1,0:T(8,128)(2,1)}, bf16[528,128]{1,0:T(8,128)(2,1)S(1)}, u32[]{:S(2)}, u32[]{:S(2)}) collective-permute-start(bf16[528,128]{1,0:T(8,128)(2,1)} %get-tuple-element.44), channel_id=1, source_target_pairs={{0,32},{128,160},{32,0},{160,128},{1,33},{129,161},{33,1},{161,129... | collective-permute-start | bytes 405512 | tf_op jit(solution)/shard_map/ppermute | solution.py:243
  17.3 6.5 %collective-permute-start = (bf16[528,128]{1,0:T(8,128)(2,1)}, bf16[528,128]{1,0:T(8,128)(2,1)S(1)}, u32[]{:S(2)}, u32[]{:S(2)}) collective-permute-start(bf16[528,128]{1,0:T(8,128)(2,1)} %get-tuple-element.44), channel_id=1, source_target_pairs={{0,128},{128,32},{32,160},{160,0},{1,129},{129,33},{33,161},{161,1... | collective-permute-start | bytes 405512 | tf_op jit(solution)/shard_map/ppermute | solution.py:243
  24.7 2.0 %collective-permute-start.3 = (bf16[4,528,128]{2,1,0:T(8,128)(2,1)S(1)}, bf16[4,528,128]{2,1,0:T(8,128)(2,1)S(1)}, u32[]{:S(2)}, u32[]{:S(2)}) collective-permute-start(bf16[4,528,128]{2,1,0:T(8,128)(2,1)S(1)} %pad_maximum_fusion.own), channel_id=1, source_target_pairs={{0,64},{64,0},{1,65},{65,1},{2,66},{66,2},{3,67},{67,3},{4,68},{68... | collective-permute-start | bytes 1622024 | tf_op jit(solution)/shard_map/ppermute | solution.py:246
  66.6 11.2 %collective-permute-start.4 = (f32[512,128]{1,0:T(8,128)S(1)}, f32[512,128]{1,0:T(8,128)S(1)}, u32[]{:S(2)}, u32[]{:S(2)}) collective-permute-start(f32[512,128]{1,0:T(8,128)S(1)} %get-tuple-element.56), channel_id=1, source_target_pairs={{0,16},{8,24},{16,0},{24,8},{1,17},{9,25},{17,1},{25,9},{2,18},{10... | collective-permute-start | bytes 786440 | tf_op jit(solution)/shard_map/ppermute | solution.py:282
  71.7 8.3 %collective-permute-start.5 = (f32[512,128]{1,0:T(8,128)S(1)}, f32[512,128]{1,0:T(8,128)S(1)}, u32[]{:S(2)}, u32[]{:S(2)}) collective-permute-start(f32[512,128]{1,0:T(8,128)S(1)} %get-tuple-element.63), channel_id=1, source_target_pairs={{0,24},{8,0},{16,8},{24,16},{1,25},{9,1},{17,9},{25,17},{2,26},{10... | collective-permute-start | bytes 786440 | tf_op jit(solution)/shard_map/ppermute | solution.py:282
  77.2 7.9 %collective-permute-start.6 = (f32[512,128]{1,0:T(8,128)S(1)}, f32[512,128]{1,0:T(8,128)S(1)}, u32[]{:S(2)}, u32[]{:S(2)}) collective-permute-start(f32[512,128]{1,0:T(8,128)S(1)} %get-tuple-element.67), channel_id=1, source_target_pairs={{0,8},{8,16},{16,24},{24,0},{1,9},{9,17},{17,25},{25,1},{2,10},{10... | collective-permute-start | bytes 786440 | tf_op jit(solution)/shard_map/ppermute | solution.py:282
  80.0 5.8 %collective-permute-start.7 = (f32[4,512,128]{2,1,0:T(8,128)S(1)}, f32[4,512,128]{2,1,0:T(8,128)S(1)}, u32[]{:S(2)}, u32[]{:S(2)}) collective-permute-start(f32[4,512,128]{2,1,0:T(8,128)S(1)} %get-tuple-element.74), channel_id=1, source_target_pairs={{0,64},{64,0},{1,65},{65,1},{2,66},{66,2},{3,67},{67,3},{4,68},{68... | collective-permute-start | bytes 3145736 | tf_op jit(solution)/shard_map/ppermute | solution.py:293
  85.9 8.8 %collective-permute-start.8 = (f32[512,128]{1,0:T(8,128)S(1)}, f32[512,128]{1,0:T(8,128)S(1)}, u32[]{:S(2)}, u32[]{:S(2)}) collective-permute-start(f32[512,128]{1,0:T(8,128)S(1)} %get-tuple-element.81), channel_id=1, source_target_pairs={{0,160},{128,0},{32,128},{160,32},{1,161},{129,1},{33,129},{161,33... | collective-permute-start | bytes 786440 | tf_op jit(solution)/shard_map/ppermute | solution.py:316
  86.4 10.1 %collective-permute-start.9 = (f32[512,128]{1,0:T(8,128)S(1)}, f32[512,128]{1,0:T(8,128)S(1)}, u32[]{:S(2)}, u32[]{:S(2)}) collective-permute-start(f32[512,128]{1,0:T(8,128)S(1)} %get-tuple-element.82), channel_id=1, source_target_pairs={{0,32},{128,160},{32,0},{160,128},{1,33},{129,161},{33,1},{161,129... | collective-permute-start | bytes 786440 | tf_op jit(solution)/shard_map/ppermute | solution.py:316
  89.3 9.9 %collective-permute-start.10 = (f32[512,128]{1,0:T(8,128)S(1)}, f32[512,128]{1,0:T(8,128)S(1)}, u32[]{:S(2)}, u32[]{:S(2)}) collective-permute-start(f32[512,128]{1,0:T(8,128)S(1)} %get-tuple-element.83), channel_id=1, source_target_pairs={{0,128},{128,32},{32,160},{160,0},{1,129},{129,33},{33,161},{161,1... | collective-permute-start | bytes 786440 | tf_op jit(solution)/shard_map/ppermute | solution.py:316
  91.1 13.9 %all-to-all-start.2 = ((f32[8,64,128]{2,1,0:T(8,128)}), f32[8,64,128]{2,1,0:T(8,128)S(1)}, u32[]{:S(2)}, u32[]{:S(2)}) async-start(f32[8,64,128]{2,1,0:T(8,128)} %bitcast.10), calls=%async_computation.2 | async-start | bytes 524288 | tf_op jit(solution)/shard_map/all_to_all | solution.py:317

commit v6 on v5

--- a/solution.py
+++ b/solution.py
@@ -56,7 +56,7 @@
 
 
 def stats_kernel(here, table, q_in, own, other, c_ext, q_ext, aux, lse_out, *refs):
-    kept, (meta, ref_max, sums) = refs[:KEPT], refs[KEPT:]
+    kept, (meta, base_max, sums) = refs[:KEPT], refs[KEPT:]
     lane = lax.broadcasted_iota(i32, (SIDE, E), 1)
     row = lax.broadcasted_iota(i32, (SIDE, E), 0)
     freq = table[...]
@@ -105,38 +105,44 @@
     queries = q_ext[...]
 
     def tall(k):
-        start = k * rows if isinstance(k, int) else pl.multiple_of(k * rows, rows)
-        logits = lax.dot_general(c_ext[pl.ds(start, rows), :], queries, NT, preferred_element_type=f32)
-        if isinstance(k, int) and k < KEPT:
-            kept[k][...] = logits
+        logits = lax.dot_general(
+            c_ext[k * rows : (k + 1) * rows, :], queries, NT, preferred_element_type=f32
+        )
         return logits.reshape(rows // 8, 8, NQ)
 
-    def summed(logits, shift):
-        return jnp.sum(jnp.exp(logits - shift[None]), axis=0)
+    def summed(k, logits):
+        expo = jnp.exp(logits - base_max[...][None])
+        if k < KEPT:
+            kept[k][...] = expo.reshape(rows, NQ)
+        return jnp.sum(expo, axis=0)
 
     block = tall(0)
-    first = jnp.max(block, axis=0)
-    top, total = first, summed(block, first)
-    ref_max[...] = first
+    top = jnp.max(block, axis=0)
+    base_max[...] = jnp.broadcast_to(jnp.max(top, axis=0, keepdims=True), (8, NQ))
+    total = summed(0, block)
     for k in range(1, NC // rows):
         block = tall(k)
         top = jnp.maximum(top, jnp.max(block, axis=0))
-        total = total + summed(block, ref_max[...])
+        total = total + summed(k, block)
     sums[...] = total
     best = jnp.max(top, axis=0, keepdims=True)
 
-    @pl.when(jnp.max(top - ref_max[...]) > 40.0)
+    @pl.when(jnp.max(best - base_max[0:1, :]) > 40.0)
     def _():
-        peak = jnp.broadcast_to(best, (8, NQ))
-        ref_max[...] = peak
-        sums[...] = lax.fori_loop(
-            0, NC // rows, lambda k, acc: acc + summed(tall(k), peak), jnp.zeros((8, NQ), f32)
-        )
-
-    total = jnp.sum(sums[...] * jnp.exp(ref_max[...] - best), axis=0, keepdims=True)
+        base_max[...] = jnp.broadcast_to(best, (8, NQ))
+        again = summed(0, tall(0))
+        for k in range(1, NC // rows):
+            again = again + summed(k, tall(k))
+        sums[...] = again
+
+    base = base_max[0:1, :]
+    lift = jnp.exp(base - best)
+    total = jnp.sum(sums[...], axis=0, keepdims=True) * lift
     aux[0:1, :] = best
     aux[1:2, :] = total
-    aux[4:8, :] = jnp.zeros((4, NQ), f32)
+    aux[4:5, :] = base
+    aux[5:6, :] = lift
+    aux[6:8, :] = jnp.zeros((2, NQ), f32)
     lse = best + jnp.log(total)
     tile = jnp.concatenate([lse[:, t * E : (t + 1) * E] for t in range(NQ // E)], axis=0)
     for k in range(NGROUP):
@@ -169,10 +175,10 @@
     g_ins = before[-n:] if len(before) >= n and shift != 2 else [None] * n
     first = pl.multiple_of(((here[2] >> 3) - shift & 3) * QUART, QUART)
     span = pl.ds(first, QUART)
-    scale = row_scale(here, aux, lse_all, first, QUART)
+    scale = row_scale(here, aux, lse_all, first, QUART) * aux[5:6, span]
     queries = q_ext[span, :]
     narrow = queries[:, :E]
-    best, weight = aux[0:1, span], aux[2:3, span]
+    base, weight = aux[4:5, span], aux[2:3, span]
     local = aux[3:4, span].astype(i32)
     total = jnp.zeros((QUART, E), f32) if u_in is None else u_in[...]
     for half, g_in, g_out in zip(halves, g_ins, g_outs):
@@ -180,11 +186,11 @@
             row = half * HALF + k * CB
             block = c_ext[row : row + CB, :]
             if half * NY + k < KEPT:
-                logits = kept[half * NY + k][:, span]
+                expo = kept[half * NY + k][:, span] * scale
             else:
                 logits = lax.dot_general(block, queries, NT, preferred_element_type=f32)
-            expo = jnp.exp(logits - best) * scale
-            matched = lax.broadcasted_iota(i32, logits.shape, 0) == (local - row)
+                expo = jnp.exp(logits - base) * scale
+            matched = lax.broadcasted_iota(i32, expo.shape, 0) == (local - row)
             grad = (expo - jnp.where(matched, weight, 0.0)).astype(bf16)
             g_part = lax.dot_general(grad, narrow, NN, preferred_element_type=f32)
             g_out[k] = g_part if g_in is None else g_in[k] + g_part

time: 106 us -> 104 us (0.981)
  Pallas kernels: 31.7 us -> 29.8 us
  transfers between devices with their start and end apart: 13 -> 13, of which waited for: 10 -> 9; matrix products, arithmetic and copies ran while one was open for 3% -> 3% of each run, Pallas kernels for 12% -> 11%
where the time goes in v6:
time: 104 us
  Pallas kernels  29.8 us (29%)
  starting transfers between devices  27.6 us (27%)
  waiting for transfers between devices  25.7 us (25%)
  blocking collectives  16.9 us (16%)
  other arithmetic  2.44 us (2%)
    all_to_all x1, blocking collectives, per_device(): lse_all = lax.all_to_all(lse, GROUP, 0, 0, tiled=True)  16.9 us
    pallas_call x5, Pallas kernels, grads(): pl.pallas_call(functools.partial(grad_kernel, shift, halves), out_shape=[...  14.1 us
    pallas_call x1, Pallas kernels, per_device(): pl.pallas_call(stats_kernel, out_shape=[shaped((NC, 2 * E), bf16), shaped...  13 us
    all_to_all x1, starting transfers between devices, per_device(): q_in = lax.all_to_all(q_block, GROUP, 0, 0, tiled=True)  11.3 us
    ppermute x3, waiting for transfers between devices, per_device(): spread.append(lax.ppermute(c_block, RING, ring(s)))  6.47 us
    all_to_all x1, waiting for transfers between devices, per_device(): q_in = lax.all_to_all(q_block, GROUP, 0, 0, tiled=True)  5.56 us
    all_to_all x1, waiting for transfers between devices, per_device(): u_in = lax.all_to_all(u_line.reshape(NZ, QB, E), 'z', 0, 0, tiled=True)  5.37 us
    ppermute x3, starting transfers between devices, per_device(): pieces[s] = lax.ppermute(pieces[s], RING, ring(-s))  5.21 us
  transfers between devices with their start and end apart: 13, of which 9 were waited for; matrix products, arithmetic and copies ran while one was open for 3% of the time, Pallas kernels for 11%

profile of v6, /device:TPU:16, one launch (start us, length us, event | category | flops | bytes accessed | tf_op | source)
XLA Modules:
  0.0 104.0 jit_solution(8694071423462296237)
XLA Ops:
  0.6 1.9 %pack.1 = (bf16[32,72,128]{2,1,0:T(8,128)(2,1)}, bf16[528,128]{1,0:T(8,128)(2,1)}) custom-call(bf16[64,128]{1,0:T(8,128)(2,1)} %queries.1, s32[1,64]{1,0:T(1,128)} %bitcast.16, bf16[1,64]{1,0:T(2,128)(2,1)} %bitcast.17, bf16[512,128]{1,0:T(8,128)(2,1)} %candidates.1, s32[4,128]{1,0:T(4,128)} %bitcast.15), custom_call_target="tpu_custom_call" | custom-call | tf_op jit(solution)/shard_map/pack/pallas_call | solution.py:232
  2.5 11.3 %all-to-all-start = ((bf16[32,72,128]{2,1,0:T(8,128)(2,1)}), bf16[32,72,128]{2,1,0:T(8,128)(2,1)S(1)}, u32[]{:S(2)}, u32[]{:S(2)}) async-start(bf16[32,72,128]{2,1,0:T(8,128)(2,1)} %get-tuple-element.43), calls=%async_computation | async-start | bytes 1179648 | tf_op jit(solution)/shard_map/all_to_all | solution.py:246
  13.8 0.5 collective-permute-start.2
  14.4 2.9 %collective-permute-start.1 = (bf16[528,128]{1,0:T(8,128)(2,1)}, bf16[528,128]{1,0:T(8,128)(2,1)S(1)}, u32[]{:S(2)}, u32[]{:S(2)}) collective-permute-start(bf16[528,128]{1,0:T(8,128)(2,1)} %get-tuple-element.44), channel_id=1, source_target_pairs={{0,32},{128,160},{32,0},{160,128},{1,33},{129,161},{33,1},{161,129... | collective-permute-start | bytes 405512 | tf_op jit(solution)/shard_map/ppermute | solution.py:249
  17.3 3.3 %collective-permute-done.2 = bf16[528,128]{1,0:T(8,128)(2,1)S(1)} collective-permute-done((bf16[528,128]{1,0:T(8,128)(2,1)}, bf16[528,128]{1,0:T(8,128)(2,1)S(1)}, u32[]{:S(2)}, u32[]{:S(2)}) %collective-permute-start.2) | collective-permute-done | bytes 135200 | tf_op jit(solution)/shard_map/ppermute | solution.py:249
  20.6 1.7 %collective-permute-done.1 = bf16[528,128]{1,0:T(8,128)(2,1)S(1)} collective-permute-done((bf16[528,128]{1,0:T(8,128)(2,1)}, bf16[528,128]{1,0:T(8,128)(2,1)S(1)}, u32[]{:S(2)}, u32[]{:S(2)}) %collective-permute-start.1) | collective-permute-done | bytes 135200 | tf_op jit(solution)/shard_map/ppermute | solution.py:249
  22.3 1.4 %collective-permute-done = bf16[528,128]{1,0:T(8,128)(2,1)S(1)} collective-permute-done((bf16[528,128]{1,0:T(8,128)(2,1)}, bf16[528,128]{1,0:T(8,128)(2,1)S(1)}, u32[]{:S(2)}, u32[]{:S(2)}) %collective-permute-start) | collective-permute-done | bytes 135200 | tf_op jit(solution)/shard_map/ppermute | solution.py:249
  23.7 1.0 pad_maximum_fusion.own
  24.8 0.8 tile.10
  25.8 0.9 collective-permute-done.3.other
  26.7 5.6 %all-to-all-done.q_in = bf16[32,72,128]{2,1,0:T(8,128)(2,1)S(1)} async-done(((bf16[32,72,128]{2,1,0:T(8,128)(2,1)}), bf16[32,72,128]{2,1,0:T(8,128)(2,1)S(1)}, u32[]{:S(2)}, u32[]{:S(2)}) %all-to-all-start) | async-done | bytes 589856 | tf_op jit(solution)/shard_map/all_to_all | solution.py:246
  32.3 13.0 %stats.1 = (bf16[4096,256]{1,0:T(8,128)(2,1)S(1)}, bf16[2048,256]{1,0:T(8,128)(2,1)S(1)}, f32[8,2048]{1,0:T(8,128)S(1)}, f32[32,16,128]{2,1,0:T(8,128)S(1)}, f32...) custom-call(s32[3]{0:T(128)S(1)} %pad_add_fusion.here, ...), custom_call_target="tpu_custom_call" | custom-call | flops 536870912 | bytes 8388608 | tf_op jit(solution)/shard_map/stats/pallas_call | solution.py:256
  45.3 16.9 %all_to_all.15.lse_all = f32[32,16,128]{2,1,0:T(8,128)S(1)} all-to-all(f32[32,16,128]{2,1,0:T(8,128)S(1)} %get-tuple-element.48), channel_id=1, replica_groups=mesh['yl'=2,'c'=2,'yh'=2,'x'=4,'z'=8] {'x','z'}, dimensions={0} | all-to-all | bytes 524288 | tf_op jit(solution)/shard_map/all_to_all | solution.py:272
  62.1 3.2 %grad.5 = (f32[512,128]{1,0:T(8,128)S(1)}, f32[4,512,128]{2,1,0:T(8,128)S(1)}, f32[4,512,128]{2,1,0:T(8,128)S(1)}) custom-call(s32[3]{0:T(128)S(1)} %pad_add_fusion.here, bf16[4096,256]{1,0:T(8,128)(2,1)S(1)} %get-tuple-element.45.c_ext, bf16[2048,256]{1,0:T(8,128)(2,1)S(1)} %get-tuple-element.46.q_ext, f32[8,2048]{1,0:T(8,128)S(1)} %get-tuple-element.47.aux, ...), custom_call_target="tpu_custom_call" | custom-call | flops 402653184 | bytes 2097152 | tf_op jit(solution)/shard_map/grad/pallas_call | solution.py:276
  65.3 1.6 %collective-permute-start.4 = (f32[512,128]{1,0:T(8,128)S(1)}, f32[512,128]{1,0:T(8,128)S(1)}, u32[]{:S(2)}, u32[]{:S(2)}) collective-permute-start(f32[512,128]{1,0:T(8,128)S(1)} %get-tuple-element.56), channel_id=1, source_target_pairs={{0,16},{8,24},{16,0},{24,8},{1,17},{9,25},{17,1},{25,9},{2,18},{10... | collective-permute-start | bytes 786440 | tf_op jit(solution)/shard_map/ppermute | solution.py:288
  66.9 3.4 %grad.6 = (f32[512,128]{1,0:T(8,128)S(1)}, f32[4,512,128]{2,1,0:T(8,128)S(1)}, f32[4,512,128]{2,1,0:T(8,128)S(1)}) custom-call(s32[3]{0:T(128)S(1)} %pad_add_fusion.here, bf16[4096,256]{1,0:T(8,128)(2,1)S(1)} %get-tuple-element.45.c_ext, bf16[2048,256]{1,0:T(8,128)(2,1)S(1)} %get-tuple-element.46.q_ext, ...), custom_call_target="tpu_custom_call", output_to_operand_aliasing={{1}: (12, {}), {2}: (13, {})} | custom-call | flops 402653184 | bytes 2097152 | tf_op jit(solution)/shard_map/grad/pallas_call | solution.py:276
  70.3 2.1 %collective-permute-start.5 = (f32[512,128]{1,0:T(8,128)S(1)}, f32[512,128]{1,0:T(8,128)S(1)}, u32[]{:S(2)}, u32[]{:S(2)}) collective-permute-start(f32[512,128]{1,0:T(8,128)S(1)} %get-tuple-element.63), channel_id=1, source_target_pairs={{0,24},{8,0},{16,8},{24,16},{1,25},{9,1},{17,9},{25,17},{2,26},{10... | collective-permute-start | bytes 786440 | tf_op jit(solution)/shard_map/ppermute | solution.py:288
  72.4 3.4 %grad.7 = (f32[512,128]{1,0:T(8,128)S(1)}, f32[4,512,128]{2,1,0:T(8,128)S(1)}, f32[4,512,128]{2,1,0:T(8,128)S(1)}) custom-call(s32[3]{0:T(128)S(1)} %pad_add_fusion.here, bf16[4096,256]{1,0:T(8,128)(2,1)S(1)} %get-tuple-element.45.c_ext, bf16[2048,256]{1,0:T(8,128)(2,1)S(1)} %get-tuple-element.46.q_ext, ...), custom_call_target="tpu_custom_call", output_to_operand_aliasing={{1}: (12, {}), {2}: (13, {})} | custom-call | flops 402653184 | bytes 2097152 | tf_op jit(solution)/shard_map/grad/pallas_call | solution.py:276
  75.7 0.3 collective-permute-start.6
  76.1 2.2 %grad.8 = (f32[512,128]{1,0:T(8,128)S(1)}, f32[4,512,128]{2,1,0:T(8,128)S(1)}) custom-call(s32[3]{0:T(128)S(1)} %pad_add_fusion.here, bf16[4096,256]{1,0:T(8,128)(2,1)S(1)} %get-tuple-element.45.c_ext, bf16[2048,256]{1,0:T(8,128)(2,1)S(1)} %get-tuple-element.46.q_ext, f32[8,2048]{1,0:T(8,128)S(1)} %get-tuple-element.47.aux, ...), custom_call_target="tpu_custom_call", output_to_operand_aliasing={{1}: (12, {})} | custom-call | flops 201326592 | bytes 1048576 | tf_op jit(solution)/shard_map/grad/pallas_call | solution.py:276
  78.4 2.0 %grad.9 = (f32[512,128]{1,0:T(8,128)S(1)}, f32[4,512,128]{2,1,0:T(8,128)S(1)}) custom-call(s32[3]{0:T(128)S(1)} %pad_add_fusion.here, bf16[4096,256]{1,0:T(8,128)(2,1)S(1)} %get-tuple-element.45.c_ext, bf16[2048,256]{1,0:T(8,128)(2,1)S(1)} %get-tuple-element.46.q_ext, ...), custom_call_target="tpu_custom_call", output_to_operand_aliasing={{0}: (12, {}), {1}: (13, {})} | custom-call | flops 201326592 | bytes 1048576 | tf_op jit(solution)/shard_map/grad/pallas_call | solution.py:276
  80.4 3.0 %collective-permute-done.6.c = f32[512,128]{1,0:T(8,128)S(1)} collective-permute-done((f32[512,128]{1,0:T(8,128)S(1)}, f32[512,128]{1,0:T(8,128)S(1)}, u32[]{:S(2)}, u32[]{:S(2)}) %collective-permute-start.6) | collective-permute-done | bytes 262176 | tf_op jit(solution)/shard_map/ppermute | solution.py:288
  83.4 0.8 add.28
  84.3 0.4 collective-permute-start.8
  84.7 3.0 %collective-permute-start.9 = (f32[512,128]{1,0:T(8,128)S(1)}, f32[512,128]{1,0:T(8,128)S(1)}, u32[]{:S(2)}, u32[]{:S(2)}) collective-permute-start(f32[512,128]{1,0:T(8,128)S(1)} %get-tuple-element.82), channel_id=1, source_target_pairs={{0,32},{128,160},{32,0},{160,128},{1,33},{129,161},{33,1},{161,129... | collective-permute-start | bytes 786440 | tf_op jit(solution)/shard_map/ppermute | solution.py:322
  87.7 1.8 %collective-permute-start.10 = (f32[512,128]{1,0:T(8,128)S(1)}, f32[512,128]{1,0:T(8,128)S(1)}, u32[]{:S(2)}, u32[]{:S(2)}) collective-permute-start(f32[512,128]{1,0:T(8,128)S(1)} %get-tuple-element.83), channel_id=1, source_target_pairs={{0,128},{128,32},{32,160},{160,0},{1,129},{129,33},{33,161},{161,1... | collective-permute-start | bytes 786440 | tf_op jit(solution)/shard_map/ppermute | solution.py:322
  89.5 3.4 %all-to-all-start.2 = ((f32[8,64,128]{2,1,0:T(8,128)}), f32[8,64,128]{2,1,0:T(8,128)S(1)}, u32[]{:S(2)}, u32[]{:S(2)}) async-start(f32[8,64,128]{2,1,0:T(8,128)} %bitcast.10), calls=%async_computation.2 | async-start | bytes 524288 | tf_op jit(solution)/shard_map/all_to_all | solution.py:323
  92.9 1.6 %collective-permute-done.9 = f32[512,128]{1,0:T(8,128)S(1)} collective-permute-done((f32[512,128]{1,0:T(8,128)S(1)}, f32[512,128]{1,0:T(8,128)S(1)}, u32[]{:S(2)}, u32[]{:S(2)}) %collective-permute-start.9) | collective-permute-done | bytes 262176 | tf_op jit(solution)/shard_map/ppermute | solution.py:322
  94.6 2.7 %collective-permute-done.10 = f32[512,128]{1,0:T(8,128)S(1)} collective-permute-done((f32[512,128]{1,0:T(8,128)S(1)}, f32[512,128]{1,0:T(8,128)S(1)}, u32[]{:S(2)}, u32[]{:S(2)}) %collective-permute-start.10) | collective-permute-done | bytes 262176 | tf_op jit(solution)/shard_map/ppermute | solution.py:322
  97.2 0.8 add_add_fusion
  98.0 5.4 %all-to-all-done.2 = f32[8,64,128]{2,1,0:T(8,128)S(1)} async-done(((f32[8,64,128]{2,1,0:T(8,128)}), f32[8,64,128]{2,1,0:T(8,128)S(1)}, u32[]{:S(2)}, u32[]{:S(2)}) %all-to-all-start.2) | async-done | bytes 262176 | tf_op jit(solution)/shard_map/all_to_all | solution.py:323
  103.4 0.6 reduce_sum.9
  (11 shorter events, 0.5 us)
Async XLA Ops:
  2.5 29.8 %all-to-all-start = ((bf16[32,72,128]{2,1,0:T(8,128)(2,1)}), bf16[32,72,128]{2,1,0:T(8,128)(2,1)S(1)}, u32[]{:S(2)}, u32[]{:S(2)}) async-start(bf16[32,72,128]{2,1,0:T(8,128)(2,1)} %get-tuple-element.43), calls=%async_computation | async-start | bytes 1179648 | tf_op jit(solution)/shard_map/all_to_all | solution.py:246
  13.8 6.8 %collective-permute-start.2 = (bf16[528,128]{1,0:T(8,128)(2,1)}, bf16[528,128]{1,0:T(8,128)(2,1)S(1)}, u32[]{:S(2)}, u32[]{:S(2)}) collective-permute-start(bf16[528,128]{1,0:T(8,128)(2,1)} %get-tuple-element.44), channel_id=1, source_target_pairs={{0,160},{128,0},{32,128},{160,32},{1,161},{129,1},{33,129},{161,33... | collective-permute-start | bytes 405512 | tf_op jit(solution)/shard_map/ppermute | solution.py:249
  14.4 8.0 %collective-permute-start.1 = (bf16[528,128]{1,0:T(8,128)(2,1)}, bf16[528,128]{1,0:T(8,128)(2,1)S(1)}, u32[]{:S(2)}, u32[]{:S(2)}) collective-permute-start(bf16[528,128]{1,0:T(8,128)(2,1)} %get-tuple-element.44), channel_id=1, source_target_pairs={{0,32},{128,160},{32,0},{160,128},{1,33},{129,161},{33,1},{161,129... | collective-permute-start | bytes 405512 | tf_op jit(solution)/shard_map/ppermute | solution.py:249
  17.3 6.5 %collective-permute-start = (bf16[528,128]{1,0:T(8,128)(2,1)}, bf16[528,128]{1,0:T(8,128)(2,1)S(1)}, u32[]{:S(2)}, u32[]{:S(2)}) collective-permute-start(bf16[528,128]{1,0:T(8,128)(2,1)} %get-tuple-element.44), channel_id=1, source_target_pairs={{0,128},{128,32},{32,160},{160,0},{1,129},{129,33},{33,161},{161,1... | collective-permute-start | bytes 405512 | tf_op jit(solution)/shard_map/ppermute | solution.py:249
  24.7 2.0 %collective-permute-start.3 = (bf16[4,528,128]{2,1,0:T(8,128)(2,1)S(1)}, bf16[4,528,128]{2,1,0:T(8,128)(2,1)S(1)}, u32[]{:S(2)}, u32[]{:S(2)}) collective-permute-start(bf16[4,528,128]{2,1,0:T(8,128)(2,1)S(1)} %pad_maximum_fusion.own), channel_id=1, source_target_pairs={{0,64},{64,0},{1,65},{65,1},{2,66},{66,2},{3,67},{67,3},{4,68},{68... | collective-permute-start | bytes 1622024 | tf_op jit(solution)/shard_map/ppermute | solution.py:252
  65.3 10.8 %collective-permute-start.4 = (f32[512,128]{1,0:T(8,128)S(1)}, f32[512,128]{1,0:T(8,128)S(1)}, u32[]{:S(2)}, u32[]{:S(2)}) collective-permute-start(f32[512,128]{1,0:T(8,128)S(1)} %get-tuple-element.56), channel_id=1, source_target_pairs={{0,16},{8,24},{16,0},{24,8},{1,17},{9,25},{17,1},{25,9},{2,18},{10... | collective-permute-start | bytes 786440 | tf_op jit(solution)/shard_map/ppermute | solution.py:288
  70.3 8.0 %collective-permute-start.5 = (f32[512,128]{1,0:T(8,128)S(1)}, f32[512,128]{1,0:T(8,128)S(1)}, u32[]{:S(2)}, u32[]{:S(2)}) collective-permute-start(f32[512,128]{1,0:T(8,128)S(1)} %get-tuple-element.63), channel_id=1, source_target_pairs={{0,24},{8,0},{16,8},{24,16},{1,25},{9,1},{17,9},{25,17},{2,26},{10... | collective-permute-start | bytes 786440 | tf_op jit(solution)/shard_map/ppermute | solution.py:288
  75.7 7.7 %collective-permute-start.6 = (f32[512,128]{1,0:T(8,128)S(1)}, f32[512,128]{1,0:T(8,128)S(1)}, u32[]{:S(2)}, u32[]{:S(2)}) collective-permute-start(f32[512,128]{1,0:T(8,128)S(1)} %get-tuple-element.67), channel_id=1, source_target_pairs={{0,8},{8,16},{16,24},{24,0},{1,9},{9,17},{17,25},{25,1},{2,10},{10... | collective-permute-start | bytes 786440 | tf_op jit(solution)/shard_map/ppermute | solution.py:288
  78.3 5.9 %collective-permute-start.7 = (f32[4,512,128]{2,1,0:T(8,128)S(1)}, f32[4,512,128]{2,1,0:T(8,128)S(1)}, u32[]{:S(2)}, u32[]{:S(2)}) collective-permute-start(f32[4,512,128]{2,1,0:T(8,128)S(1)} %get-tuple-element.74), channel_id=1, source_target_pairs={{0,64},{64,0},{1,65},{65,1},{2,66},{66,2},{3,67},{67,3},{4,68},{68... | collective-permute-start | bytes 3145736 | tf_op jit(solution)/shard_map/ppermute | solution.py:299
  84.3 8.6 %collective-permute-start.8 = (f32[512,128]{1,0:T(8,128)S(1)}, f32[512,128]{1,0:T(8,128)S(1)}, u32[]{:S(2)}, u32[]{:S(2)}) collective-permute-start(f32[512,128]{1,0:T(8,128)S(1)} %get-tuple-element.81), channel_id=1, source_target_pairs={{0,160},{128,0},{32,128},{160,32},{1,161},{129,1},{33,129},{161,33... | collective-permute-start | bytes 786440 | tf_op jit(solution)/shard_map/ppermute | solution.py:322
  84.7 9.8 %collective-permute-start.9 = (f32[512,128]{1,0:T(8,128)S(1)}, f32[512,128]{1,0:T(8,128)S(1)}, u32[]{:S(2)}, u32[]{:S(2)}) collective-permute-start(f32[512,128]{1,0:T(8,128)S(1)} %get-tuple-element.82), channel_id=1, source_target_pairs={{0,32},{128,160},{32,0},{160,128},{1,33},{129,161},{33,1},{161,129... | collective-permute-start | bytes 786440 | tf_op jit(solution)/shard_map/ppermute | solution.py:322
  87.7 9.5 %collective-permute-start.10 = (f32[512,128]{1,0:T(8,128)S(1)}, f32[512,128]{1,0:T(8,128)S(1)}, u32[]{:S(2)}, u32[]{:S(2)}) collective-permute-start(f32[512,128]{1,0:T(8,128)S(1)} %get-tuple-element.83), channel_id=1, source_target_pairs={{0,128},{128,32},{32,160},{160,0},{1,129},{129,33},{33,161},{161,1... | collective-permute-start | bytes 786440 | tf_op jit(solution)/shard_map/ppermute | solution.py:322
  89.5 13.9 %all-to-all-start.2 = ((f32[8,64,128]{2,1,0:T(8,128)}), f32[8,64,128]{2,1,0:T(8,128)S(1)}, u32[]{:S(2)}, u32[]{:S(2)}) async-start(f32[8,64,128]{2,1,0:T(8,128)} %bitcast.10), calls=%async_computation.2 | async-start | bytes 524288 | tf_op jit(solution)/shard_map/all_to_all | solution.py:323

commit v7 on v6

--- a/solution.py
+++ b/solution.py
@@ -166,36 +166,42 @@
     return weight / (aux[1:2, pl.ds(first, count)] + others)
 
 
-def grad_kernel(shift, halves, here, c_ext, q_ext, aux, lse_all, *refs):
-    n = len(halves)
-    kept, refs = refs[: KEPT], refs[KEPT:]
-    before = refs[: len(refs) - 1 - n]
-    u_out, g_outs = refs[-1 - n], refs[-n:]
-    u_in = before[0] if len(before) in (1, n + 1) and shift == 0 and halves == (0,) else None
-    g_ins = before[-n:] if len(before) >= n and shift != 2 else [None] * n
-    first = pl.multiple_of(((here[2] >> 3) - shift & 3) * QUART, QUART)
-    span = pl.ds(first, QUART)
-    scale = row_scale(here, aux, lse_all, first, QUART) * aux[5:6, span]
-    queries = q_ext[span, :]
-    narrow = queries[:, :E]
-    base, weight = aux[4:5, span], aux[2:3, span]
-    local = aux[3:4, span].astype(i32)
-    total = jnp.zeros((QUART, E), f32) if u_in is None else u_in[...]
+def grad_kernel(shifts, halves, here, c_ext, q_ext, aux, lse_all, *refs):
+    n, m = len(halves), len(shifts)
+    kept, refs = refs[:KEPT], refs[KEPT:]
+    before = refs[: len(refs) - m - n]
+    u_outs, g_outs = refs[-m - n : -n], refs[-n:]
+    u_in = before[0] if len(before) == n + 1 else None
+    g_ins = before[-n:] if before else [None] * n
+    rows = []
+    for shift in shifts:
+        first = pl.multiple_of(((here[2] >> 3) - shift & 3) * QUART, QUART)
+        span = pl.ds(first, QUART)
+        scale = row_scale(here, aux, lse_all, first, QUART) * aux[5:6, span]
+        rows.append((span, scale, aux[4:5, span], aux[2:3, span], aux[3:4, span].astype(i32)))
+    totals = [jnp.zeros((QUART, E), f32) if u_in is None else u_in[...] for _ in shifts]
     for half, g_in, g_out in zip(halves, g_ins, g_outs):
         for k in range(NY):
             row = half * HALF + k * CB
             block = c_ext[row : row + CB, :]
-            if half * NY + k < KEPT:
-                expo = kept[half * NY + k][:, span] * scale
-            else:
-                logits = lax.dot_general(block, queries, NT, preferred_element_type=f32)
-                expo = jnp.exp(logits - base) * scale
-            matched = lax.broadcasted_iota(i32, expo.shape, 0) == (local - row)
-            grad = (expo - jnp.where(matched, weight, 0.0)).astype(bf16)
-            g_part = lax.dot_general(grad, narrow, NN, preferred_element_type=f32)
-            g_out[k] = g_part if g_in is None else g_in[k] + g_part
-            total = total + lax.dot_general(grad, block[:, :E], TN, preferred_element_type=f32)
-    u_out[...] = total
+            g_sum = None if g_in is None else g_in[k]
+            for t, (span, scale, base, weight, local) in enumerate(rows):
+                queries = q_ext[span, :]
+                if half * NY + k < KEPT:
+                    expo = kept[half * NY + k][:, span] * scale
+                else:
+                    logits = lax.dot_general(block, queries, NT, preferred_element_type=f32)
+                    expo = jnp.exp(logits - base) * scale
+                matched = lax.broadcasted_iota(i32, expo.shape, 0) == (local - row)
+                grad = (expo - jnp.where(matched, weight, 0.0)).astype(bf16)
+                g_part = lax.dot_general(grad, queries[:, :E], NN, preferred_element_type=f32)
+                g_sum = g_part if g_sum is None else g_sum + g_part
+                totals[t] = totals[t] + lax.dot_general(
+                    grad, block[:, :E], TN, preferred_element_type=f32
+                )
+            g_out[k] = g_sum
+    for u_out, total in zip(u_outs, totals):
+        u_out[...] = total
 
 
 def merge_kernel(own, came, *outs):
@@ -271,33 +277,31 @@
     )(here, table, q_in, own, other)
     lse_all = lax.all_to_all(lse, GROUP, 0, 0, tiled=True)
 
-    def grads(shift, halves, *extra, aliases):
+    def grads(shifts, halves, *extra, aliases):
         n = len(halves)
         return pl.pallas_call(
-            functools.partial(grad_kernel, shift, halves),
-            out_shape=[shaped((QUART, E), f32)] + [shaped((NY, CB, E), f32)] * n,
+            functools.partial(grad_kernel, shifts, halves),
+            out_shape=[shaped((QUART, E), f32)] * len(shifts) + [shaped((NY, CB, E), f32)] * n,
             in_specs=[SMEM] + [VMEM] * (4 + KEPT + len(extra)),
-            out_specs=[VMEM] * (1 + n),
+            out_specs=[VMEM] * (len(shifts) + n),
             input_output_aliases={i + KEPT: o for i, o in aliases.items()},
             compiler_params=PARAMS,
-            cost_estimate=cost(QUART * HALF * n, 3),
+            cost_estimate=cost(QUART * HALF * n * len(shifts), 3),
             name="grad",
         )(here, c_ext, q_ext, aux, lse_all, *kept, *extra)
 
     def along_x(piece, shift):
         return lax.ppermute(piece, "x", [(i, (i - shift) % NX) for i in range(NX)])
 
-    piece, g_a, g_b = grads(2, (0, 1), aliases={})
+    piece, g_a, g_b = grads((2,), (0, 1), aliases={})
     u_two = along_x(piece, 2)
-    piece, g_a, g_b = grads(1, (0, 1), g_a, g_b, aliases={5: 1, 6: 2})
-    u_one = along_x(piece, 1)
-    piece, g_a, g_b = grads(3, (0, 1), g_a, g_b, aliases={5: 1, 6: 2})
-    u_three = along_x(piece, 3)
+    one, three, g_a, g_b = grads((1, 3), (0, 1), g_a, g_b, aliases={5: 2, 6: 3})
+    u_one = along_x(one, 1)
+    u_three = along_x(three, 3)
     u_two, g_b = lax.optimization_barrier((u_two, g_b))
-    u_own, g_other = grads(0, (1,), g_b, aliases={5: 1})
-    u_one, g_other = lax.optimization_barrier((u_one, g_other))
+    u_own, g_other = grads((0,), (1,), g_b, aliases={5: 1})
     g_came = lax.ppermute(g_other, "c", swap)
-    u_own, g_own = grads(0, (0,), u_own, g_a, aliases={5: 0, 6: 1})
+    u_own, g_own = grads((0,), (0,), u_own, g_a, aliases={5: 0, 6: 1})
 
     u_line = pl.pallas_call(
         add_kernel,

time: 104 us -> 103 us (level)
    pallas_call x5 -> x4, Pallas kernels: 14.1 us -> 13.3 us  [grads(): pl.pallas_call(functools.partial(grad_kernel, shifts, halves), out_shape=...]
  transfers between devices with their start and end apart: 13 -> 13, of which waited for: 9 -> 10; matrix products, arithmetic and copies ran while one was open for 3% -> 3% of each run, Pallas kernels for 11% -> 10%
where the time goes in v7:
time: 103 us
  Pallas kernels  28.9 us (28%)
  starting transfers between devices  27.5 us (27%)
  waiting for transfers between devices  25.8 us (25%)
  blocking collectives  16.9 us (16%)
  other arithmetic  2.44 us (2%)
    all_to_all x1, blocking collectives, per_device(): lse_all = lax.all_to_all(lse, GROUP, 0, 0, tiled=True)  16.9 us
    pallas_call x4, Pallas kernels, grads(): pl.pallas_call(functools.partial(grad_kernel, shifts, halves), out_shape=...  13.3 us
    pallas_call x1, Pallas kernels, per_device(): pl.pallas_call(stats_kernel, out_shape=[shaped((NC, 2 * E), bf16), shaped...  12.9 us
    all_to_all x1, starting transfers between devices, per_device(): q_in = lax.all_to_all(q_block, GROUP, 0, 0, tiled=True)  11.3 us
    ppermute x3, waiting for transfers between devices, per_device(): spread.append(lax.ppermute(c_block, RING, ring(s)))  6.47 us
    all_to_all x1, waiting for transfers between devices, per_device(): q_in = lax.all_to_all(q_block, GROUP, 0, 0, tiled=True)  5.56 us
    all_to_all x1, waiting for transfers between devices, per_device(): u_in = lax.all_to_all(u_line.reshape(NZ, QB, E), 'z', 0, 0, tiled=True)  5.31 us
    ppermute x3, starting transfers between devices, per_device(): pieces[s] = lax.ppermute(pieces[s], RING, ring(-s))  5.22 us
  transfers between devices with their start and end apart: 13, of which 10 were waited for; matrix products, arithmetic and copies ran while one was open for 3% of the time, Pallas kernels for 10%

profile of v7, /device:TPU:16, one launch (start us, length us, event | category | flops | bytes accessed | tf_op | source)
XLA Modules:
  0.0 103.1 jit_solution(11164850168936789303)
XLA Ops:
  0.6 1.9 %pack.1 = (bf16[32,72,128]{2,1,0:T(8,128)(2,1)}, bf16[528,128]{1,0:T(8,128)(2,1)}) custom-call(bf16[64,128]{1,0:T(8,128)(2,1)} %queries.1, s32[1,64]{1,0:T(1,128)} %bitcast.16, bf16[1,64]{1,0:T(2,128)(2,1)} %bitcast.17, bf16[512,128]{1,0:T(8,128)(2,1)} %candidates.1, s32[4,128]{1,0:T(4,128)} %bitcast.15), custom_call_target="tpu_custom_call" | custom-call | tf_op jit(solution)/shard_map/pack/pallas_call | solution.py:238
  2.5 11.3 %all-to-all-start = ((bf16[32,72,128]{2,1,0:T(8,128)(2,1)}), bf16[32,72,128]{2,1,0:T(8,128)(2,1)S(1)}, u32[]{:S(2)}, u32[]{:S(2)}) async-start(bf16[32,72,128]{2,1,0:T(8,128)(2,1)} %get-tuple-element.39), calls=%async_computation | async-start | bytes 1179648 | tf_op jit(solution)/shard_map/all_to_all | solution.py:252
  13.8 0.5 collective-permute-start.2
  14.3 2.9 %collective-permute-start.1 = (bf16[528,128]{1,0:T(8,128)(2,1)}, bf16[528,128]{1,0:T(8,128)(2,1)S(1)}, u32[]{:S(2)}, u32[]{:S(2)}) collective-permute-start(bf16[528,128]{1,0:T(8,128)(2,1)} %get-tuple-element.40), channel_id=1, source_target_pairs={{0,32},{128,160},{32,0},{160,128},{1,33},{129,161},{33,1},{161,129... | collective-permute-start | bytes 405512 | tf_op jit(solution)/shard_map/ppermute | solution.py:255
  17.3 3.3 %collective-permute-done.2 = bf16[528,128]{1,0:T(8,128)(2,1)S(1)} collective-permute-done((bf16[528,128]{1,0:T(8,128)(2,1)}, bf16[528,128]{1,0:T(8,128)(2,1)S(1)}, u32[]{:S(2)}, u32[]{:S(2)}) %collective-permute-start.2) | collective-permute-done | bytes 135200 | tf_op jit(solution)/shard_map/ppermute | solution.py:255
  20.6 1.7 %collective-permute-done.1 = bf16[528,128]{1,0:T(8,128)(2,1)S(1)} collective-permute-done((bf16[528,128]{1,0:T(8,128)(2,1)}, bf16[528,128]{1,0:T(8,128)(2,1)S(1)}, u32[]{:S(2)}, u32[]{:S(2)}) %collective-permute-start.1) | collective-permute-done | bytes 135200 | tf_op jit(solution)/shard_map/ppermute | solution.py:255
  22.3 1.4 %collective-permute-done = bf16[528,128]{1,0:T(8,128)(2,1)S(1)} collective-permute-done((bf16[528,128]{1,0:T(8,128)(2,1)}, bf16[528,128]{1,0:T(8,128)(2,1)S(1)}, u32[]{:S(2)}, u32[]{:S(2)}) %collective-permute-start) | collective-permute-done | bytes 135200 | tf_op jit(solution)/shard_map/ppermute | solution.py:255
  23.7 1.0 pad_maximum_fusion.own
  24.8 0.8 tile.10
  25.8 0.9 collective-permute-done.3.other
  26.7 5.6 %all-to-all-done.q_in = bf16[32,72,128]{2,1,0:T(8,128)(2,1)S(1)} async-done(((bf16[32,72,128]{2,1,0:T(8,128)(2,1)}), bf16[32,72,128]{2,1,0:T(8,128)(2,1)S(1)}, u32[]{:S(2)}, u32[]{:S(2)}) %all-to-all-start) | async-done | bytes 589856 | tf_op jit(solution)/shard_map/all_to_all | solution.py:252
  32.3 12.9 %stats.1 = (bf16[4096,256]{1,0:T(8,128)(2,1)S(1)}, bf16[2048,256]{1,0:T(8,128)(2,1)S(1)}, f32[8,2048]{1,0:T(8,128)S(1)}, f32[32,16,128]{2,1,0:T(8,128)S(1)}, f32...) custom-call(s32[3]{0:T(128)S(1)} %pad_add_fusion.here, ...), custom_call_target="tpu_custom_call" | custom-call | flops 536870912 | bytes 8388608 | tf_op jit(solution)/shard_map/stats/pallas_call | solution.py:262
  45.2 16.9 %all_to_all.15.lse_all = f32[32,16,128]{2,1,0:T(8,128)S(1)} all-to-all(f32[32,16,128]{2,1,0:T(8,128)S(1)} %get-tuple-element.44), channel_id=1, replica_groups=mesh['yl'=2,'c'=2,'yh'=2,'x'=4,'z'=8] {'x','z'}, dimensions={0} | all-to-all | bytes 524288 | tf_op jit(solution)/shard_map/all_to_all | solution.py:278
  62.1 3.2 %grad.4 = (f32[512,128]{1,0:T(8,128)S(1)}, f32[4,512,128]{2,1,0:T(8,128)S(1)}, f32[4,512,128]{2,1,0:T(8,128)S(1)}) custom-call(s32[3]{0:T(128)S(1)} %pad_add_fusion.here, bf16[4096,256]{1,0:T(8,128)(2,1)S(1)} %get-tuple-element.41.c_ext, bf16[2048,256]{1,0:T(8,128)(2,1)S(1)} %get-tuple-element.42.q_ext, f32[8,2048]{1,0:T(8,128)S(1)} %get-tuple-element.43.aux, ...), custom_call_target="tpu_custom_call" | custom-call | flops 402653184 | bytes 2097152 | tf_op jit(solution)/shard_map/grad/pallas_call | solution.py:282
  65.3 1.8 %collective-permute-start.4 = (f32[512,128]{1,0:T(8,128)S(1)}, f32[512,128]{1,0:T(8,128)S(1)}, u32[]{:S(2)}, u32[]{:S(2)}) collective-permute-start(f32[512,128]{1,0:T(8,128)S(1)} %get-tuple-element.52), channel_id=1, source_target_pairs={{0,16},{8,24},{16,0},{24,8},{1,17},{9,25},{17,1},{25,9},{2,18},{10... | collective-permute-start | bytes 786440 | tf_op jit(solution)/shard_map/ppermute | solution.py:294
  67.1 5.9 %grad.5 = (f32[512,128]{1,0:T(8,128)S(1)}, f32[512,128]{1,0:T(8,128)S(1)}, f32[4,512,128]{2,1,0:T(8,128)S(1)}, f32[4,512,128]{2,1,0:T(8,128)S(1)}) custom-call(s32[3]{0:T(128)S(1)} %pad_add_fusion.here, bf16[4096,256]{1,0:T(8,128)(2,1)S(1)} %get-tuple-element.41.c_ext, ...), custom_call_target="tpu_custom_call", output_to_operand_aliasing={{2}: (12, {}), {3}: (13, {})} | custom-call | flops 805306368 | bytes 4194304 | tf_op jit(solution)/shard_map/grad/pallas_call | solution.py:282
  73.1 1.9 %collective-permute-start.5 = (f32[512,128]{1,0:T(8,128)S(1)}, f32[512,128]{1,0:T(8,128)S(1)}, u32[]{:S(2)}, u32[]{:S(2)}) collective-permute-start(f32[512,128]{1,0:T(8,128)S(1)} %get-tuple-element.57), channel_id=1, source_target_pairs={{0,24},{8,0},{16,8},{24,16},{1,25},{9,1},{17,9},{25,17},{2,26},{10... | collective-permute-start | bytes 786440 | tf_op jit(solution)/shard_map/ppermute | solution.py:294
  74.9 0.3 collective-permute-start.6
  75.2 2.2 %grad.6 = (f32[512,128]{1,0:T(8,128)S(1)}, f32[4,512,128]{2,1,0:T(8,128)S(1)}) custom-call(s32[3]{0:T(128)S(1)} %pad_add_fusion.here, bf16[4096,256]{1,0:T(8,128)(2,1)S(1)} %get-tuple-element.41.c_ext, bf16[2048,256]{1,0:T(8,128)(2,1)S(1)} %get-tuple-element.42.q_ext, f32[8,2048]{1,0:T(8,128)S(1)} %get-tuple-element.43.aux, ...), custom_call_target="tpu_custom_call", output_to_operand_aliasing={{1}: (12, {})} | custom-call | flops 201326592 | bytes 1048576 | tf_op jit(solution)/shard_map/grad/pallas_call | solution.py:282
  77.4 2.0 %grad.7 = (f32[512,128]{1,0:T(8,128)S(1)}, f32[4,512,128]{2,1,0:T(8,128)S(1)}) custom-call(s32[3]{0:T(128)S(1)} %pad_add_fusion.here, bf16[4096,256]{1,0:T(8,128)(2,1)S(1)} %get-tuple-element.41.c_ext, bf16[2048,256]{1,0:T(8,128)(2,1)S(1)} %get-tuple-element.42.q_ext, ...), custom_call_target="tpu_custom_call", output_to_operand_aliasing={{0}: (12, {}), {1}: (13, {})} | custom-call | flops 201326592 | bytes 1048576 | tf_op jit(solution)/shard_map/grad/pallas_call | solution.py:282
  79.5 3.0 %collective-permute-done.6.c = f32[512,128]{1,0:T(8,128)S(1)} collective-permute-done((f32[512,128]{1,0:T(8,128)S(1)}, f32[512,128]{1,0:T(8,128)S(1)}, u32[]{:S(2)}, u32[]{:S(2)}) %collective-permute-start.6) | collective-permute-done | bytes 262176 | tf_op jit(solution)/shard_map/ppermute | solution.py:294
  82.5 0.7 add.28
  83.2 0.1 merge.1
  83.4 0.5 collective-permute-start.8
  83.9 2.9 %collective-permute-start.9 = (f32[512,128]{1,0:T(8,128)S(1)}, f32[512,128]{1,0:T(8,128)S(1)}, u32[]{:S(2)}, u32[]{:S(2)}) collective-permute-start(f32[512,128]{1,0:T(8,128)S(1)} %get-tuple-element.74), channel_id=1, source_target_pairs={{0,32},{128,160},{32,0},{160,128},{1,33},{129,161},{33,1},{161,129... | collective-permute-start | bytes 786440 | tf_op jit(solution)/shard_map/ppermute | solution.py:326
  86.8 1.8 %collective-permute-start.10 = (f32[512,128]{1,0:T(8,128)S(1)}, f32[512,128]{1,0:T(8,128)S(1)}, u32[]{:S(2)}, u32[]{:S(2)}) collective-permute-start(f32[512,128]{1,0:T(8,128)S(1)} %get-tuple-element.75), channel_id=1, source_target_pairs={{0,128},{128,32},{32,160},{160,0},{1,129},{129,33},{33,161},{161,1... | collective-permute-start | bytes 786440 | tf_op jit(solution)/shard_map/ppermute | solution.py:326
  88.6 3.4 %all-to-all-start.2 = ((f32[8,64,128]{2,1,0:T(8,128)}), f32[8,64,128]{2,1,0:T(8,128)S(1)}, u32[]{:S(2)}, u32[]{:S(2)}) async-start(f32[8,64,128]{2,1,0:T(8,128)} %bitcast.10), calls=%async_computation.2 | async-start | bytes 524288 | tf_op jit(solution)/shard_map/all_to_all | solution.py:327
  92.0 1.7 %collective-permute-done.9 = f32[512,128]{1,0:T(8,128)S(1)} collective-permute-done((f32[512,128]{1,0:T(8,128)S(1)}, f32[512,128]{1,0:T(8,128)S(1)}, u32[]{:S(2)}, u32[]{:S(2)}) %collective-permute-start.9) | collective-permute-done | bytes 262176 | tf_op jit(solution)/shard_map/ppermute | solution.py:326
  93.7 2.7 %collective-permute-done.10 = f32[512,128]{1,0:T(8,128)S(1)} collective-permute-done((f32[512,128]{1,0:T(8,128)S(1)}, f32[512,128]{1,0:T(8,128)S(1)}, u32[]{:S(2)}, u32[]{:S(2)}) %collective-permute-start.10) | collective-permute-done | bytes 262176 | tf_op jit(solution)/shard_map/ppermute | solution.py:326
  96.4 0.8 add_add_fusion
  97.2 5.3 %all-to-all-done.2 = f32[8,64,128]{2,1,0:T(8,128)S(1)} async-done(((f32[8,64,128]{2,1,0:T(8,128)}), f32[8,64,128]{2,1,0:T(8,128)S(1)}, u32[]{:S(2)}, u32[]{:S(2)}) %all-to-all-start.2) | async-done | bytes 262176 | tf_op jit(solution)/shard_map/all_to_all | solution.py:327
  102.5 0.6 reduce_sum.9
  (10 shorter events, 0.5 us)
Async XLA Ops:
  2.5 29.8 %all-to-all-start = ((bf16[32,72,128]{2,1,0:T(8,128)(2,1)}), bf16[32,72,128]{2,1,0:T(8,128)(2,1)S(1)}, u32[]{:S(2)}, u32[]{:S(2)}) async-start(bf16[32,72,128]{2,1,0:T(8,128)(2,1)} %get-tuple-element.39), calls=%async_computation | async-start | bytes 1179648 | tf_op jit(solution)/shard_map/all_to_all | solution.py:252
  13.8 6.8 %collective-permute-start.2 = (bf16[528,128]{1,0:T(8,128)(2,1)}, bf16[528,128]{1,0:T(8,128)(2,1)S(1)}, u32[]{:S(2)}, u32[]{:S(2)}) collective-permute-start(bf16[528,128]{1,0:T(8,128)(2,1)} %get-tuple-element.40), channel_id=1, source_target_pairs={{0,160},{128,0},{32,128},{160,32},{1,161},{129,1},{33,129},{161,33... | collective-permute-start | bytes 405512 | tf_op jit(solution)/shard_map/ppermute | solution.py:255
  14.3 8.0 %collective-permute-start.1 = (bf16[528,128]{1,0:T(8,128)(2,1)}, bf16[528,128]{1,0:T(8,128)(2,1)S(1)}, u32[]{:S(2)}, u32[]{:S(2)}) collective-permute-start(bf16[528,128]{1,0:T(8,128)(2,1)} %get-tuple-element.40), channel_id=1, source_target_pairs={{0,32},{128,160},{32,0},{160,128},{1,33},{129,161},{33,1},{161,129... | collective-permute-start | bytes 405512 | tf_op jit(solution)/shard_map/ppermute | solution.py:255
  17.3 6.5 %collective-permute-start = (bf16[528,128]{1,0:T(8,128)(2,1)}, bf16[528,128]{1,0:T(8,128)(2,1)S(1)}, u32[]{:S(2)}, u32[]{:S(2)}) collective-permute-start(bf16[528,128]{1,0:T(8,128)(2,1)} %get-tuple-element.40), channel_id=1, source_target_pairs={{0,128},{128,32},{32,160},{160,0},{1,129},{129,33},{33,161},{161,1... | collective-permute-start | bytes 405512 | tf_op jit(solution)/shard_map/ppermute | solution.py:255
  24.7 2.0 %collective-permute-start.3 = (bf16[4,528,128]{2,1,0:T(8,128)(2,1)S(1)}, bf16[4,528,128]{2,1,0:T(8,128)(2,1)S(1)}, u32[]{:S(2)}, u32[]{:S(2)}) collective-permute-start(bf16[4,528,128]{2,1,0:T(8,128)(2,1)S(1)} %pad_maximum_fusion.own), channel_id=1, source_target_pairs={{0,64},{64,0},{1,65},{65,1},{2,66},{66,2},{3,67},{67,3},{4,68},{68... | collective-permute-start | bytes 1622024 | tf_op jit(solution)/shard_map/ppermute | solution.py:258
  65.3 9.8 %collective-permute-start.4 = (f32[512,128]{1,0:T(8,128)S(1)}, f32[512,128]{1,0:T(8,128)S(1)}, u32[]{:S(2)}, u32[]{:S(2)}) collective-permute-start(f32[512,128]{1,0:T(8,128)S(1)} %get-tuple-element.52), channel_id=1, source_target_pairs={{0,16},{8,24},{16,0},{24,8},{1,17},{9,25},{17,1},{25,9},{2,18},{10... | collective-permute-start | bytes 786440 | tf_op jit(solution)/shard_map/ppermute | solution.py:294
  73.1 6.4 %collective-permute-start.5 = (f32[512,128]{1,0:T(8,128)S(1)}, f32[512,128]{1,0:T(8,128)S(1)}, u32[]{:S(2)}, u32[]{:S(2)}) collective-permute-start(f32[512,128]{1,0:T(8,128)S(1)} %get-tuple-element.57), channel_id=1, source_target_pairs={{0,24},{8,0},{16,8},{24,16},{1,25},{9,1},{17,9},{25,17},{2,26},{10... | collective-permute-start | bytes 786440 | tf_op jit(solution)/shard_map/ppermute | solution.py:294
  74.9 7.6 %collective-permute-start.6 = (f32[512,128]{1,0:T(8,128)S(1)}, f32[512,128]{1,0:T(8,128)S(1)}, u32[]{:S(2)}, u32[]{:S(2)}) collective-permute-start(f32[512,128]{1,0:T(8,128)S(1)} %get-tuple-element.58), channel_id=1, source_target_pairs={{0,8},{8,16},{16,24},{24,0},{1,9},{9,17},{17,25},{25,1},{2,10},{10... | collective-permute-start | bytes 786440 | tf_op jit(solution)/shard_map/ppermute | solution.py:294
  77.3 5.9 %collective-permute-start.7 = (f32[4,512,128]{2,1,0:T(8,128)S(1)}, f32[4,512,128]{2,1,0:T(8,128)S(1)}, u32[]{:S(2)}, u32[]{:S(2)}) collective-permute-start(f32[4,512,128]{2,1,0:T(8,128)S(1)} %get-tuple-element.66), channel_id=1, source_target_pairs={{0,64},{64,0},{1,65},{65,1},{2,66},{66,2},{3,67},{67,3},{4,68},{68... | collective-permute-start | bytes 3145736 | tf_op jit(solution)/shard_map/ppermute | solution.py:303
  83.4 8.6 %collective-permute-start.8 = (f32[512,128]{1,0:T(8,128)S(1)}, f32[512,128]{1,0:T(8,128)S(1)}, u32[]{:S(2)}, u32[]{:S(2)}) collective-permute-start(f32[512,128]{1,0:T(8,128)S(1)} %get-tuple-element.73), channel_id=1, source_target_pairs={{0,160},{128,0},{32,128},{160,32},{1,161},{129,1},{33,129},{161,33... | collective-permute-start | bytes 786440 | tf_op jit(solution)/shard_map/ppermute | solution.py:326
  83.9 9.8 %collective-permute-start.9 = (f32[512,128]{1,0:T(8,128)S(1)}, f32[512,128]{1,0:T(8,128)S(1)}, u32[]{:S(2)}, u32[]{:S(2)}) collective-permute-start(f32[512,128]{1,0:T(8,128)S(1)} %get-tuple-element.74), channel_id=1, source_target_pairs={{0,32},{128,160},{32,0},{160,128},{1,33},{129,161},{33,1},{161,129... | collective-permute-start | bytes 786440 | tf_op jit(solution)/shard_map/ppermute | solution.py:326
  86.8 9.6 %collective-permute-start.10 = (f32[512,128]{1,0:T(8,128)S(1)}, f32[512,128]{1,0:T(8,128)S(1)}, u32[]{:S(2)}, u32[]{:S(2)}) collective-permute-start(f32[512,128]{1,0:T(8,128)S(1)} %get-tuple-element.75), channel_id=1, source_target_pairs={{0,128},{128,32},{32,160},{160,0},{1,129},{129,33},{33,161},{161,1... | collective-permute-start | bytes 786440 | tf_op jit(solution)/shard_map/ppermute | solution.py:326
  88.6 13.9 %all-to-all-start.2 = ((f32[8,64,128]{2,1,0:T(8,128)}), f32[8,64,128]{2,1,0:T(8,128)S(1)}, u32[]{:S(2)}, u32[]{:S(2)}) async-start(f32[8,64,128]{2,1,0:T(8,128)} %bitcast.10), calls=%async_computation.2 | async-start | bytes 524288 | tf_op jit(solution)/shard_map/all_to_all | solution.py:327

commit v8 on v7

--- a/solution.py
+++ b/solution.py
@@ -322,7 +322,7 @@
         name="merge",
     )(g_own, g_came)
     u_line, *pieces = lax.optimization_barrier((u_line, *pieces))
-    for s in range(1, NY):
+    for s in (2, 1, 3):
         pieces[s] = lax.ppermute(pieces[s], RING, ring(-s))
     u_in = lax.all_to_all(u_line.reshape(NZ, QB, E), "z", 0, 0, tiled=True)
     query_grad = jnp.sum(u_in, axis=0)

time: 103 us -> 104 us (level)
  no operation moved by 1% of the time
where the time goes in v8:
time: 104 us; the launch traced here: 103 us
  Pallas kernels  28.9 us (28%)
  starting transfers between devices  27.7 us (27%)
  waiting for transfers between devices  25.8 us (25%)
  blocking collectives  16.9 us (16%)
  other arithmetic  2.44 us (2%)
    all_to_all x1, blocking collectives, per_device(): lse_all = lax.all_to_all(lse, GROUP, 0, 0, tiled=True)  16.9 us
    pallas_call x4, Pallas kernels, grads(): pl.pallas_call(functools.partial(grad_kernel, shifts, halves), out_shape=...  13.3 us
    pallas_call x1, Pallas kernels, per_device(): pl.pallas_call(stats_kernel, out_shape=[shaped((NC, 2 * E), bf16), shaped...  12.9 us
    all_to_all x1, starting transfers between devices, per_device(): q_in = lax.all_to_all(q_block, GROUP, 0, 0, tiled=True)  11.3 us
    ppermute x3, waiting for transfers between devices, per_device(): spread.append(lax.ppermute(c_block, RING, ring(s)))  6.47 us
    all_to_all x1, waiting for transfers between devices, per_device(): u_in = lax.all_to_all(u_line.reshape(NZ, QB, E), 'z', 0, 0, tiled=True)  5.66 us
    all_to_all x1, waiting for transfers between devices, per_device(): q_in = lax.all_to_all(q_block, GROUP, 0, 0, tiled=True)  5.56 us
    ppermute x3, starting transfers between devices, per_device(): pieces[s] = lax.ppermute(pieces[s], RING, ring(-s))  5.07 us
  transfers between devices with their start and end apart: 13, of which 10 were waited for; matrix products, arithmetic and copies ran while one was open for 3% of the time, Pallas kernels for 10%

profile of v8, /device:TPU:16, one launch (start us, length us, event | category | flops | bytes accessed | tf_op | source)
XLA Modules:
  0.0 103.4 jit_solution(11164850168936789303)
XLA Ops:
  0.6 1.9 %pack.1 = (bf16[32,72,128]{2,1,0:T(8,128)(2,1)}, bf16[528,128]{1,0:T(8,128)(2,1)}) custom-call(bf16[64,128]{1,0:T(8,128)(2,1)} %queries.1, s32[1,64]{1,0:T(1,128)} %bitcast.16, bf16[1,64]{1,0:T(2,128)(2,1)} %bitcast.17, bf16[512,128]{1,0:T(8,128)(2,1)} %candidates.1, s32[4,128]{1,0:T(4,128)} %bitcast.15), custom_call_target="tpu_custom_call" | custom-call | tf_op jit(solution)/shard_map/pack/pallas_call | solution.py:238
  2.5 11.3 %all-to-all-start = ((bf16[32,72,128]{2,1,0:T(8,128)(2,1)}), bf16[32,72,128]{2,1,0:T(8,128)(2,1)S(1)}, u32[]{:S(2)}, u32[]{:S(2)}) async-start(bf16[32,72,128]{2,1,0:T(8,128)(2,1)} %get-tuple-element.39), calls=%async_computation | async-start | bytes 1179648 | tf_op jit(solution)/shard_map/all_to_all | solution.py:252
  13.8 0.5 collective-permute-start.2
  14.3 2.9 %collective-permute-start.1 = (bf16[528,128]{1,0:T(8,128)(2,1)}, bf16[528,128]{1,0:T(8,128)(2,1)S(1)}, u32[]{:S(2)}, u32[]{:S(2)}) collective-permute-start(bf16[528,128]{1,0:T(8,128)(2,1)} %get-tuple-element.40), channel_id=1, source_target_pairs={{0,32},{128,160},{32,0},{160,128},{1,33},{129,161},{33,1},{161,129... | collective-permute-start | bytes 405512 | tf_op jit(solution)/shard_map/ppermute | solution.py:255
  17.3 3.3 %collective-permute-done.2 = bf16[528,128]{1,0:T(8,128)(2,1)S(1)} collective-permute-done((bf16[528,128]{1,0:T(8,128)(2,1)}, bf16[528,128]{1,0:T(8,128)(2,1)S(1)}, u32[]{:S(2)}, u32[]{:S(2)}) %collective-permute-start.2) | collective-permute-done | bytes 135200 | tf_op jit(solution)/shard_map/ppermute | solution.py:255
  20.6 1.7 %collective-permute-done.1 = bf16[528,128]{1,0:T(8,128)(2,1)S(1)} collective-permute-done((bf16[528,128]{1,0:T(8,128)(2,1)}, bf16[528,128]{1,0:T(8,128)(2,1)S(1)}, u32[]{:S(2)}, u32[]{:S(2)}) %collective-permute-start.1) | collective-permute-done | bytes 135200 | tf_op jit(solution)/shard_map/ppermute | solution.py:255
  22.3 1.4 %collective-permute-done = bf16[528,128]{1,0:T(8,128)(2,1)S(1)} collective-permute-done((bf16[528,128]{1,0:T(8,128)(2,1)}, bf16[528,128]{1,0:T(8,128)(2,1)S(1)}, u32[]{:S(2)}, u32[]{:S(2)}) %collective-permute-start) | collective-permute-done | bytes 135200 | tf_op jit(solution)/shard_map/ppermute | solution.py:255
  23.7 1.0 pad_maximum_fusion.own
  24.8 0.8 tile.10
  25.8 0.9 collective-permute-done.3.other
  26.7 5.6 %all-to-all-done.q_in = bf16[32,72,128]{2,1,0:T(8,128)(2,1)S(1)} async-done(((bf16[32,72,128]{2,1,0:T(8,128)(2,1)}), bf16[32,72,128]{2,1,0:T(8,128)(2,1)S(1)}, u32[]{:S(2)}, u32[]{:S(2)}) %all-to-all-start) | async-done | bytes 589856 | tf_op jit(solution)/shard_map/all_to_all | solution.py:252
  32.3 12.9 %stats.1 = (bf16[4096,256]{1,0:T(8,128)(2,1)S(1)}, bf16[2048,256]{1,0:T(8,128)(2,1)S(1)}, f32[8,2048]{1,0:T(8,128)S(1)}, f32[32,16,128]{2,1,0:T(8,128)S(1)}, f32...) custom-call(s32[3]{0:T(128)S(1)} %pad_add_fusion.here, ...), custom_call_target="tpu_custom_call" | custom-call | flops 536870912 | bytes 8388608 | tf_op jit(solution)/shard_map/stats/pallas_call | solution.py:262
  45.2 16.9 %all_to_all.15.lse_all = f32[32,16,128]{2,1,0:T(8,128)S(1)} all-to-all(f32[32,16,128]{2,1,0:T(8,128)S(1)} %get-tuple-element.44), channel_id=1, replica_groups=mesh['yl'=2,'c'=2,'yh'=2,'x'=4,'z'=8] {'x','z'}, dimensions={0} | all-to-all | bytes 524288 | tf_op jit(solution)/shard_map/all_to_all | solution.py:278
  62.1 3.2 %grad.4 = (f32[512,128]{1,0:T(8,128)S(1)}, f32[4,512,128]{2,1,0:T(8,128)S(1)}, f32[4,512,128]{2,1,0:T(8,128)S(1)}) custom-call(s32[3]{0:T(128)S(1)} %pad_add_fusion.here, bf16[4096,256]{1,0:T(8,128)(2,1)S(1)} %get-tuple-element.41.c_ext, bf16[2048,256]{1,0:T(8,128)(2,1)S(1)} %get-tuple-element.42.q_ext, f32[8,2048]{1,0:T(8,128)S(1)} %get-tuple-element.43.aux, ...), custom_call_target="tpu_custom_call" | custom-call | flops 402653184 | bytes 2097152 | tf_op jit(solution)/shard_map/grad/pallas_call | solution.py:282
  65.3 1.8 %collective-permute-start.4 = (f32[512,128]{1,0:T(8,128)S(1)}, f32[512,128]{1,0:T(8,128)S(1)}, u32[]{:S(2)}, u32[]{:S(2)}) collective-permute-start(f32[512,128]{1,0:T(8,128)S(1)} %get-tuple-element.52), channel_id=1, source_target_pairs={{0,16},{8,24},{16,0},{24,8},{1,17},{9,25},{17,1},{25,9},{2,18},{10... | collective-permute-start | bytes 786440 | tf_op jit(solution)/shard_map/ppermute | solution.py:294
  67.1 5.9 %grad.5 = (f32[512,128]{1,0:T(8,128)S(1)}, f32[512,128]{1,0:T(8,128)S(1)}, f32[4,512,128]{2,1,0:T(8,128)S(1)}, f32[4,512,128]{2,1,0:T(8,128)S(1)}) custom-call(s32[3]{0:T(128)S(1)} %pad_add_fusion.here, bf16[4096,256]{1,0:T(8,128)(2,1)S(1)} %get-tuple-element.41.c_ext, ...), custom_call_target="tpu_custom_call", output_to_operand_aliasing={{2}: (12, {}), {3}: (13, {})} | custom-call | flops 805306368 | bytes 4194304 | tf_op jit(solution)/shard_map/grad/pallas_call | solution.py:282
  73.1 1.9 %collective-permute-start.5 = (f32[512,128]{1,0:T(8,128)S(1)}, f32[512,128]{1,0:T(8,128)S(1)}, u32[]{:S(2)}, u32[]{:S(2)}) collective-permute-start(f32[512,128]{1,0:T(8,128)S(1)} %get-tuple-element.57), channel_id=1, source_target_pairs={{0,24},{8,0},{16,8},{24,16},{1,25},{9,1},{17,9},{25,17},{2,26},{10... | collective-permute-start | bytes 786440 | tf_op jit(solution)/shard_map/ppermute | solution.py:294
  74.9 0.3 collective-permute-start.6
  75.2 2.2 %grad.6 = (f32[512,128]{1,0:T(8,128)S(1)}, f32[4,512,128]{2,1,0:T(8,128)S(1)}) custom-call(s32[3]{0:T(128)S(1)} %pad_add_fusion.here, bf16[4096,256]{1,0:T(8,128)(2,1)S(1)} %get-tuple-element.41.c_ext, bf16[2048,256]{1,0:T(8,128)(2,1)S(1)} %get-tuple-element.42.q_ext, f32[8,2048]{1,0:T(8,128)S(1)} %get-tuple-element.43.aux, ...), custom_call_target="tpu_custom_call", output_to_operand_aliasing={{1}: (12, {})} | custom-call | flops 201326592 | bytes 1048576 | tf_op jit(solution)/shard_map/grad/pallas_call | solution.py:282
  77.4 2.0 %grad.7 = (f32[512,128]{1,0:T(8,128)S(1)}, f32[4,512,128]{2,1,0:T(8,128)S(1)}) custom-call(s32[3]{0:T(128)S(1)} %pad_add_fusion.here, bf16[4096,256]{1,0:T(8,128)(2,1)S(1)} %get-tuple-element.41.c_ext, bf16[2048,256]{1,0:T(8,128)(2,1)S(1)} %get-tuple-element.42.q_ext, ...), custom_call_target="tpu_custom_call", output_to_operand_aliasing={{0}: (12, {}), {1}: (13, {})} | custom-call | flops 201326592 | bytes 1048576 | tf_op jit(solution)/shard_map/grad/pallas_call | solution.py:282
  79.5 3.0 %collective-permute-done.6.c = f32[512,128]{1,0:T(8,128)S(1)} collective-permute-done((f32[512,128]{1,0:T(8,128)S(1)}, f32[512,128]{1,0:T(8,128)S(1)}, u32[]{:S(2)}, u32[]{:S(2)}) %collective-permute-start.6) | collective-permute-done | bytes 262176 | tf_op jit(solution)/shard_map/ppermute | solution.py:294
  82.5 0.7 add.28
  83.2 0.1 merge.1
  83.4 0.4 collective-permute-start.8
  83.8 3.0 %collective-permute-start.9 = (f32[512,128]{1,0:T(8,128)S(1)}, f32[512,128]{1,0:T(8,128)S(1)}, u32[]{:S(2)}, u32[]{:S(2)}) collective-permute-start(f32[512,128]{1,0:T(8,128)S(1)} %get-tuple-element.74), channel_id=1, source_target_pairs={{0,32},{128,160},{32,0},{160,128},{1,33},{129,161},{33,1},{161,129... | collective-permute-start | bytes 786440 | tf_op jit(solution)/shard_map/ppermute | solution.py:326
  86.8 1.6 %collective-permute-start.10 = (f32[512,128]{1,0:T(8,128)S(1)}, f32[512,128]{1,0:T(8,128)S(1)}, u32[]{:S(2)}, u32[]{:S(2)}) collective-permute-start(f32[512,128]{1,0:T(8,128)S(1)} %get-tuple-element.75), channel_id=1, source_target_pairs={{0,128},{128,32},{32,160},{160,0},{1,129},{129,33},{33,161},{161,1... | collective-permute-start | bytes 786440 | tf_op jit(solution)/shard_map/ppermute | solution.py:326
  88.4 3.8 %all-to-all-start.2 = ((f32[8,64,128]{2,1,0:T(8,128)}), f32[8,64,128]{2,1,0:T(8,128)S(1)}, u32[]{:S(2)}, u32[]{:S(2)}) async-start(f32[8,64,128]{2,1,0:T(8,128)} %bitcast.10), calls=%async_computation.2 | async-start | bytes 524288 | tf_op jit(solution)/shard_map/all_to_all | solution.py:327
  92.2 1.4 %collective-permute-done.9 = f32[512,128]{1,0:T(8,128)S(1)} collective-permute-done((f32[512,128]{1,0:T(8,128)S(1)}, f32[512,128]{1,0:T(8,128)S(1)}, u32[]{:S(2)}, u32[]{:S(2)}) %collective-permute-start.9) | collective-permute-done | bytes 262176 | tf_op jit(solution)/shard_map/ppermute | solution.py:326
  93.6 2.7 %collective-permute-done.10 = f32[512,128]{1,0:T(8,128)S(1)} collective-permute-done((f32[512,128]{1,0:T(8,128)S(1)}, f32[512,128]{1,0:T(8,128)S(1)}, u32[]{:S(2)}, u32[]{:S(2)}) %collective-permute-start.10) | collective-permute-done | bytes 262176 | tf_op jit(solution)/shard_map/ppermute | solution.py:326
  96.3 0.8 add_add_fusion
  97.1 5.7 %all-to-all-done.2 = f32[8,64,128]{2,1,0:T(8,128)S(1)} async-done(((f32[8,64,128]{2,1,0:T(8,128)}), f32[8,64,128]{2,1,0:T(8,128)S(1)}, u32[]{:S(2)}, u32[]{:S(2)}) %all-to-all-start.2) | async-done | bytes 262176 | tf_op jit(solution)/shard_map/all_to_all | solution.py:327
  102.7 0.6 reduce_sum.9
  (10 shorter events, 0.5 us)
Async XLA Ops:
  2.5 29.8 %all-to-all-start = ((bf16[32,72,128]{2,1,0:T(8,128)(2,1)}), bf16[32,72,128]{2,1,0:T(8,128)(2,1)S(1)}, u32[]{:S(2)}, u32[]{:S(2)}) async-start(bf16[32,72,128]{2,1,0:T(8,128)(2,1)} %get-tuple-element.39), calls=%async_computation | async-start | bytes 1179648 | tf_op jit(solution)/shard_map/all_to_all | solution.py:252
  13.8 6.8 %collective-permute-start.2 = (bf16[528,128]{1,0:T(8,128)(2,1)}, bf16[528,128]{1,0:T(8,128)(2,1)S(1)}, u32[]{:S(2)}, u32[]{:S(2)}) collective-permute-start(bf16[528,128]{1,0:T(8,128)(2,1)} %get-tuple-element.40), channel_id=1, source_target_pairs={{0,160},{128,0},{32,128},{160,32},{1,161},{129,1},{33,129},{161,33... | collective-permute-start | bytes 405512 | tf_op jit(solution)/shard_map/ppermute | solution.py:255
  14.3 8.0 %collective-permute-start.1 = (bf16[528,128]{1,0:T(8,128)(2,1)}, bf16[528,128]{1,0:T(8,128)(2,1)S(1)}, u32[]{:S(2)}, u32[]{:S(2)}) collective-permute-start(bf16[528,128]{1,0:T(8,128)(2,1)} %get-tuple-element.40), channel_id=1, source_target_pairs={{0,32},{128,160},{32,0},{160,128},{1,33},{129,161},{33,1},{161,129... | collective-permute-start | bytes 405512 | tf_op jit(solution)/shard_map/ppermute | solution.py:255
  17.3 6.5 %collective-permute-start = (bf16[528,128]{1,0:T(8,128)(2,1)}, bf16[528,128]{1,0:T(8,128)(2,1)S(1)}, u32[]{:S(2)}, u32[]{:S(2)}) collective-permute-start(bf16[528,128]{1,0:T(8,128)(2,1)} %get-tuple-element.40), channel_id=1, source_target_pairs={{0,128},{128,32},{32,160},{160,0},{1,129},{129,33},{33,161},{161,1... | collective-permute-start | bytes 405512 | tf_op jit(solution)/shard_map/ppermute | solution.py:255
  24.7 2.0 %collective-permute-start.3 = (bf16[4,528,128]{2,1,0:T(8,128)(2,1)S(1)}, bf16[4,528,128]{2,1,0:T(8,128)(2,1)S(1)}, u32[]{:S(2)}, u32[]{:S(2)}) collective-permute-start(bf16[4,528,128]{2,1,0:T(8,128)(2,1)S(1)} %pad_maximum_fusion.own), channel_id=1, source_target_pairs={{0,64},{64,0},{1,65},{65,1},{2,66},{66,2},{3,67},{67,3},{4,68},{68... | collective-permute-start | bytes 1622024 | tf_op jit(solution)/shard_map/ppermute | solution.py:258
  65.3 9.8 %collective-permute-start.4 = (f32[512,128]{1,0:T(8,128)S(1)}, f32[512,128]{1,0:T(8,128)S(1)}, u32[]{:S(2)}, u32[]{:S(2)}) collective-permute-start(f32[512,128]{1,0:T(8,128)S(1)} %get-tuple-element.52), channel_id=1, source_target_pairs={{0,16},{8,24},{16,0},{24,8},{1,17},{9,25},{17,1},{25,9},{2,18},{10... | collective-permute-start | bytes 786440 | tf_op jit(solution)/shard_map/ppermute | solution.py:294
  73.1 6.4 %collective-permute-start.5 = (f32[512,128]{1,0:T(8,128)S(1)}, f32[512,128]{1,0:T(8,128)S(1)}, u32[]{:S(2)}, u32[]{:S(2)}) collective-permute-start(f32[512,128]{1,0:T(8,128)S(1)} %get-tuple-element.57), channel_id=1, source_target_pairs={{0,24},{8,0},{16,8},{24,16},{1,25},{9,1},{17,9},{25,17},{2,26},{10... | collective-permute-start | bytes 786440 | tf_op jit(solution)/shard_map/ppermute | solution.py:294
  74.9 7.6 %collective-permute-start.6 = (f32[512,128]{1,0:T(8,128)S(1)}, f32[512,128]{1,0:T(8,128)S(1)}, u32[]{:S(2)}, u32[]{:S(2)}) collective-permute-start(f32[512,128]{1,0:T(8,128)S(1)} %get-tuple-element.58), channel_id=1, source_target_pairs={{0,8},{8,16},{16,24},{24,0},{1,9},{9,17},{17,25},{25,1},{2,10},{10... | collective-permute-start | bytes 786440 | tf_op jit(solution)/shard_map/ppermute | solution.py:294
  77.3 5.9 %collective-permute-start.7 = (f32[4,512,128]{2,1,0:T(8,128)S(1)}, f32[4,512,128]{2,1,0:T(8,128)S(1)}, u32[]{:S(2)}, u32[]{:S(2)}) collective-permute-start(f32[4,512,128]{2,1,0:T(8,128)S(1)} %get-tuple-element.66), channel_id=1, source_target_pairs={{0,64},{64,0},{1,65},{65,1},{2,66},{66,2},{3,67},{67,3},{4,68},{68... | collective-permute-start | bytes 3145736 | tf_op jit(solution)/shard_map/ppermute | solution.py:303
  83.4 8.9 %collective-permute-start.8 = (f32[512,128]{1,0:T(8,128)S(1)}, f32[512,128]{1,0:T(8,128)S(1)}, u32[]{:S(2)}, u32[]{:S(2)}) collective-permute-start(f32[512,128]{1,0:T(8,128)S(1)} %get-tuple-element.73), channel_id=1, source_target_pairs={{0,160},{128,0},{32,128},{160,32},{1,161},{129,1},{33,129},{161,33... | collective-permute-start | bytes 786440 | tf_op jit(solution)/shard_map/ppermute | solution.py:326
  83.8 9.8 %collective-permute-start.9 = (f32[512,128]{1,0:T(8,128)S(1)}, f32[512,128]{1,0:T(8,128)S(1)}, u32[]{:S(2)}, u32[]{:S(2)}) collective-permute-start(f32[512,128]{1,0:T(8,128)S(1)} %get-tuple-element.74), channel_id=1, source_target_pairs={{0,32},{128,160},{32,0},{160,128},{1,33},{129,161},{33,1},{161,129... | collective-permute-start | bytes 786440 | tf_op jit(solution)/shard_map/ppermute | solution.py:326
  86.8 9.5 %collective-permute-start.10 = (f32[512,128]{1,0:T(8,128)S(1)}, f32[512,128]{1,0:T(8,128)S(1)}, u32[]{:S(2)}, u32[]{:S(2)}) collective-permute-start(f32[512,128]{1,0:T(8,128)S(1)} %get-tuple-element.75), channel_id=1, source_target_pairs={{0,128},{128,32},{32,160},{160,0},{1,129},{129,33},{33,161},{161,1... | collective-permute-start | bytes 786440 | tf_op jit(solution)/shard_map/ppermute | solution.py:326
  88.4 14.3 %all-to-all-start.2 = ((f32[8,64,128]{2,1,0:T(8,128)}), f32[8,64,128]{2,1,0:T(8,128)S(1)}, u32[]{:S(2)}, u32[]{:S(2)}) async-start(f32[8,64,128]{2,1,0:T(8,128)} %bitcast.10), calls=%async_computation.2 | async-start | bytes 524288 | tf_op jit(solution)/shard_map/all_to_all | solution.py:327
